TPU v7x, 256 devices: a whole 4x4x8 slice. The times are simulated.
256 devices in a mesh: dp: 8 (over z), heads: 4 (over x_hi, core), ctx: 8 (over x_lo, y).
Axes of the slice: x: 4 (x_hi: 2, x_lo: 2; x = x_hi * 2 + x_lo), y: 4, z: 8, core: 2. Of those that a mesh axis runs over, the one named last changes fastest.
Arguments:
- inputs: bfloat16 [8, 2048, 5120], P('dp', 'ctx'), may hold values from -6 to 6
- queries: bfloat16 [8, 2048, 4096], P('dp', 'ctx', 'heads'), may hold values from -6 to 6
- keys: bfloat16 [8, 2048, 512], P('dp', 'ctx', 'heads'), may hold values from -6 to 6
- values: bfloat16 [8, 2048, 512], P('dp', 'ctx', 'heads'), may hold values from -6 to 6
- outputs: bfloat16 [8, 2048, 4096], P('dp', 'ctx', 'heads'), may hold values from -6 to 6
- out_grad: bfloat16 [8, 2048, 4096], P('dp', 'ctx', 'heads'), may hold values from -6 to 6
- lse: float32 [8, 2048, 32], P('dp', 'ctx', 'heads'), may hold values from 6 to 9
- positions: int32 [8, 2048], P('dp', 'ctx'), may hold values from 0 to 2047, as said below
Outputs:
- query_grad: float32 [8, 2048, 4096], P('dp', 'ctx', 'heads')
- key_grad: float32 [8, 2048, 512], P('dp', 'ctx', 'heads')
- value_grad: float32 [8, 2048, 512], P('dp', 'ctx', 'heads')
- weight_grad: float32 [5120, 1024], P(('dp', 'ctx'), 'heads')
Inputs may be any that keep to these rules, and one draw needn't show every extreme that they name: Each sequence's positions are a permutation of 0 to 2047 made of 16 runs of 128 rising consecutive positions; each run fills an aligned block of 128 slots and starts at a multiple of 128.
All inputs are finite; a program needn't handle non-finite values.
Results may differ from a plain program's by a relative error of at most 0.0045.
Values may be sent and summed in bfloat16 or wider, within the bound.
No kernel may reach another device: no remote copies, remote signals or barrier semaphores. Data moves between devices by JAX's collectives and lax.ppermute only.
A program may use at most 64 MiB of HBM per device.

v0:
```python
import jax
import jax.numpy as jnp
from jax import lax
from jax.sharding import PartitionSpec as P

HD = 128


def passed_along(block, axis, distance):
    devices = range(lax.axis_size(axis))
    route = [((i - distance) % len(devices), i) for i in devices]
    return lax.ppermute(block, axis, route)


def block_grads(query_blk, grad_blk, lse_blk, delta_blk, query_pos, key_blk, value_blk, key_pos):
    factor = HD ** (-0.5)
    tokens_q = query_blk.shape[0]
    tokens_k = key_blk.shape[0]
    kv_local = key_blk.shape[1] // HD
    group_size = query_blk.shape[1] // key_blk.shape[1]
    query_four = query_blk.reshape(tokens_q, kv_local, group_size, HD)
    grad_four = grad_blk.reshape(tokens_q, kv_local, group_size, HD)
    key_three = key_blk.reshape(tokens_k, kv_local, HD)
    value_three = value_blk.reshape(tokens_k, kv_local, HD)
    lse_four = jnp.transpose(lse_blk.reshape(tokens_q, kv_local, group_size), (1, 2, 0))[..., None]
    delta_four = jnp.transpose(delta_blk.reshape(tokens_q, kv_local, group_size), (1, 2, 0))[
        ..., None
    ]
    visible = key_pos[None, :] <= query_pos[:, None]
    scores = (
        jnp.einsum("qhgd,khd->hgqk", query_four, key_three, preferred_element_type=jnp.float32)
        * factor
    )
    probs = jnp.where(visible, jnp.exp(scores - lse_four), jnp.float32(0.0))
    dprobs = jnp.einsum(
        "qhgd,khd->hgqk", grad_four, value_three, preferred_element_type=jnp.float32
    )
    dscores = probs * (dprobs - delta_four)
    probs_low = probs.astype(jnp.bfloat16)
    dscores_low = dscores.astype(jnp.bfloat16)
    value_part = jnp.einsum(
        "hgqk,qhgd->khd", probs_low, grad_four, preferred_element_type=jnp.float32
    )
    key_part = (
        jnp.einsum("hgqk,qhgd->khd", dscores_low, query_four, preferred_element_type=jnp.float32)
        * factor
    )
    query_part = (
        jnp.einsum("hgqk,khd->qhgd", dscores_low, key_three, preferred_element_type=jnp.float32)
        * factor
    )
    return (
        query_part.reshape(tokens_q, kv_local * group_size * HD),
        key_part.reshape(tokens_k, kv_local * HD),
        value_part.reshape(tokens_k, kv_local * HD),
    )


def shards(inputs, queries, keys, values, outputs, out_grad, lse, positions):
    query_loc = queries[0]
    grad_loc = out_grad[0]
    key_loc = keys[0]
    value_loc = values[0]
    lse_loc = lse[0]
    tokens = query_loc.shape[0]
    heads_q = query_loc.shape[1] // HD
    kv_local = key_loc.shape[1] // HD
    delta_loc = jnp.sum(
        (grad_loc.astype(jnp.float32) * outputs[0].astype(jnp.float32)).reshape(
            tokens, heads_q, HD
        ),
        axis=2,
    )
    pos_loc = positions[0].astype(jnp.float32)
    rounds = lax.axis_size("ctx")
    zero_query = jnp.zeros((tokens, heads_q * HD), jnp.float32)
    zero_key = jnp.zeros((tokens, kv_local * HD), jnp.float32)

    def spin(index, carry):
        key_blk, value_blk, key_acc, value_acc, kpos_blk, dq_acc = carry
        query_part, key_part, value_part = block_grads(
            query_loc, grad_loc, lse_loc, delta_loc, pos_loc, key_blk, value_blk, kpos_blk
        )
        key_blk, value_blk = passed_along((key_blk, value_blk), "ctx", 1)
        key_acc, value_acc, kpos_blk = passed_along(
            (key_acc + key_part, value_acc + value_part, kpos_blk), "ctx", 1
        )
        return (key_blk, value_blk, key_acc, value_acc, kpos_blk, dq_acc + query_part)

    key_blk, value_blk, key_acc, value_acc, kpos_blk, dq_acc = lax.fori_loop(
        0, rounds - 1, spin, (key_loc, value_loc, zero_key, zero_key, pos_loc, zero_query)
    )
    query_part, key_part, value_part = block_grads(
        query_loc, grad_loc, lse_loc, delta_loc, pos_loc, key_blk, value_blk, kpos_blk
    )
    key_grad, value_grad = passed_along((key_acc + key_part, value_acc + value_part), "ctx", 1)
    query_grad = dq_acc + query_part
    kv_low = jnp.stack(
        [key_grad.reshape(tokens, kv_local, HD), value_grad.reshape(tokens, kv_local, HD)], axis=2
    )
    kv_low = kv_low.reshape(tokens, kv_local * 2 * HD).astype(jnp.bfloat16)
    inputs_loc = inputs[0]
    weight_grad = lax.psum_scatter(
        jnp.einsum("td,tc->dc", inputs_loc, kv_low, preferred_element_type=jnp.float32),
        ("dp", "ctx"),
        scatter_dimension=0,
        tiled=True,
    )
    return (query_grad[None], key_grad[None], value_grad[None], weight_grad)


def solution(mesh):
    return jax.shard_map(
        shards,
        mesh=mesh,
        in_specs=(
            P("dp", "ctx", None),
            P("dp", "ctx", "heads"),
            P("dp", "ctx", "heads"),
            P("dp", "ctx", "heads"),
            P("dp", "ctx", "heads"),
            P("dp", "ctx", "heads"),
            P("dp", "ctx", "heads"),
            P("dp", "ctx"),
        ),
        out_specs=(
            P("dp", "ctx", "heads"),
            P("dp", "ctx", "heads"),
            P("dp", "ctx", "heads"),
            P(("dp", "ctx"), "heads"),
        ),
        check_vma=False,
    )
```

profile of v0, /device:TPU:6, one launch (start us, length us, event | category | flops | bytes accessed | tf_op | source)
XLA Modules:
  0.0 504.1 jit_solution(17957280612306744279)
XLA Ops:
  7.2 1.7 copy.129
  10.1 1.6 copy.51
  11.7 1.1 copy.74
  12.8 2.2 copy.76
  16.5 139.0 %while.21 = (s32[]{:T(128)}, bf16[256,128]{0,1:T(8,128)(2,1)}, bf16[256,128]{1,0:T(8,128)(2,1)}, f32[256,128]{1,0:T(8,128)S(1)}, f32[256,128]{1,0:T(8,128)S(1)},...) while((s32[]{:T(128)}, bf16[256,128]{0,1:T(8,128)(2,1)}, ...), condition=%wide.region_2.3_spmd.clone, body=%wide.region_1.2_spmd.clone.sunk | while | flops 675708928 | bytes 20570480 | solution.py:90
  17.2 1.6 collective-permute-start.4
  19.6 1.6 collective-permute-start.1
  22.0 1.3 collective-permute-start
  23.5 1.1 copy.104
  28.4 1.6 collective-permute-start.3
  30.0 1.3 convolution_multiply_fusion.3
  31.3 2.3 bitcast_add_fusion.2
  33.6 1.3 collective-permute-done.2
  35.0 1.4 collective-permute-done.3
  39.2 1.6 collective-permute-start
  41.0 1.1 copy.104
  44.4 3.1 collective-permute-start.2
  47.5 1.1 fusion.67
  48.6 1.3 convolution_multiply_fusion.3
  49.9 2.6 bitcast_add_fusion.2
  52.6 3.3 collective-permute-done.3
  58.2 1.7 collective-permute-start
  60.1 1.1 copy.104
  63.5 3.3 collective-permute-start.2
  66.8 1.1 fusion.67
  67.9 1.3 convolution_multiply_fusion.3
  69.2 2.6 bitcast_add_fusion.2
  71.9 3.3 collective-permute-done.3
  77.5 1.9 collective-permute-start
  79.6 1.1 copy.104
  83.0 3.3 collective-permute-start.2
  86.3 1.1 fusion.67
  87.4 1.3 convolution_multiply_fusion.3
  88.7 2.6 bitcast_add_fusion.2
  91.4 3.5 collective-permute-done.3
  97.3 1.5 collective-permute-start
  99.0 1.1 copy.104
  102.3 3.3 collective-permute-start.2
  105.6 1.1 fusion.67
  106.7 1.3 convolution_multiply_fusion.3
  108.0 2.6 bitcast_add_fusion.2
  110.7 4.7 collective-permute-done.3
  118.7 1.1 copy.104
  122.0 3.8 collective-permute-start.2
  126.9 1.3 convolution_multiply_fusion.3
  128.2 2.6 bitcast_add_fusion.2
  130.8 3.3 collective-permute-done.3
  136.5 2.4 collective-permute-start
  139.1 1.1 copy.104
  142.5 3.3 collective-permute-start.2
  146.9 1.3 convolution_multiply_fusion.3
  148.2 2.6 bitcast_add_fusion.2
  150.8 4.7 collective-permute-done.3
  156.3 1.7 fusion.21
  158.0 1.3 fusion.22
  160.5 6.5 %collective-permute-done.5 = f32[256,128]{1,0:T(8,128)S(1)} collective-permute-done((f32[256,128]{1,0:T(8,128)S(1)}, f32[256,128]{1,0:T(8,128)S(1)}, u32[]{:S(2)}, u32[]{:S(2)}) %collective-permute-start.5) | collective-permute-done | bytes 131104 | tf_op jit(solution)/shard_map/ppermute | solution.py:12
  167.0 1.4 collective-permute-done.6
  168.6 3.2 convolution_bitcast_fusion.2
  171.8 5.9 %copy.70 = f32[5120,256]{1,0:T(8,128)} copy(f32[5120,256]{0,1:T(8,128)} %convolution_bitcast_fusion.2) | data formatting | bytes 10485760
  177.7 2.6 copy.58
  180.3 2.5 convolution_multiply_fusion.1
  182.8 2.6 copy.59
  185.4 2.7 add_bitcast_fusion
  188.1 307.8 %reduce-scatter.4.cloned.1.call-done = f32[80,256]{1,0:T(8,128)} async-done(((f32[5120,256]{1,0:T(8,128)}), f32[80,256]{1,0:T(8,128)}) %reduce-scatter.4.cloned.1.call-update) | async-done | bytes 81936
  (159 shorter events, 44.3 us)
Async XLA Ops:
  7.2 161.4 %copy-start = (bf16[1,256,5120]{2,1,0:T(8,128)(2,1)S(1)}, bf16[1,256,5120]{2,1,0:T(8,128)(2,1)}, u32[]{:S(2)}) copy-start(bf16[1,256,5120]{2,1,0:T(8,128)(2,1)} %param.10) | copy-start | bytes 7864324
  7.2 7.8 %copy-start.6 = (bf16[1,256,1024]{2,1,0:T(8,128)(2,1)S(1)}, bf16[1,256,1024]{2,1,0:T(8,128)(2,1)}, u32[]{:S(2)}) copy-start(bf16[1,256,1024]{2,1,0:T(8,128)(2,1)} %param.14) | copy-start | bytes 1572868
  7.2 488.7 %reduce-scatter.4.cloned.1.call-start = ((), (), s32[]{:S(2)}) async-start(), calls=%async_computation.1 | async-start | bytes 5324800
  12.8 2.5 copy-start.3
  15.1 1.4 copy-start.1
  16.5 8.1 %copy-start.8 = (f32[1,256,8]{1,2,0:T(8,128)S(1)}, f32[1,256,8]{1,2,0:T(8,128)}, u32[]{:S(2)}) copy-start(f32[1,256,8]{1,2,0:T(8,128)} %get-tuple-element.274) | copy-start | bytes 24580 | tf_op jit(solution)/shard_map/while
  17.2 16.5 %collective-permute-start.4 = (f32[256]{0:T(256)S(1)}, f32[256]{0:T(256)}, u32[]{:S(2)}, u32[]{:S(2)}) collective-permute-start(f32[256]{0:T(256)S(1)} %copy.117), channel_id=1, source_target_pairs={{7,0},{0,1},{1,2},{2,3},{3,4},{4,5},{5,6},{6,7},{15,8},{8,9},{9,10... | collective-permute-start | bytes 3080 | tf_op jit(solution)/shard_map/while/body/eval_jaxpr/ppermute | solution.py:12
  19.6 14.0 %collective-permute-start.1 = (bf16[256,128]{1,0:T(8,128)(2,1)S(1)}, bf16[256,128]{1,0:T(8,128)(2,1)}, u32[]{:S(2)}, u32[]{:S(2)}) collective-permute-start(bf16[256,128]{1,0:T(8,128)(2,1)S(1)} %copy.114), channel_id=1, source_target_pairs={{7,0},{0,1},{1,2},{2,3},{3,4},{4,5},{5,6},{6,7},{15,8},{8,9},{9,10... | collective-permute-start | bytes 196616 | tf_op jit(solution)/shard_map/while/body/eval_jaxpr/ppermute | solution.py:12
  22.0 11.6 %collective-permute-start = (bf16[256,128]{0,1:T(8,128)(2,1)S(1)}, bf16[256,128]{0,1:T(8,128)(2,1)}, u32[]{:S(2)}, u32[]{:S(2)}) collective-permute-start(bf16[256,128]{0,1:T(8,128)(2,1)S(1)} %copy.113), channel_id=1, source_target_pairs={{7,0},{0,1},{1,2},{2,3},{3,4},{4,5},{5,6},{6,7},{15,8},{8,9},{9,10... | collective-permute-start | bytes 196616 | tf_op jit(solution)/shard_map/while/body/eval_jaxpr/ppermute | solution.py:12
  26.9 8.1 %collective-permute-start.2 = (f32[256,128]{1,0:T(8,128)}, f32[256,128]{1,0:T(8,128)S(1)}, u32[]{:S(2)}, u32[]{:S(2)}) collective-permute-start(f32[256,128]{1,0:T(8,128)} %fusion.66), channel_id=1, source_target_pairs={{7,0},{0,1},{1,2},{2,3},{3,4},{4,5},{5,6},{6,7},{15,8},{8,9},{9,10... | collective-permute-start | bytes 393224 | tf_op jit(solution)/shard_map/while/body/eval_jaxpr/ppermute | solution.py:12
  28.4 7.9 %collective-permute-start.3 = (f32[256,128]{1,0:T(8,128)}, f32[256,128]{1,0:T(8,128)S(1)}, u32[]{:S(2)}, u32[]{:S(2)}) collective-permute-start(f32[256,128]{1,0:T(8,128)} %fusion.67), channel_id=1, source_target_pairs={{7,0},{0,1},{1,2},{2,3},{3,4},{4,5},{5,6},{6,7},{15,8},{8,9},{9,10... | collective-permute-start | bytes 393224 | tf_op jit(solution)/shard_map/while/body/eval_jaxpr/ppermute | solution.py:12
  36.4 5.8 %copy-start.8 = (f32[1,256,8]{1,2,0:T(8,128)S(1)}, f32[1,256,8]{1,2,0:T(8,128)}, u32[]{:S(2)}) copy-start(f32[1,256,8]{1,2,0:T(8,128)} %get-tuple-element.274) | copy-start | bytes 24580 | tf_op jit(solution)/shard_map/while
  37.0 15.5 %collective-permute-start.4 = (f32[256]{0:T(256)S(1)}, f32[256]{0:T(256)}, u32[]{:S(2)}, u32[]{:S(2)}) collective-permute-start(f32[256]{0:T(256)S(1)} %copy.117), channel_id=1, source_target_pairs={{7,0},{0,1},{1,2},{2,3},{3,4},{4,5},{5,6},{6,7},{15,8},{8,9},{9,10... | collective-permute-start | bytes 3080 | tf_op jit(solution)/shard_map/while/body/eval_jaxpr/ppermute | solution.py:12
  37.9 14.7 %collective-permute-start.1 = (bf16[256,128]{1,0:T(8,128)(2,1)S(1)}, bf16[256,128]{1,0:T(8,128)(2,1)}, u32[]{:S(2)}, u32[]{:S(2)}) collective-permute-start(bf16[256,128]{1,0:T(8,128)(2,1)S(1)} %copy.114), channel_id=1, source_target_pairs={{7,0},{0,1},{1,2},{2,3},{3,4},{4,5},{5,6},{6,7},{15,8},{8,9},{9,10... | collective-permute-start | bytes 196616 | tf_op jit(solution)/shard_map/while/body/eval_jaxpr/ppermute | solution.py:12
  39.2 13.3 %collective-permute-start = (bf16[256,128]{0,1:T(8,128)(2,1)S(1)}, bf16[256,128]{0,1:T(8,128)(2,1)}, u32[]{:S(2)}, u32[]{:S(2)}) collective-permute-start(bf16[256,128]{0,1:T(8,128)(2,1)S(1)} %copy.113), channel_id=1, source_target_pairs={{7,0},{0,1},{1,2},{2,3},{3,4},{4,5},{5,6},{6,7},{15,8},{8,9},{9,10... | collective-permute-start | bytes 196616 | tf_op jit(solution)/shard_map/while/body/eval_jaxpr/ppermute | solution.py:12
  44.4 8.2 %collective-permute-start.2 = (f32[256,128]{1,0:T(8,128)}, f32[256,128]{1,0:T(8,128)S(1)}, u32[]{:S(2)}, u32[]{:S(2)}) collective-permute-start(f32[256,128]{1,0:T(8,128)} %fusion.66), channel_id=1, source_target_pairs={{7,0},{0,1},{1,2},{2,3},{3,4},{4,5},{5,6},{6,7},{15,8},{8,9},{9,10... | collective-permute-start | bytes 393224 | tf_op jit(solution)/shard_map/while/body/eval_jaxpr/ppermute | solution.py:12
  48.6 7.3 %collective-permute-start.3 = (f32[256,128]{1,0:T(8,128)}, f32[256,128]{1,0:T(8,128)S(1)}, u32[]{:S(2)}, u32[]{:S(2)}) collective-permute-start(f32[256,128]{1,0:T(8,128)} %fusion.67), channel_id=1, source_target_pairs={{7,0},{0,1},{1,2},{2,3},{3,4},{4,5},{5,6},{6,7},{15,8},{8,9},{9,10... | collective-permute-start | bytes 393224 | tf_op jit(solution)/shard_map/while/body/eval_jaxpr/ppermute | solution.py:12
  55.9 5.4 %copy-start.8 = (f32[1,256,8]{1,2,0:T(8,128)S(1)}, f32[1,256,8]{1,2,0:T(8,128)}, u32[]{:S(2)}) copy-start(f32[1,256,8]{1,2,0:T(8,128)} %get-tuple-element.274) | copy-start | bytes 24580 | tf_op jit(solution)/shard_map/while
  56.5 15.3 %collective-permute-start.4 = (f32[256]{0:T(256)S(1)}, f32[256]{0:T(256)}, u32[]{:S(2)}, u32[]{:S(2)}) collective-permute-start(f32[256]{0:T(256)S(1)} %copy.117), channel_id=1, source_target_pairs={{7,0},{0,1},{1,2},{2,3},{3,4},{4,5},{5,6},{6,7},{15,8},{8,9},{9,10... | collective-permute-start | bytes 3080 | tf_op jit(solution)/shard_map/while/body/eval_jaxpr/ppermute | solution.py:12
  57.4 14.5 %collective-permute-start.1 = (bf16[256,128]{1,0:T(8,128)(2,1)S(1)}, bf16[256,128]{1,0:T(8,128)(2,1)}, u32[]{:S(2)}, u32[]{:S(2)}) collective-permute-start(bf16[256,128]{1,0:T(8,128)(2,1)S(1)} %copy.114), channel_id=1, source_target_pairs={{7,0},{0,1},{1,2},{2,3},{3,4},{4,5},{5,6},{6,7},{15,8},{8,9},{9,10... | collective-permute-start | bytes 196616 | tf_op jit(solution)/shard_map/while/body/eval_jaxpr/ppermute | solution.py:12
  58.2 13.6 %collective-permute-start = (bf16[256,128]{0,1:T(8,128)(2,1)S(1)}, bf16[256,128]{0,1:T(8,128)(2,1)}, u32[]{:S(2)}, u32[]{:S(2)}) collective-permute-start(bf16[256,128]{0,1:T(8,128)(2,1)S(1)} %copy.113), channel_id=1, source_target_pairs={{7,0},{0,1},{1,2},{2,3},{3,4},{4,5},{5,6},{6,7},{15,8},{8,9},{9,10... | collective-permute-start | bytes 196616 | tf_op jit(solution)/shard_map/while/body/eval_jaxpr/ppermute | solution.py:12
  63.5 8.4 %collective-permute-start.2 = (f32[256,128]{1,0:T(8,128)}, f32[256,128]{1,0:T(8,128)S(1)}, u32[]{:S(2)}, u32[]{:S(2)}) collective-permute-start(f32[256,128]{1,0:T(8,128)} %fusion.66), channel_id=1, source_target_pairs={{7,0},{0,1},{1,2},{2,3},{3,4},{4,5},{5,6},{6,7},{15,8},{8,9},{9,10... | collective-permute-start | bytes 393224 | tf_op jit(solution)/shard_map/while/body/eval_jaxpr/ppermute | solution.py:12
  67.9 7.3 %collective-permute-start.3 = (f32[256,128]{1,0:T(8,128)}, f32[256,128]{1,0:T(8,128)S(1)}, u32[]{:S(2)}, u32[]{:S(2)}) collective-permute-start(f32[256,128]{1,0:T(8,128)} %fusion.67), channel_id=1, source_target_pairs={{7,0},{0,1},{1,2},{2,3},{3,4},{4,5},{5,6},{6,7},{15,8},{8,9},{9,10... | collective-permute-start | bytes 393224 | tf_op jit(solution)/shard_map/while/body/eval_jaxpr/ppermute | solution.py:12
  75.2 5.6 %copy-start.8 = (f32[1,256,8]{1,2,0:T(8,128)S(1)}, f32[1,256,8]{1,2,0:T(8,128)}, u32[]{:S(2)}) copy-start(f32[1,256,8]{1,2,0:T(8,128)} %get-tuple-element.274) | copy-start | bytes 24580 | tf_op jit(solution)/shard_map/while
  75.9 15.5 %collective-permute-start.4 = (f32[256]{0:T(256)S(1)}, f32[256]{0:T(256)}, u32[]{:S(2)}, u32[]{:S(2)}) collective-permute-start(f32[256]{0:T(256)S(1)} %copy.117), channel_id=1, source_target_pairs={{7,0},{0,1},{1,2},{2,3},{3,4},{4,5},{5,6},{6,7},{15,8},{8,9},{9,10... | collective-permute-start | bytes 3080 | tf_op jit(solution)/shard_map/while/body/eval_jaxpr/ppermute | solution.py:12
  76.7 14.6 %collective-permute-start.1 = (bf16[256,128]{1,0:T(8,128)(2,1)S(1)}, bf16[256,128]{1,0:T(8,128)(2,1)}, u32[]{:S(2)}, u32[]{:S(2)}) collective-permute-start(bf16[256,128]{1,0:T(8,128)(2,1)S(1)} %copy.114), channel_id=1, source_target_pairs={{7,0},{0,1},{1,2},{2,3},{3,4},{4,5},{5,6},{6,7},{15,8},{8,9},{9,10... | collective-permute-start | bytes 196616 | tf_op jit(solution)/shard_map/while/body/eval_jaxpr/ppermute | solution.py:12
  77.5 13.8 %collective-permute-start = (bf16[256,128]{0,1:T(8,128)(2,1)S(1)}, bf16[256,128]{0,1:T(8,128)(2,1)}, u32[]{:S(2)}, u32[]{:S(2)}) collective-permute-start(bf16[256,128]{0,1:T(8,128)(2,1)S(1)} %copy.113), channel_id=1, source_target_pairs={{7,0},{0,1},{1,2},{2,3},{3,4},{4,5},{5,6},{6,7},{15,8},{8,9},{9,10... | collective-permute-start | bytes 196616 | tf_op jit(solution)/shard_map/while/body/eval_jaxpr/ppermute | solution.py:12
  83.0 8.4 %collective-permute-start.2 = (f32[256,128]{1,0:T(8,128)}, f32[256,128]{1,0:T(8,128)S(1)}, u32[]{:S(2)}, u32[]{:S(2)}) collective-permute-start(f32[256,128]{1,0:T(8,128)} %fusion.66), channel_id=1, source_target_pairs={{7,0},{0,1},{1,2},{2,3},{3,4},{4,5},{5,6},{6,7},{15,8},{8,9},{9,10... | collective-permute-start | bytes 393224 | tf_op jit(solution)/shard_map/while/body/eval_jaxpr/ppermute | solution.py:12
  87.4 7.5 %collective-permute-start.3 = (f32[256,128]{1,0:T(8,128)}, f32[256,128]{1,0:T(8,128)S(1)}, u32[]{:S(2)}, u32[]{:S(2)}) collective-permute-start(f32[256,128]{1,0:T(8,128)} %fusion.67), channel_id=1, source_target_pairs={{7,0},{0,1},{1,2},{2,3},{3,4},{4,5},{5,6},{6,7},{15,8},{8,9},{9,10... | collective-permute-start | bytes 393224 | tf_op jit(solution)/shard_map/while/body/eval_jaxpr/ppermute | solution.py:12
  94.9 5.2 %copy-start.8 = (f32[1,256,8]{1,2,0:T(8,128)S(1)}, f32[1,256,8]{1,2,0:T(8,128)}, u32[]{:S(2)}) copy-start(f32[1,256,8]{1,2,0:T(8,128)} %get-tuple-element.274) | copy-start | bytes 24580 | tf_op jit(solution)/shard_map/while
  95.6 15.1 %collective-permute-start.4 = (f32[256]{0:T(256)S(1)}, f32[256]{0:T(256)}, u32[]{:S(2)}, u32[]{:S(2)}) collective-permute-start(f32[256]{0:T(256)S(1)} %copy.117), channel_id=1, source_target_pairs={{7,0},{0,1},{1,2},{2,3},{3,4},{4,5},{5,6},{6,7},{15,8},{8,9},{9,10... | collective-permute-start | bytes 3080 | tf_op jit(solution)/shard_map/while/body/eval_jaxpr/ppermute | solution.py:12
  96.4 14.2 %collective-permute-start.1 = (bf16[256,128]{1,0:T(8,128)(2,1)S(1)}, bf16[256,128]{1,0:T(8,128)(2,1)}, u32[]{:S(2)}, u32[]{:S(2)}) collective-permute-start(bf16[256,128]{1,0:T(8,128)(2,1)S(1)} %copy.114), channel_id=1, source_target_pairs={{7,0},{0,1},{1,2},{2,3},{3,4},{4,5},{5,6},{6,7},{15,8},{8,9},{9,10... | collective-permute-start | bytes 196616 | tf_op jit(solution)/shard_map/while/body/eval_jaxpr/ppermute | solution.py:12
  97.3 13.4 %collective-permute-start = (bf16[256,128]{0,1:T(8,128)(2,1)S(1)}, bf16[256,128]{0,1:T(8,128)(2,1)}, u32[]{:S(2)}, u32[]{:S(2)}) collective-permute-start(bf16[256,128]{0,1:T(8,128)(2,1)S(1)} %copy.113), channel_id=1, source_target_pairs={{7,0},{0,1},{1,2},{2,3},{3,4},{4,5},{5,6},{6,7},{15,8},{8,9},{9,10... | collective-permute-start | bytes 196616 | tf_op jit(solution)/shard_map/while/body/eval_jaxpr/ppermute | solution.py:12
  102.3 8.4 %collective-permute-start.2 = (f32[256,128]{1,0:T(8,128)}, f32[256,128]{1,0:T(8,128)S(1)}, u32[]{:S(2)}, u32[]{:S(2)}) collective-permute-start(f32[256,128]{1,0:T(8,128)} %fusion.66), channel_id=1, source_target_pairs={{7,0},{0,1},{1,2},{2,3},{3,4},{4,5},{5,6},{6,7},{15,8},{8,9},{9,10... | collective-permute-start | bytes 393224 | tf_op jit(solution)/shard_map/while/body/eval_jaxpr/ppermute | solution.py:12
  106.7 8.7 %collective-permute-start.3 = (f32[256,128]{1,0:T(8,128)}, f32[256,128]{1,0:T(8,128)S(1)}, u32[]{:S(2)}, u32[]{:S(2)}) collective-permute-start(f32[256,128]{1,0:T(8,128)} %fusion.67), channel_id=1, source_target_pairs={{7,0},{0,1},{1,2},{2,3},{3,4},{4,5},{5,6},{6,7},{15,8},{8,9},{9,10... | collective-permute-start | bytes 393224 | tf_op jit(solution)/shard_map/while/body/eval_jaxpr/ppermute | solution.py:12
  115.4 4.5 copy-start.8
  116.0 14.8 %collective-permute-start.4 = (f32[256]{0:T(256)S(1)}, f32[256]{0:T(256)}, u32[]{:S(2)}, u32[]{:S(2)}) collective-permute-start(f32[256]{0:T(256)S(1)} %copy.117), channel_id=1, source_target_pairs={{7,0},{0,1},{1,2},{2,3},{3,4},{4,5},{5,6},{6,7},{15,8},{8,9},{9,10... | collective-permute-start | bytes 3080 | tf_op jit(solution)/shard_map/while/body/eval_jaxpr/ppermute | solution.py:12
  116.9 14.0 %collective-permute-start.1 = (bf16[256,128]{1,0:T(8,128)(2,1)S(1)}, bf16[256,128]{1,0:T(8,128)(2,1)}, u32[]{:S(2)}, u32[]{:S(2)}) collective-permute-start(bf16[256,128]{1,0:T(8,128)(2,1)S(1)} %copy.114), channel_id=1, source_target_pairs={{7,0},{0,1},{1,2},{2,3},{3,4},{4,5},{5,6},{6,7},{15,8},{8,9},{9,10... | collective-permute-start | bytes 196616 | tf_op jit(solution)/shard_map/while/body/eval_jaxpr/ppermute | solution.py:12
  117.7 13.1 %collective-permute-start = (bf16[256,128]{0,1:T(8,128)(2,1)S(1)}, bf16[256,128]{0,1:T(8,128)(2,1)}, u32[]{:S(2)}, u32[]{:S(2)}) collective-permute-start(bf16[256,128]{0,1:T(8,128)(2,1)S(1)} %copy.113), channel_id=1, source_target_pairs={{7,0},{0,1},{1,2},{2,3},{3,4},{4,5},{5,6},{6,7},{15,8},{8,9},{9,10... | collective-permute-start | bytes 196616 | tf_op jit(solution)/shard_map/while/body/eval_jaxpr/ppermute | solution.py:12
  122.0 8.8 %collective-permute-start.2 = (f32[256,128]{1,0:T(8,128)}, f32[256,128]{1,0:T(8,128)S(1)}, u32[]{:S(2)}, u32[]{:S(2)}) collective-permute-start(f32[256,128]{1,0:T(8,128)} %fusion.66), channel_id=1, source_target_pairs={{7,0},{0,1},{1,2},{2,3},{3,4},{4,5},{5,6},{6,7},{15,8},{8,9},{9,10... | collective-permute-start | bytes 393224 | tf_op jit(solution)/shard_map/while/body/eval_jaxpr/ppermute | solution.py:12
  126.9 7.3 %collective-permute-start.3 = (f32[256,128]{1,0:T(8,128)}, f32[256,128]{1,0:T(8,128)S(1)}, u32[]{:S(2)}, u32[]{:S(2)}) collective-permute-start(f32[256,128]{1,0:T(8,128)} %fusion.67), channel_id=1, source_target_pairs={{7,0},{0,1},{1,2},{2,3},{3,4},{4,5},{5,6},{6,7},{15,8},{8,9},{9,10... | collective-permute-start | bytes 393224 | tf_op jit(solution)/shard_map/while/body/eval_jaxpr/ppermute | solution.py:12
  134.2 6.1 %copy-start.8 = (f32[1,256,8]{1,2,0:T(8,128)S(1)}, f32[1,256,8]{1,2,0:T(8,128)}, u32[]{:S(2)}) copy-start(f32[1,256,8]{1,2,0:T(8,128)} %get-tuple-element.274) | copy-start | bytes 24580 | tf_op jit(solution)/shard_map/while
  134.8 16.0 %collective-permute-start.4 = (f32[256]{0:T(256)S(1)}, f32[256]{0:T(256)}, u32[]{:S(2)}, u32[]{:S(2)}) collective-permute-start(f32[256]{0:T(256)S(1)} %copy.117), channel_id=1, source_target_pairs={{7,0},{0,1},{1,2},{2,3},{3,4},{4,5},{5,6},{6,7},{15,8},{8,9},{9,10... | collective-permute-start | bytes 3080 | tf_op jit(solution)/shard_map/while/body/eval_jaxpr/ppermute | solution.py:12
  135.7 15.1 %collective-permute-start.1 = (bf16[256,128]{1,0:T(8,128)(2,1)S(1)}, bf16[256,128]{1,0:T(8,128)(2,1)}, u32[]{:S(2)}, u32[]{:S(2)}) collective-permute-start(bf16[256,128]{1,0:T(8,128)(2,1)S(1)} %copy.114), channel_id=1, source_target_pairs={{7,0},{0,1},{1,2},{2,3},{3,4},{4,5},{5,6},{6,7},{15,8},{8,9},{9,10... | collective-permute-start | bytes 196616 | tf_op jit(solution)/shard_map/while/body/eval_jaxpr/ppermute | solution.py:12
  136.5 14.3 %collective-permute-start = (bf16[256,128]{0,1:T(8,128)(2,1)S(1)}, bf16[256,128]{0,1:T(8,128)(2,1)}, u32[]{:S(2)}, u32[]{:S(2)}) collective-permute-start(bf16[256,128]{0,1:T(8,128)(2,1)S(1)} %copy.113), channel_id=1, source_target_pairs={{7,0},{0,1},{1,2},{2,3},{3,4},{4,5},{5,6},{6,7},{15,8},{8,9},{9,10... | collective-permute-start | bytes 196616 | tf_op jit(solution)/shard_map/while/body/eval_jaxpr/ppermute | solution.py:12
  142.5 8.4 %collective-permute-start.2 = (f32[256,128]{1,0:T(8,128)}, f32[256,128]{1,0:T(8,128)S(1)}, u32[]{:S(2)}, u32[]{:S(2)}) collective-permute-start(f32[256,128]{1,0:T(8,128)} %fusion.66), channel_id=1, source_target_pairs={{7,0},{0,1},{1,2},{2,3},{3,4},{4,5},{5,6},{6,7},{15,8},{8,9},{9,10... | collective-permute-start | bytes 393224 | tf_op jit(solution)/shard_map/while/body/eval_jaxpr/ppermute | solution.py:12
  146.9 8.6 %collective-permute-start.3 = (f32[256,128]{1,0:T(8,128)}, f32[256,128]{1,0:T(8,128)S(1)}, u32[]{:S(2)}, u32[]{:S(2)}) collective-permute-start(f32[256,128]{1,0:T(8,128)} %fusion.67), channel_id=1, source_target_pairs={{7,0},{0,1},{1,2},{2,3},{3,4},{4,5},{5,6},{6,7},{15,8},{8,9},{9,10... | collective-permute-start | bytes 393224 | tf_op jit(solution)/shard_map/while/body/eval_jaxpr/ppermute | solution.py:12
  155.5 2.5 copy-start.4
  155.5 2.5 copy-start.7
  158.0 1.4 copy-start.5
  159.4 1.0 copy-start.2
  159.8 7.2 %collective-permute-start.5 = (f32[256,128]{1,0:T(8,128)S(1)}, f32[256,128]{1,0:T(8,128)S(1)}, u32[]{:S(2)}, u32[]{:S(2)}) collective-permute-start(f32[256,128]{1,0:T(8,128)S(1)} %fusion.24), channel_id=1, source_target_pairs={{7,0},{0,1},{1,2},{2,3},{3,4},{4,5},{5,6},{6,7},{15,8},{8,9},{9,10... | collective-permute-start | bytes 393224 | tf_op jit(solution)/shard_map/ppermute | solution.py:12
  160.4 8.0 %collective-permute-start.6 = (f32[256,128]{1,0:T(8,128)S(1)}, f32[256,128]{1,0:T(8,128)S(1)}, u32[]{:S(2)}, u32[]{:S(2)}) collective-permute-start(f32[256,128]{1,0:T(8,128)S(1)} %fusion.25), channel_id=1, source_target_pairs={{7,0},{0,1},{1,2},{2,3},{3,4},{4,5},{5,6},{6,7},{15,8},{8,9},{9,10... | collective-permute-start | bytes 393224 | tf_op jit(solution)/shard_map/ppermute | solution.py:12
Sparse Core Ops, SparseCore 0:
  177.8 318.0 reduce-scatter.3
where the time goes:
time: 514 us; the launch traced here: 504 us
  waiting for transfers between devices  341 us (66%)
  local copies, waits for them, and re-layouts  45.6 us (9%)
  matrix products  41.7 us (8%)
  starting transfers between devices  37.1 us (7%)
  other arithmetic  23.6 us (5%)
  between operations  14.2 us (3%)
    unnamed x2, waiting for transfers between devices  308 us
    ppermute x37, starting transfers between devices, passed_along(): return lax.ppermute(block, axis, route)  37.1 us
    ppermute x37, waiting for transfers between devices, passed_along(): return lax.ppermute(block, axis, route)  33.5 us
    while x49, local copies, waits for them, and re-layouts  25.1 us
    add x7, other arithmetic, spin(): dq_acc + query_part  18.2 us
    unnamed x26, local copies, waits for them, and re-layouts  14.6 us
    dot_general x8, matrix products, block_grads(): jnp.einsum('hgqk,khd->qhgd', dscores_low, key_three, preferred_element_ty...  11.7 us
  transfers between devices with their start and end apart: 38, of which 12 were waited for; matrix products, arithmetic and copies ran while one was open for 16% of the time, Pallas kernels for 0%

commit v1 on v0

v1 whole, which is shorter than its diff:
```python
import math

import jax
import jax.numpy as jnp
from jax import lax
from jax.experimental import pallas as pl
from jax.experimental.pallas import tpu as pltpu
from jax.sharding import PartitionSpec as P

HD = 128
RUN = 128
PAD = 16
FACTOR = HD ** (-0.5)
LOG2E = math.log2(math.e)
BF16 = jnp.bfloat16
F32 = jnp.float32

ROWS_ROWS = (((1,), (1,)), ((), ()))
COLS_ROWS = (((1,), (0,)), ((), ()))
COLS_COLS = (((0,), (0,)), ((), ()))


def dot(a, b, dims):
    return lax.dot_general(a, b, dims, preferred_element_type=F32)


def attention_kernel(
    query_ref, grad_ref, out_ref, lse_ref, pos_ref, kv_ref, dq_ref, dkv_ref, acc, lse_t
):
    head = pl.program_id(0)
    blocks, rows, _ = kv_ref.shape
    keys = rows - PAD
    tokens = query_ref.shape[0]

    @pl.when(head == 0)
    def _():
        acc[...] = jnp.zeros_like(acc)
        lse_t[...] = jnp.transpose(lse_ref[...]) * LOG2E

    query = query_ref[...]
    grad = grad_ref[...]
    delta = jnp.sum(
        jnp.transpose(grad.astype(F32) * out_ref[...].astype(F32)), axis=0, keepdims=True
    )
    lse = lse_t[pl.ds(head, 1), :]
    query_pos = pos_ref[...].astype(F32)
    offsets = lax.broadcasted_iota(jnp.int32, (RUN, tokens), 0).astype(F32)
    dq = jnp.zeros((tokens, HD), F32)
    for block in range(blocks):
        key = kv_ref[block, :keys, :HD]
        value = kv_ref[block, :keys, HD:]
        scores = dot(key, query, ROWS_ROWS)
        probs = jnp.exp2(scores * (FACTOR * LOG2E) - lse)
        visible = []
        for run in range(keys // RUN):
            start = kv_ref[block, keys + run : keys + run + 1, :1].astype(F32) * RUN
            visible.append(offsets <= query_pos - start)
        probs = jnp.where(jnp.concatenate(visible, axis=0), probs, 0.0)
        dprobs = dot(value, grad, ROWS_ROWS)
        dscores = (probs * (dprobs - delta)).astype(BF16)
        probs = probs.astype(BF16)
        acc[block, :, HD:] += dot(probs, grad, COLS_ROWS)
        acc[block, :, :HD] += dot(dscores, query, COLS_ROWS)
        dq += dot(dscores, key, COLS_COLS)
    dq_ref[...] = dq * FACTOR

    @pl.when(head == pl.num_programs(0) - 1)
    def _():
        dkv_ref[:, :, :HD] = (acc[:, :, :HD] * FACTOR).astype(BF16)
        dkv_ref[:, :, HD:] = acc[:, :, HD:].astype(BF16)


def attention(query, grad, out, lse, pos, kv):
    tokens, width = query.shape
    heads = width // HD
    blocks, rows, cols = kv.shape
    keys = rows - PAD
    by_head = pl.BlockSpec((tokens, HD), lambda h: (0, h))

    def whole(*shape):
        return pl.BlockSpec(shape, lambda h: (0,) * len(shape))

    return pl.pallas_call(
        attention_kernel,
        grid=(heads,),
        in_specs=[
            by_head,
            by_head,
            by_head,
            whole(tokens, heads),
            whole(1, tokens),
            whole(blocks, rows, cols),
        ],
        out_specs=[by_head, whole(blocks, keys, cols)],
        out_shape=[
            jax.ShapeDtypeStruct((tokens, width), F32),
            jax.ShapeDtypeStruct((blocks, keys, cols), BF16),
        ],
        scratch_shapes=[pltpu.VMEM((blocks, keys, cols), F32), pltpu.VMEM((heads, tokens), F32)],
        compiler_params=pltpu.CompilerParams(vmem_limit_bytes=40 * 2**20),
        cost_estimate=pl.CostEstimate(
            flops=10 * blocks * keys * tokens * width,
            bytes_accessed=12 * 2**20,
            transcendentals=blocks * keys * tokens * heads,
        ),
    )(query, grad, out, lse, pos, kv)


def spread_kernel(in_ref, out_ref):
    parts, _, rows, tokens = out_ref.shape
    out_ref[...] = jnp.transpose(in_ref[...]).reshape(parts, 1, rows, tokens)


def spread(inputs, outer, inner):
    tokens, width = inputs.shape
    rows = width // (outer * inner)
    return pl.pallas_call(
        spread_kernel,
        grid=(outer,),
        in_specs=[pl.BlockSpec((tokens, inner * rows), lambda i: (0, i))],
        out_specs=pl.BlockSpec((inner, 1, rows, tokens), lambda i: (0, i, 0, 0)),
        out_shape=jax.ShapeDtypeStruct((inner, outer, rows, tokens), inputs.dtype),
        compiler_params=pltpu.CompilerParams(vmem_limit_bytes=40 * 2**20),
    )(inputs)


def exchange(parts, axis):
    return lax.all_to_all(parts, axis, 0, 0, tiled=True)


def to_all(block, axis):
    return exchange(jnp.broadcast_to(block, (lax.axis_size(axis),) + block.shape), axis)


def shards(inputs, queries, keys, values, outputs, out_grad, lse, positions):
    tokens = queries.shape[1]
    ctx = lax.axis_size("ctx")
    dp = lax.axis_size("dp")
    runs = tokens // RUN
    starts = (positions[0, ::RUN] // RUN).astype(BF16)
    starts = jnp.broadcast_to(starts[:, None], (runs, 2 * HD))
    kv = jnp.concatenate(
        [
            jnp.concatenate([keys[0], values[0]], axis=1),
            starts,
            jnp.zeros((PAD - runs, 2 * HD), BF16),
        ]
    )
    kv = to_all(kv, "ctx")
    turned = exchange(spread(inputs[0], dp, ctx), "ctx")
    query_grad, partial = attention(
        queries[0], out_grad[0], outputs[0], lse[0], positions, kv
    )
    both = jnp.sum(exchange(partial, "ctx").astype(F32), axis=0)
    kv_low = to_all(both.astype(BF16), "ctx")
    terms = jnp.einsum("sdrt,stc->drc", turned, kv_low, preferred_element_type=F32)
    weight_grad = jnp.sum(exchange(terms.astype(BF16), "dp").astype(F32), axis=0)
    return (query_grad[None], both[None, :, :HD], both[None, :, HD:], weight_grad)


def solution(mesh):
    return jax.shard_map(
        shards,
        mesh=mesh,
        in_specs=(
            P("dp", "ctx", None),
            P("dp", "ctx", "heads"),
            P("dp", "ctx", "heads"),
            P("dp", "ctx", "heads"),
            P("dp", "ctx", "heads"),
            P("dp", "ctx", "heads"),
            P("dp", "ctx", "heads"),
            P("dp", "ctx"),
        ),
        out_specs=(
            P("dp", "ctx", "heads"),
            P("dp", "ctx", "heads"),
            P("dp", "ctx", "heads"),
            P(("dp", "ctx"), "heads"),
        ),
        check_vma=False,
    )
```

time: 514 us -> 148 us (0.29); the launches traced: 504 us -> 148 us
  waiting for transfers between devices: 341 us -> 66.5 us
  matrix products: 41.7 us -> 1.57 us
  local copies, waits for them, and re-layouts: 45.6 us -> 8.22 us
  Pallas kernels: 0 us -> 25.8 us
  other arithmetic: 23.6 us -> 3.1 us
  blocking collectives: 0 us -> 18.5 us
  starting transfers between devices: 37.1 us -> 23.2 us
  between operations: 14.2 us -> 0.71 us
    unnamed x2 -> x0, waiting for transfers between devices: 308 us -> none
    all_to_all x0 -> x4, waiting for transfers between devices: none -> 66.5 us  [exchange(): return lax.all_to_all(parts, axis, 0, 0, tiled=True)]
    dot_general x41 -> x1, matrix products: 41.7 us -> 1.57 us  [shards(): jnp.einsum('sdrt,stc->drc', turned, kv_low, preferred_element_type=F32)]
    ppermute x37 -> x0, starting transfers between devices: 37.1 us -> none  [passed_along(): return lax.ppermute(block, axis, route)]
    ppermute x37 -> x0, waiting for transfers between devices: 33.5 us -> none  [passed_along(): return lax.ppermute(block, axis, route)]
    while x50 -> x0, local copies, waits for them, and re-layouts: 27.6 us -> none
    pallas_call x0 -> x2, Pallas kernels: none -> 25.8 us  [the longest x1 21.8 us: attention(): pl.pallas_call(attention_kernel, grid=(heads,), in_specs=[by_head, by_hea...]
    all_to_all x0 -> x4, starting transfers between devices: none -> 23.2 us  [exchange(): return lax.all_to_all(parts, axis, 0, 0, tiled=True)]
  transfers between devices with their start and end apart: 38 -> 4, of which waited for: 12 -> 4; matrix products, arithmetic and copies ran while one was open for 16% -> 2% of each run, Pallas kernels for 0% -> 3%
where the time goes in v1:
time: 148 us
  waiting for transfers between devices  66.5 us (45%)
  Pallas kernels  25.8 us (17%)
  starting transfers between devices  23.2 us (16%)
  blocking collectives  18.5 us (12%)
  local copies, waits for them, and re-layouts  8.22 us (6%)
  other arithmetic  3.1 us (2%)
  matrix products  1.57 us (1%)
    all_to_all x4, waiting for transfers between devices, exchange(): return lax.all_to_all(parts, axis, 0, 0, tiled=True)  66.5 us
    all_to_all x4, starting transfers between devices, exchange(): return lax.all_to_all(parts, axis, 0, 0, tiled=True)  23.2 us
    pallas_call x1, Pallas kernels, attention(): pl.pallas_call(attention_kernel, grid=(heads,), in_specs=[by_head, by_hea...  21.8 us
    all_to_all x1, blocking collectives, exchange(): return lax.all_to_all(parts, axis, 0, 0, tiled=True)  18.5 us
    unnamed x19, local copies, waits for them, and re-layouts  5.45 us
    pallas_call x1, Pallas kernels, spread(): pl.pallas_call(spread_kernel, grid=(outer,), in_specs=[pl.BlockSpec((toke...  3.92 us
  transfers between devices with their start and end apart: 4, of which 4 were waited for; matrix products, arithmetic and copies ran while one was open for 2% of the time, Pallas kernels for 3%

profile of v1, /device:TPU:6, one launch (start us, length us, event | category | flops | bytes accessed | tf_op | source)
XLA Modules:
  0.0 147.6 jit_solution(784706541011951580)
XLA Ops:
  0.6 0.0 copy-start.7
  0.6 0.0 copy-start.8
  0.7 0.0 copy-start.4
  0.7 0.8 slice.9
  1.5 0.1 pad.3.clone
  1.6 1.0 maximum_maximum_fusion
  2.6 1.1 broadcast_in_dim.26
  3.7 5.9 %all-to-all-start = ((bf16[8,272,256]{2,1,0:T(8,128)(2,1)}), bf16[8,272,256]{2,1,0:T(8,128)(2,1)S(1)}, u32[]{:S(2)}, u32[]{:S(2)}) async-start(bf16[8,272,256]{2,1,0:T(8,128)(2,1)} %broadcast_in_dim.26), calls=%async_computation | async-start | bytes 2228224 | tf_op jit(solution)/shard_map/all_to_all | solution.py:128
  9.6 0.0 copy-done.8
  9.6 0.1 copy.12
  9.7 14.8 %all-to-all-done.kv_ref = bf16[8,272,256]{2,1,0:T(8,128)(2,1)S(1)} async-done(((bf16[8,272,256]{2,1,0:T(8,128)(2,1)}), bf16[8,272,256]{2,1,0:T(8,128)(2,1)S(1)}, u32[]{:S(2)}, u32[]{:S(2)}) %all-to-all-start) | async-done | bytes 1114144 | tf_op jit(solution)/shard_map/all_to_all | solution.py:128
  24.6 0.0 copy-start.1
  24.6 1.0 copy-done.1
  25.6 0.0 copy-done.7
  25.6 0.0 copy-done.4
  25.6 0.0 copy-start.2
  25.6 1.2 copy-done.2
  26.8 0.0 copy-start.5
  26.8 1.0 copy-done.5
  27.9 0.0 copy-start.6
  27.9 1.0 copy-done.6
  28.9 0.0 copy-start
  28.9 21.8 %shard_map.111 = (f32[256,1024]{1,0:T(8,128)}, bf16[8,256,256]{2,1,0:T(8,128)(2,1)S(1)}) custom-call(bf16[256,1024]{1,0:T(8,128)(2,1)S(1)} %bitcast.41, bf16[256,1024]{1,0:T(8,128)(2,1)S(1)} %bitcast.42, bf16[256,1024]{1,0:T(8,128)(2,1)S(1)} %bitcast.43, f32[256,8]{1,0:T(8,128)S(1)} %bitcast.40, s32[1,256]{1,0:T(1,128)S(1)} %copy-done.7, ...), custom_call_target="tpu_custom_call" | custom-call | flops 5368709120 | bytes 12582912 | tf_op jit(solution)/shard_map/pallas_call | solution.py:83
  50.7 0.0 copy-start.3
  50.7 1.0 copy-done.3
  51.7 4.7 %all-to-all-start.1 = ((bf16[8,256,256]{2,1,0:T(8,128)(2,1)}), bf16[8,256,256]{2,1,0:T(8,128)(2,1)}, u32[]{:S(2)}, u32[]{:S(2)}) async-start(bf16[8,256,256]{2,1,0:T(8,128)(2,1)} %copy-done.3), calls=%async_computation.1 | async-start | bytes 2097152 | tf_op jit(solution)/shard_map/all_to_all | solution.py:128
  56.4 0.0 copy-done
  56.4 3.9 %shard_map.112 = bf16[8,8,80,256]{3,2,1,0:T(8,128)(2,1)} custom-call(bf16[256,5120]{1,0:T(8,128)(2,1)S(1)} %bitcast.39), custom_call_target="tpu_custom_call" | custom-call | tf_op jit(solution)/shard_map/pallas_call | solution.py:117
  60.3 10.6 %all-to-all-done.1 = bf16[8,256,256]{2,1,0:T(8,128)(2,1)} async-done(((bf16[8,256,256]{2,1,0:T(8,128)(2,1)}), bf16[8,256,256]{2,1,0:T(8,128)(2,1)}, u32[]{:S(2)}, u32[]{:S(2)}) %all-to-all-start.1) | async-done | bytes 1048608 | tf_op jit(solution)/shard_map/all_to_all | solution.py:128
  70.9 4.2 %all-to-all-start.3 = ((bf16[8,8,80,256]{3,2,1,0:T(8,128)(2,1)}), bf16[8,8,80,256]{3,2,1,0:T(8,128)(2,1)S(1)}, u32[]{:S(2)}, u32[]{:S(2)}) async-start(bf16[8,8,80,256]{3,2,1,0:T(8,128)(2,1)} %shard_map.112), calls=%async_computation.3 | async-start | bytes 5242880 | tf_op jit(solution)/shard_map/all_to_all | solution.py:128
  75.0 1.4 convert_reduce_fusion
  76.5 29.9 %all-to-all-done.3 = bf16[8,8,80,256]{3,2,1,0:T(8,128)(2,1)S(1)} async-done(((bf16[8,8,80,256]{3,2,1,0:T(8,128)(2,1)}), bf16[8,8,80,256]{3,2,1,0:T(8,128)(2,1)S(1)}, u32[]{:S(2)}, u32[]{:S(2)}) %all-to-all-start.3) | async-done | bytes 2621472 | tf_op jit(solution)/shard_map/all_to_all | solution.py:128
  106.3 0.1 broadcast_in_dim.30
  106.4 18.5 %all_to_all.25 = bf16[8,256,256]{2,1,0:T(8,128)(2,1)S(1)} all-to-all(bf16[8,256,256]{2,1,0:T(8,128)(2,1)S(1)} %broadcast_in_dim.30), channel_id=1, replica_groups=mesh['dp'=8,'heads'=4,'ctx'=8] {'ctx'}, dimensions={0} | all-to-all | bytes 2097152 | tf_op jit(solution)/shard_map/all_to_all | solution.py:128
  124.9 1.6 %fusion.1 = bf16[8,80,256]{2,1,0:T(8,128)(2,1)} fusion(bf16[8,8,80,256]{3,2,1,0:T(8,128)(2,1)S(1)} %all-to-all-done.3, bf16[8,256,256]{2,1,0:T(8,128)(2,1)S(1)} %all_to_all.25), kind=kOutput, calls=%fused_computation.3 | convolution fusion | flops 671252480 | bytes 3997696 | tf_op jit(solution)/shard_map/sdrt,stc->drc/dot_general | solution.py:156
  126.5 8.5 %all-to-all-start.4 = ((bf16[8,80,256]{2,1,0:T(8,128)(2,1)}), bf16[8,80,256]{2,1,0:T(8,128)(2,1)S(1)}, u32[]{:S(2)}, u32[]{:S(2)}) async-start(bf16[8,80,256]{2,1,0:T(8,128)(2,1)} %fusion.1), calls=%async_computation.4 | async-start | bytes 655360 | tf_op jit(solution)/shard_map/all_to_all | solution.py:128
  135.0 0.7 slice_bitcast_fusion
  135.7 11.3 %all-to-all-done.4 = bf16[8,80,256]{2,1,0:T(8,128)(2,1)S(1)} async-done(((bf16[8,80,256]{2,1,0:T(8,128)(2,1)}), bf16[8,80,256]{2,1,0:T(8,128)(2,1)S(1)}, u32[]{:S(2)}, u32[]{:S(2)}) %all-to-all-start.4) | async-done | bytes 327712 | tf_op jit(solution)/shard_map/all_to_all | solution.py:128
  146.9 0.7 convert_reduce_fusion.1
  (4 shorter events, 0.0 us)
Async XLA Ops:
  0.6 24.9 %copy-start.7 = (s32[1,256]{1,0:T(1,128)S(1)}, s32[1,256]{1,0:T(1,128)}, u32[]{:S(2)}) copy-start(s32[1,256]{1,0:T(1,128)} %pos_ref.1) | copy-start | bytes 3076
  0.6 9.0 %copy-start.8 = (f32[1,256,8]{1,2,0:T(8,128)S(1)}, f32[1,256,8]{1,2,0:T(8,128)}, u32[]{:S(2)}) copy-start(f32[1,256,8]{1,2,0:T(8,128)} %param.14) | copy-start | bytes 24580
  0.7 24.9 %copy-start.4 = (bf16[1,256,1024]{2,1,0:T(8,128)(2,1)S(1)}, bf16[1,256,1024]{2,1,0:T(8,128)(2,1)}, u32[]{:S(2)}) copy-start(bf16[1,256,1024]{2,1,0:T(8,128)(2,1)} %param.9) | copy-start | bytes 1572868
  3.7 20.9 %all-to-all-start = ((bf16[8,272,256]{2,1,0:T(8,128)(2,1)}), bf16[8,272,256]{2,1,0:T(8,128)(2,1)S(1)}, u32[]{:S(2)}, u32[]{:S(2)}) async-start(bf16[8,272,256]{2,1,0:T(8,128)(2,1)} %broadcast_in_dim.26), calls=%async_computation | async-start | bytes 2228224 | tf_op jit(solution)/shard_map/all_to_all | solution.py:128
  24.6 1.0 copy-start.1
  25.6 1.2 copy-start.2
  26.8 1.0 copy-start.5
  27.9 1.0 copy-start.6
  28.9 27.5 %copy-start = (bf16[1,256,5120]{2,1,0:T(8,128)(2,1)S(1)}, bf16[1,256,5120]{2,1,0:T(8,128)(2,1)}, u32[]{:S(2)}) copy-start(bf16[1,256,5120]{2,1,0:T(8,128)(2,1)} %param.8) | copy-start | bytes 7864324
  50.7 1.0 copy-start.3
  51.7 19.2 %all-to-all-start.1 = ((bf16[8,256,256]{2,1,0:T(8,128)(2,1)}), bf16[8,256,256]{2,1,0:T(8,128)(2,1)}, u32[]{:S(2)}, u32[]{:S(2)}) async-start(bf16[8,256,256]{2,1,0:T(8,128)(2,1)} %copy-done.3), calls=%async_computation.1 | async-start | bytes 2097152 | tf_op jit(solution)/shard_map/all_to_all | solution.py:128
  70.9 35.4 %all-to-all-start.3 = ((bf16[8,8,80,256]{3,2,1,0:T(8,128)(2,1)}), bf16[8,8,80,256]{3,2,1,0:T(8,128)(2,1)S(1)}, u32[]{:S(2)}, u32[]{:S(2)}) async-start(bf16[8,8,80,256]{3,2,1,0:T(8,128)(2,1)} %shard_map.112), calls=%async_computation.3 | async-start | bytes 5242880 | tf_op jit(solution)/shard_map/all_to_all | solution.py:128
  126.5 20.4 %all-to-all-start.4 = ((bf16[8,80,256]{2,1,0:T(8,128)(2,1)}), bf16[8,80,256]{2,1,0:T(8,128)(2,1)S(1)}, u32[]{:S(2)}, u32[]{:S(2)}) async-start(bf16[8,80,256]{2,1,0:T(8,128)(2,1)} %fusion.1), calls=%async_computation.4 | async-start | bytes 655360 | tf_op jit(solution)/shard_map/all_to_all | solution.py:128

commit v2 on v1

v2 whole, which is shorter than its diff:
```python
import math

import jax
import jax.numpy as jnp
from jax import lax
from jax.experimental import pallas as pl
from jax.experimental.pallas import tpu as pltpu
from jax.sharding import PartitionSpec as P

HD = 128
RUN = 128
PAD = 16
PAIR = 2
CHUNK = 1024
VMEM = 60 * 2**20
FACTOR = HD ** (-0.5)
LOG2E = math.log2(math.e)
BF16 = jnp.bfloat16
F32 = jnp.float32

ROWS_ROWS = (((1,), (1,)), ((), ()))
COLS_ROWS = (((1,), (0,)), ((), ()))


def dot(a, b, dims):
    return lax.dot_general(a, b, dims, preferred_element_type=F32)


def pack_kernel(key_ref, value_ref, pos_ref, out_ref):
    tokens = key_ref.shape[0]
    out_ref[0, :tokens, :HD] = key_ref[...]
    out_ref[0, :tokens, HD:] = value_ref[...]
    row = lax.broadcasted_iota(jnp.int32, (PAD, 2 * HD), 0)
    number = jnp.zeros((PAD, 2 * HD), F32)
    for run in range(tokens // RUN):
        first = pos_ref[:, run * RUN : run * RUN + 1].astype(F32) * (1.0 / RUN)
        number = jnp.where(row == run, first, number)
    out_ref[0, tokens:, :] = number.astype(BF16)


def packed(keys, values, pos, copies):
    tokens = keys.shape[0]
    return pl.pallas_call(
        pack_kernel,
        grid=(copies,),
        in_specs=[
            pl.BlockSpec((tokens, HD), lambda i: (0, 0)),
            pl.BlockSpec((tokens, HD), lambda i: (0, 0)),
            pl.BlockSpec((1, tokens), lambda i: (0, 0)),
        ],
        out_specs=pl.BlockSpec((1, tokens + PAD, 2 * HD), lambda i: (i, 0, 0)),
        out_shape=jax.ShapeDtypeStruct((copies, tokens + PAD, 2 * HD), BF16),
        compiler_params=pltpu.CompilerParams(vmem_limit_bytes=VMEM),
        name="pack",
    )(keys, values, pos)


def attention_kernel(
    query_ref, grad_ref, out_ref, lse_ref, pos_ref, kv_ref, dq_ref, dkv_ref, key, key_t, value, acc
):
    step = pl.program_id(0)
    blocks, rows, _ = kv_ref.shape
    keys = rows - PAD
    tokens = query_ref.shape[0]

    @pl.when(step == 0)
    def _():
        acc[...] = jnp.zeros_like(acc)
        for block in range(blocks):
            here = slice(block * keys, (block + 1) * keys)
            key[here, :] = kv_ref[block, :keys, :HD]
            value[here, :] = kv_ref[block, :keys, HD:]
            key_t[:, here] = jnp.transpose(kv_ref[block, :keys, :HD])

    query_pos = pos_ref[...].astype(F32)
    offsets = lax.broadcasted_iota(jnp.int32, (RUN, tokens), 0).astype(F32)
    for chunk in range(blocks * keys // CHUNK):
        here = slice(chunk * CHUNK, (chunk + 1) * CHUNK)
        visible = []
        for run in range(chunk * CHUNK // RUN, (chunk + 1) * CHUNK // RUN):
            block, row = run // (keys // RUN), keys + run % (keys // RUN)
            start = kv_ref[block, row : row + 1, :1].astype(F32) * RUN
            visible.append(offsets <= query_pos - start)
        visible = jnp.concatenate(visible, axis=0)
        key_part = None
        value_part = None
        for i in range(PAIR):
            cols = slice(i * HD, (i + 1) * HD)
            query = query_ref[:, cols]
            grad = grad_ref[:, cols]
            delta = jnp.sum(
                jnp.transpose(grad.astype(F32) * out_ref[:, cols].astype(F32)),
                axis=0,
                keepdims=True,
            )
            lse = lse_ref[pl.ds(step * PAIR + i, 1), :] * LOG2E
            scores = dot(key[here, :], query, ROWS_ROWS)
            probs = jnp.where(visible, jnp.exp2(scores * (FACTOR * LOG2E) - lse), 0.0)
            dprobs = dot(value[here, :], grad, ROWS_ROWS)
            dscores = (probs * (dprobs - delta)).astype(BF16)
            dv = dot(probs.astype(BF16), grad, COLS_ROWS)
            dk = dot(dscores, query, COLS_ROWS)
            dq = jnp.transpose(dot(key_t[:, here], dscores, COLS_ROWS)) * FACTOR
            if chunk == 0:
                dq_ref[:, cols] = dq
            else:
                dq_ref[:, cols] += dq
            key_part = dk if key_part is None else key_part + dk
            value_part = dv if value_part is None else value_part + dv
        acc[here, :HD] += key_part
        acc[here, HD:] += value_part

    @pl.when(step == pl.num_programs(0) - 1)
    def _():
        for block in range(blocks):
            here = slice(block * keys, (block + 1) * keys)
            dkv_ref[block, :, :HD] = (acc[here, :HD] * FACTOR).astype(BF16)
            dkv_ref[block, :, HD:] = acc[here, HD:].astype(BF16)


def attention(query, grad, out, lse, pos, kv):
    tokens, width = query.shape
    heads = width // HD
    blocks, rows, cols = kv.shape
    keys = rows - PAD
    by_head = pl.BlockSpec((tokens, PAIR * HD), lambda h: (0, h))

    def whole(*shape):
        return pl.BlockSpec(shape, lambda h: (0,) * len(shape))

    return pl.pallas_call(
        attention_kernel,
        grid=(heads // PAIR,),
        in_specs=[
            by_head,
            by_head,
            by_head,
            whole(heads, tokens),
            whole(1, tokens),
            whole(blocks, rows, cols),
        ],
        out_specs=[by_head, whole(blocks, keys, cols)],
        out_shape=[
            jax.ShapeDtypeStruct((tokens, width), F32),
            jax.ShapeDtypeStruct((blocks, keys, cols), BF16),
        ],
        scratch_shapes=[
            pltpu.VMEM((blocks * keys, HD), BF16),
            pltpu.VMEM((HD, blocks * keys), BF16),
            pltpu.VMEM((blocks * keys, HD), BF16),
            pltpu.VMEM((blocks * keys, cols), F32),
        ],
        compiler_params=pltpu.CompilerParams(vmem_limit_bytes=VMEM),
        cost_estimate=pl.CostEstimate(
            flops=10 * blocks * keys * tokens * width,
            bytes_accessed=12 * 2**20,
            transcendentals=blocks * keys * tokens * heads,
        ),
        name="attention",
    )(query, grad, out, lse, pos, kv)


def spread_kernel(half_ref, in_ref, out_ref):
    parts, _, rows, tokens = out_ref.shape
    out_ref[...] = jnp.transpose(in_ref[...]).reshape(parts, 1, rows, tokens)


def spread(inputs, half, outer, inner):
    tokens, width = inputs.shape
    tokens = tokens // 2
    rows = width // (outer * inner)
    return pl.pallas_call(
        spread_kernel,
        grid_spec=pltpu.PrefetchScalarGridSpec(
            num_scalar_prefetch=1,
            grid=(outer,),
            in_specs=[pl.BlockSpec((tokens, inner * rows), lambda i, h: (h[0], i))],
            out_specs=pl.BlockSpec((inner, 1, rows, tokens), lambda i, h: (0, i, 0, 0)),
        ),
        out_shape=jax.ShapeDtypeStruct((inner, outer, rows, tokens), inputs.dtype),
        compiler_params=pltpu.CompilerParams(vmem_limit_bytes=VMEM),
        name="spread",
    )(half, inputs)


def project_kernel(own_ref, other_ref, kv_ref, out_ref):
    blocks, _, tokens = own_ref.shape
    total = None
    for block in range(blocks):
        for half, ref in enumerate((own_ref, other_ref)):
            here = slice(half * tokens, (half + 1) * tokens)
            term = dot(ref[block], kv_ref[block, here, :], COLS_ROWS)
            total = term if total is None else total + term
    out_ref[...] = total.astype(BF16)


def project(own, other, kv):
    rows = own.shape[1]
    cols = kv.shape[2]
    return pl.pallas_call(
        project_kernel,
        out_shape=jax.ShapeDtypeStruct((rows, cols), BF16),
        compiler_params=pltpu.CompilerParams(vmem_limit_bytes=32 * 2**20),
        name="project",
    )(own, other, kv)


def exchange(parts, axis):
    return lax.all_to_all(parts, axis, 0, 0, tiled=True)


def with_neighbour(block):
    devices = range(lax.axis_size("heads"))
    return lax.ppermute(block, "heads", [(i, i ^ 1) for i in devices])


def shards(inputs, queries, keys, values, outputs, out_grad, lse, positions):
    tokens = queries.shape[1]
    ctx = lax.axis_size("ctx")
    dp = lax.axis_size("dp")
    half = lax.axis_index("heads") % 2
    kv = exchange(packed(keys[0], values[0], positions, ctx), "ctx")
    turned = spread(inputs[0], half.reshape(1), dp, ctx)
    kv, turned = lax.optimization_barrier((kv, turned))
    own = exchange(turned, "ctx")
    query_grad, partial = attention(
        queries[0], out_grad[0], outputs[0], jnp.transpose(lse[0]), positions, kv
    )
    partial, own = lax.optimization_barrier((partial, own))
    own = own.reshape(ctx, -1, tokens // 2)
    other = with_neighbour(own)
    both = jnp.sum(exchange(partial, "ctx").astype(F32), axis=0)
    kv_low = both.astype(BF16)
    kv_low = jnp.where(half == 0, kv_low, jnp.roll(kv_low, tokens // 2, axis=0))
    kv_low = exchange(jnp.broadcast_to(kv_low, (ctx,) + kv_low.shape), "ctx")
    terms = project(own, other, kv_low).reshape(dp, -1, 2 * HD)
    weight_grad = jnp.sum(exchange(terms, "dp").astype(F32), axis=0)
    return (query_grad[None], both[None, :, :HD], both[None, :, HD:], weight_grad)


def solution(mesh):
    return jax.shard_map(
        shards,
        mesh=mesh,
        in_specs=(
            P("dp", "ctx", None),
            P("dp", "ctx", "heads"),
            P("dp", "ctx", "heads"),
            P("dp", "ctx", "heads"),
            P("dp", "ctx", "heads"),
            P("dp", "ctx", "heads"),
            P("dp", "ctx", "heads"),
            P("dp", "ctx"),
        ),
        out_specs=(
            P("dp", "ctx", "heads"),
            P("dp", "ctx", "heads"),
            P("dp", "ctx", "heads"),
            P(("dp", "ctx"), "heads"),
        ),
        check_vma=False,
    )
```

time: 148 us -> 112 us (0.76)
  blocking collectives: 18.5 us -> 0 us
  waiting for transfers between devices: 66.5 us -> 53.3 us
  local copies, waits for them, and re-layouts: 8.22 us -> 1.77 us
  starting transfers between devices: 23.2 us -> 27 us
  other arithmetic: 3.1 us -> 0.87 us
  Pallas kernels: 25.8 us -> 27.6 us
  matrix products: 1.57 us -> 0 us
    all_to_all x1 -> x0, blocking collectives: 18.5 us -> none  [exchange(): return lax.all_to_all(parts, axis, 0, 0, tiled=True)]
    all_to_all x4 -> x5, waiting for transfers between devices: 66.5 us -> 53.3 us  [exchange(): return lax.all_to_all(parts, axis, 0, 0, tiled=True)]
    unnamed x19 -> x2, local copies, waits for them, and re-layouts: 5.45 us -> 0.01 us
    all_to_all x4 -> x5, starting transfers between devices: 23.2 us -> 27 us  [exchange(): return lax.all_to_all(parts, axis, 0, 0, tiled=True)]
    pallas_call x2 -> x4, Pallas kernels: 25.8 us -> 27.6 us  [the longest x1 14.4 us: attention(): pl.pallas_call(attention_kernel, grid=(heads // PAIR,), in_specs=[by_head...]
    dot_general x1 -> x0, matrix products: 1.57 us -> none  [shards(): jnp.einsum('sdrt,stc->drc', turned, kv_low, preferred_element_type=F32)]
  transfers between devices with their start and end apart: 4 -> 6, of which waited for: 4 -> 5; matrix products, arithmetic and copies ran while one was open for 2% -> 2% of each run, Pallas kernels for 3% -> 18%
where the time goes in v2:
time: 112 us; the launch traced here: 111 us
  waiting for transfers between devices  53.3 us (48%)
  Pallas kernels  27.6 us (25%)
  starting transfers between devices  27 us (24%)
  local copies, waits for them, and re-layouts  1.77 us (2%)
    all_to_all x5, waiting for transfers between devices, exchange(): return lax.all_to_all(parts, axis, 0, 0, tiled=True)  53.3 us
    all_to_all x5, starting transfers between devices, exchange(): return lax.all_to_all(parts, axis, 0, 0, tiled=True)  27 us
    pallas_call x1, Pallas kernels, attention(): pl.pallas_call(attention_kernel, grid=(heads // PAIR,), in_specs=[by_head...  14.4 us
    pallas_call x1, Pallas kernels, spread(): pl.pallas_call(spread_kernel, grid_spec=pltpu.PrefetchScalarGridSpec(num_...  5.67 us
    pallas_call x1, Pallas kernels, packed(): pl.pallas_call(pack_kernel, grid=(copies,), in_specs=[pl.BlockSpec((token...  3.9 us
    pallas_call x1, Pallas kernels, project(): pl.pallas_call(project_kernel, out_shape=jax.ShapeDtypeStruct((rows, cols...  3.54 us
  transfers between devices with their start and end apart: 6, of which 5 were waited for; matrix products, arithmetic and copies ran while one was open for 2% of the time, Pallas kernels for 18%

profile of v2, /device:TPU:6, one launch (start us, length us, event | category | flops | bytes accessed | tf_op | source)
XLA Modules:
  0.0 111.2 jit_solution(2315768437263810038)
XLA Ops:
  0.6 3.9 %pack.1 = bf16[8,272,256]{2,1,0:T(8,128)(2,1)} custom-call(bf16[256,128]{1,0:T(8,128)(2,1)} %bitcast.20, bf16[256,128]{1,0:T(8,128)(2,1)} %bitcast.21, s32[1,256]{1,0:T(1,128)} %pos_ref.3), custom_call_target="tpu_custom_call" | custom-call | tf_op jit(solution)/shard_map/pack/pallas_call | solution.py:43
  4.5 5.9 %all-to-all-start = ((bf16[8,272,256]{2,1,0:T(8,128)(2,1)}), bf16[8,272,256]{2,1,0:T(8,128)(2,1)S(1)}, u32[]{:S(2)}, u32[]{:S(2)}) async-start(bf16[8,272,256]{2,1,0:T(8,128)(2,1)} %pack.1), calls=%async_computation | async-start | bytes 2228224 | tf_op jit(solution)/shard_map/all_to_all | solution.py:209
  10.5 5.7 %spread.1 = bf16[8,8,80,128]{3,2,1,0:T(8,128)(2,1)} custom-call(s32[1]{0:T(128)} %bitcast.7.half_ref, bf16[256,5120]{1,0:T(8,128)(2,1)} %bitcast.19), custom_call_target="tpu_custom_call" | custom-call | tf_op jit(solution)/shard_map/spread/pallas_call | solution.py:172
  16.1 9.3 %all-to-all-done.kv_ref = bf16[8,272,256]{2,1,0:T(8,128)(2,1)S(1)} async-done(((bf16[8,272,256]{2,1,0:T(8,128)(2,1)}), bf16[8,272,256]{2,1,0:T(8,128)(2,1)S(1)}, u32[]{:S(2)}, u32[]{:S(2)}) %all-to-all-start) | async-done | bytes 1114144 | tf_op jit(solution)/shard_map/all_to_all | solution.py:209
  25.4 0.0 copy-start
  25.4 4.2 %all-to-all-start.1 = ((bf16[8,8,80,128]{3,2,1,0:T(8,128)(2,1)}), bf16[8,8,80,128]{3,2,1,0:T(8,128)(2,1)S(1)}, u32[]{:S(2)}, u32[]{:S(2)}) async-start(bf16[8,8,80,128]{3,2,1,0:T(8,128)(2,1)} %spread.1), calls=%async_computation.1 | async-start | bytes 2621440 | tf_op jit(solution)/shard_map/all_to_all | solution.py:209
  29.6 0.0 copy-done
  29.6 14.4 %attention.1 = (f32[256,1024]{1,0:T(8,128)}, bf16[8,256,256]{2,1,0:T(8,128)(2,1)}) custom-call(bf16[256,1024]{1,0:T(8,128)(2,1)} %bitcast.22, bf16[256,1024]{1,0:T(8,128)(2,1)} %bitcast.23, bf16[256,1024]{1,0:T(8,128)(2,1)} %bitcast.24, f32[8,256]{1,0:T(8,128)} %bitcast.25, s32[1,256]{1,0:T(1,128)} %pos_ref.3, bf16[8,272,256]{2,1,0:T(8,128)(2,1)} %copy-done), custom_call_target="tpu_custom_call" | custom-call | flops 5368709120 | bytes 12582912 | tf_op jit(solution)/shard_map/attention/pallas_call | solution.py:131
  44.1 2.8 %all-to-all-done.1 = bf16[8,8,80,128]{3,2,1,0:T(8,128)(2,1)S(1)} async-done(((bf16[8,8,80,128]{3,2,1,0:T(8,128)(2,1)}), bf16[8,8,80,128]{3,2,1,0:T(8,128)(2,1)S(1)}, u32[]{:S(2)}, u32[]{:S(2)}) %all-to-all-start.1) | async-done | bytes 1310752 | tf_op jit(solution)/shard_map/all_to_all | solution.py:209
  46.8 4.2 %all-to-all-start.2 = ((bf16[8,256,256]{2,1,0:T(8,128)(2,1)}), bf16[8,256,256]{2,1,0:T(8,128)(2,1)S(1)}, u32[]{:S(2)}, u32[]{:S(2)}) async-start(bf16[8,256,256]{2,1,0:T(8,128)(2,1)} %get-tuple-element.14), calls=%async_computation.2 | async-start | bytes 2097152 | tf_op jit(solution)/shard_map/all_to_all | solution.py:209
  51.0 0.0 collective-permute-start
  51.0 14.4 %all-to-all-done.2 = bf16[8,256,256]{2,1,0:T(8,128)(2,1)S(1)} async-done(((bf16[8,256,256]{2,1,0:T(8,128)(2,1)}), bf16[8,256,256]{2,1,0:T(8,128)(2,1)S(1)}, u32[]{:S(2)}, u32[]{:S(2)}) %all-to-all-start.2) | async-done | bytes 1048608 | tf_op jit(solution)/shard_map/all_to_all | solution.py:209
  65.5 0.1 convert_reduce_fusion
  65.7 1.0 broadcast_in_dim.15
  66.7 4.2 %all-to-all-start.3 = ((bf16[8,256,256]{2,1,0:T(8,128)(2,1)}), bf16[8,256,256]{2,1,0:T(8,128)(2,1)S(1)}, u32[]{:S(2)}, u32[]{:S(2)}) async-start(bf16[8,256,256]{2,1,0:T(8,128)(2,1)} %broadcast_in_dim.15), calls=%async_computation.3 | async-start | bytes 2097152 | tf_op jit(solution)/shard_map/all_to_all | solution.py:209
  70.9 0.0 collective-permute-done.other_ref
  70.9 14.4 %all-to-all-done.3.kv_ref = bf16[8,256,256]{2,1,0:T(8,128)(2,1)S(1)} async-done(((bf16[8,256,256]{2,1,0:T(8,128)(2,1)}), bf16[8,256,256]{2,1,0:T(8,128)(2,1)S(1)}, u32[]{:S(2)}, u32[]{:S(2)}) %all-to-all-start.3) | async-done | bytes 1048608 | tf_op jit(solution)/shard_map/all_to_all | solution.py:209
  85.3 3.5 %project.1 = bf16[640,256]{1,0:T(8,128)(2,1)} custom-call(bf16[8,640,128]{2,1,0:T(8,128)(2,1)S(1)} %bitcast.18, bf16[8,640,128]{2,1,0:T(8,128)(2,1)} %collective-permute-done.other_ref, bf16[8,256,256]{2,1,0:T(8,128)(2,1)S(1)} %all-to-all-done.3.kv_ref), custom_call_target="tpu_custom_call" | custom-call | tf_op jit(solution)/shard_map/project/pallas_call | solution.py:200
  88.9 8.5 %all-to-all-start.4 = ((bf16[8,80,256]{2,1,0:T(8,128)(2,1)}), bf16[8,80,256]{2,1,0:T(8,128)(2,1)S(1)}, u32[]{:S(2)}, u32[]{:S(2)}) async-start(bf16[8,80,256]{2,1,0:T(8,128)(2,1)} %bitcast.13), calls=%async_computation.4 | async-start | bytes 655360 | tf_op jit(solution)/shard_map/all_to_all | solution.py:209
  97.3 0.7 slice_bitcast_fusion
  98.1 12.4 %all-to-all-done.4 = bf16[8,80,256]{2,1,0:T(8,128)(2,1)S(1)} async-done(((bf16[8,80,256]{2,1,0:T(8,128)(2,1)}), bf16[8,80,256]{2,1,0:T(8,128)(2,1)S(1)}, u32[]{:S(2)}, u32[]{:S(2)}) %all-to-all-start.4) | async-done | bytes 327712 | tf_op jit(solution)/shard_map/all_to_all | solution.py:209
  110.5 0.7 convert_reduce_fusion.1
  (3 shorter events, 0.1 us)
Async XLA Ops:
  4.5 20.9 %all-to-all-start = ((bf16[8,272,256]{2,1,0:T(8,128)(2,1)}), bf16[8,272,256]{2,1,0:T(8,128)(2,1)S(1)}, u32[]{:S(2)}, u32[]{:S(2)}) async-start(bf16[8,272,256]{2,1,0:T(8,128)(2,1)} %pack.1), calls=%async_computation | async-start | bytes 2228224 | tf_op jit(solution)/shard_map/all_to_all | solution.py:209
  25.4 4.2 %copy-start = (bf16[8,272,256]{2,1,0:T(8,128)(2,1)}, bf16[8,272,256]{2,1,0:T(8,128)(2,1)S(1)}, u32[]{:S(2)}) copy-start(bf16[8,272,256]{2,1,0:T(8,128)(2,1)S(1)} %all-to-all-done.kv_ref) | copy-start | bytes 3342340
  25.4 21.4 %all-to-all-start.1 = ((bf16[8,8,80,128]{3,2,1,0:T(8,128)(2,1)}), bf16[8,8,80,128]{3,2,1,0:T(8,128)(2,1)S(1)}, u32[]{:S(2)}, u32[]{:S(2)}) async-start(bf16[8,8,80,128]{3,2,1,0:T(8,128)(2,1)} %spread.1), calls=%async_computation.1 | async-start | bytes 2621440 | tf_op jit(solution)/shard_map/all_to_all | solution.py:209
  46.8 18.6 %all-to-all-start.2 = ((bf16[8,256,256]{2,1,0:T(8,128)(2,1)}), bf16[8,256,256]{2,1,0:T(8,128)(2,1)S(1)}, u32[]{:S(2)}, u32[]{:S(2)}) async-start(bf16[8,256,256]{2,1,0:T(8,128)(2,1)} %get-tuple-element.14), calls=%async_computation.2 | async-start | bytes 2097152 | tf_op jit(solution)/shard_map/all_to_all | solution.py:209
  51.0 19.9 %collective-permute-start = (bf16[8,640,128]{2,1,0:T(8,128)(2,1)S(1)}, bf16[8,640,128]{2,1,0:T(8,128)(2,1)}, u32[]{:S(2)}, u32[]{:S(2)}) collective-permute-start(bf16[8,640,128]{2,1,0:T(8,128)(2,1)S(1)} %bitcast.17), channel_id=1, source_target_pairs={{0,8},{8,0},{16,24},{24,16},{1,9},{9,1},{17,25},{25,17},{2,10},{10... | collective-permute-start | bytes 3932168 | tf_op jit(solution)/shard_map/ppermute | solution.py:214
  66.7 18.6 %all-to-all-start.3 = ((bf16[8,256,256]{2,1,0:T(8,128)(2,1)}), bf16[8,256,256]{2,1,0:T(8,128)(2,1)S(1)}, u32[]{:S(2)}, u32[]{:S(2)}) async-start(bf16[8,256,256]{2,1,0:T(8,128)(2,1)} %broadcast_in_dim.15), calls=%async_computation.3 | async-start | bytes 2097152 | tf_op jit(solution)/shard_map/all_to_all | solution.py:209
  88.9 21.6 %all-to-all-start.4 = ((bf16[8,80,256]{2,1,0:T(8,128)(2,1)}), bf16[8,80,256]{2,1,0:T(8,128)(2,1)S(1)}, u32[]{:S(2)}, u32[]{:S(2)}) async-start(bf16[8,80,256]{2,1,0:T(8,128)(2,1)} %bitcast.13), calls=%async_computation.4 | async-start | bytes 655360 | tf_op jit(solution)/shard_map/all_to_all | solution.py:209

commit v3 on v2

--- a/solution.py
+++ b/solution.py
@@ -1,3 +1,4 @@
+import functools
 import math
 
 import jax
@@ -26,30 +27,32 @@
     return lax.dot_general(a, b, dims, preferred_element_type=F32)
 
 
-def pack_kernel(key_ref, value_ref, pos_ref, out_ref):
+def pack_kernel(key_ref, value_ref, pos_ref, out_ref, block, sems):
     tokens = key_ref.shape[0]
-    out_ref[0, :tokens, :HD] = key_ref[...]
-    out_ref[0, :tokens, HD:] = value_ref[...]
+    block[:tokens, :HD] = key_ref[...]
+    block[:tokens, HD:] = value_ref[...]
     row = lax.broadcasted_iota(jnp.int32, (PAD, 2 * HD), 0)
     number = jnp.zeros((PAD, 2 * HD), F32)
     for run in range(tokens // RUN):
         first = pos_ref[:, run * RUN : run * RUN + 1].astype(F32) * (1.0 / RUN)
         number = jnp.where(row == run, first, number)
-    out_ref[0, tokens:, :] = number.astype(BF16)
+    block[tokens:, :] = number.astype(BF16)
+    copies = [
+        pltpu.make_async_copy(block, out_ref.at[i], sems.at[i]) for i in range(out_ref.shape[0])
+    ]
+    for copy in copies:
+        copy.start()
+    for copy in copies:
+        copy.wait()
 
 
 def packed(keys, values, pos, copies):
-    tokens = keys.shape[0]
+    rows = keys.shape[0] + PAD
     return pl.pallas_call(
         pack_kernel,
-        grid=(copies,),
-        in_specs=[
-            pl.BlockSpec((tokens, HD), lambda i: (0, 0)),
-            pl.BlockSpec((tokens, HD), lambda i: (0, 0)),
-            pl.BlockSpec((1, tokens), lambda i: (0, 0)),
-        ],
-        out_specs=pl.BlockSpec((1, tokens + PAD, 2 * HD), lambda i: (i, 0, 0)),
-        out_shape=jax.ShapeDtypeStruct((copies, tokens + PAD, 2 * HD), BF16),
+        out_specs=pl.BlockSpec(memory_space=pl.ANY),
+        out_shape=jax.ShapeDtypeStruct((copies, rows, 2 * HD), BF16),
+        scratch_shapes=[pltpu.VMEM((rows, 2 * HD), BF16), pltpu.SemaphoreType.DMA((copies,))],
         compiler_params=pltpu.CompilerParams(vmem_limit_bytes=VMEM),
         name="pack",
     )(keys, values, pos)
@@ -160,49 +163,56 @@
     )(query, grad, out, lse, pos, kv)
 
 
-def spread_kernel(half_ref, in_ref, out_ref):
-    parts, _, rows, tokens = out_ref.shape
-    out_ref[...] = jnp.transpose(in_ref[...]).reshape(parts, 1, rows, tokens)
-
-
-def spread(inputs, half, outer, inner):
+def spread_kernel(half, outer, inner, turn_ref, in_ref, *refs):
+    out_ref, block, turned, in_sems, out_sems = refs[-5:]
+    tokens = block.shape[1]
+    width = block.shape[2]
+
+    @pl.when(turn_ref[0] == half)
+    def _():
+        here = pl.ds(pl.multiple_of(turn_ref[1] * tokens, tokens), tokens)
+        loads = [
+            pltpu.make_async_copy(
+                in_ref.at[here, pl.ds(i * width, width)], block.at[i], in_sems.at[i]
+            )
+            for i in range(outer)
+        ]
+        stores = [
+            pltpu.make_async_copy(turned.at[:, i], out_ref.at[:, i], out_sems.at[i])
+            for i in range(outer)
+        ]
+        for load in loads:
+            load.start()
+        for i in range(outer):
+            loads[i].wait()
+            turned[:, i] = jnp.transpose(block[i]).reshape(inner, width // inner, tokens)
+            stores[i].start()
+        for store in stores:
+            store.wait()
+
+
+def spread(inputs, turn, half, outer, inner, before=None):
     tokens, width = inputs.shape
     tokens = tokens // 2
-    rows = width // (outer * inner)
+    width = width // outer
+    shape = (inner, outer, width // inner, tokens)
+    given = () if before is None else (before,)
+    anywhere = pl.BlockSpec(memory_space=pl.ANY)
     return pl.pallas_call(
-        spread_kernel,
-        grid_spec=pltpu.PrefetchScalarGridSpec(
-            num_scalar_prefetch=1,
-            grid=(outer,),
-            in_specs=[pl.BlockSpec((tokens, inner * rows), lambda i, h: (h[0], i))],
-            out_specs=pl.BlockSpec((inner, 1, rows, tokens), lambda i, h: (0, i, 0, 0)),
-        ),
-        out_shape=jax.ShapeDtypeStruct((inner, outer, rows, tokens), inputs.dtype),
+        functools.partial(spread_kernel, half, outer, inner),
+        in_specs=[pl.BlockSpec(memory_space=pltpu.SMEM), anywhere] + [anywhere for _ in given],
+        out_specs=anywhere,
+        out_shape=jax.ShapeDtypeStruct(shape, inputs.dtype),
+        input_output_aliases={2: 0} if given else {},
+        scratch_shapes=[
+            pltpu.VMEM((outer, tokens, width), inputs.dtype),
+            pltpu.VMEM(shape, inputs.dtype),
+            pltpu.SemaphoreType.DMA((outer,)),
+            pltpu.SemaphoreType.DMA((outer,)),
+        ],
         compiler_params=pltpu.CompilerParams(vmem_limit_bytes=VMEM),
         name="spread",
-    )(half, inputs)
-
-
-def project_kernel(own_ref, other_ref, kv_ref, out_ref):
-    blocks, _, tokens = own_ref.shape
-    total = None
-    for block in range(blocks):
-        for half, ref in enumerate((own_ref, other_ref)):
-            here = slice(half * tokens, (half + 1) * tokens)
-            term = dot(ref[block], kv_ref[block, here, :], COLS_ROWS)
-            total = term if total is None else total + term
-    out_ref[...] = total.astype(BF16)
-
-
-def project(own, other, kv):
-    rows = own.shape[1]
-    cols = kv.shape[2]
-    return pl.pallas_call(
-        project_kernel,
-        out_shape=jax.ShapeDtypeStruct((rows, cols), BF16),
-        compiler_params=pltpu.CompilerParams(vmem_limit_bytes=32 * 2**20),
-        name="project",
-    )(own, other, kv)
+    )(turn, inputs, *given)
 
 
 def exchange(parts, axis):
@@ -219,8 +229,12 @@
     ctx = lax.axis_size("ctx")
     dp = lax.axis_size("dp")
     half = lax.axis_index("heads") % 2
-    kv = exchange(packed(keys[0], values[0], positions, ctx), "ctx")
-    turned = spread(inputs[0], half.reshape(1), dp, ctx)
+    turn = jnp.stack([half, half])
+    kv = packed(keys[0], values[0], positions, ctx)
+    turned = spread(inputs[0], turn, 1, dp, ctx)
+    kv, turned = lax.optimization_barrier((kv, turned))
+    kv = exchange(kv, "ctx")
+    turned = spread(inputs[0], turn, 0, dp, ctx, turned)
     kv, turned = lax.optimization_barrier((kv, turned))
     own = exchange(turned, "ctx")
     query_grad, partial = attention(
@@ -230,10 +244,15 @@
     own = own.reshape(ctx, -1, tokens // 2)
     other = with_neighbour(own)
     both = jnp.sum(exchange(partial, "ctx").astype(F32), axis=0)
-    kv_low = both.astype(BF16)
-    kv_low = jnp.where(half == 0, kv_low, jnp.roll(kv_low, tokens // 2, axis=0))
-    kv_low = exchange(jnp.broadcast_to(kv_low, (ctx,) + kv_low.shape), "ctx")
-    terms = project(own, other, kv_low).reshape(dp, -1, 2 * HD)
+    kv_low = jnp.broadcast_to(both.astype(BF16), (ctx,) + both.shape)
+    kv_low = exchange(kv_low, "ctx")
+    first = half == 0
+    turned = jnp.concatenate(
+        [jnp.where(first, own, other), jnp.where(first, other, own)], axis=2
+    )
+    kv_low, turned = lax.optimization_barrier((kv_low, turned))
+    terms = jnp.einsum("srt,stc->rc", turned, kv_low, preferred_element_type=F32)
+    terms = terms.astype(BF16).reshape(dp, -1, 2 * HD)
     weight_grad = jnp.sum(exchange(terms, "dp").astype(F32), axis=0)
     return (query_grad[None], both[None, :, :HD], both[None, :, HD:], weight_grad)
 

time: 112 us -> 112 us (level)
  Pallas kernels: 27.6 us -> 20.5 us
  matrix products: 0 us -> 2.78 us
  other arithmetic: 0.87 us -> 3.22 us
  waiting for transfers between devices: 53.3 us -> 55.1 us
    pallas_call x3, Pallas kernels: 13.1 us -> 6.07 us  [the longest x2 4.07 us: spread(): pl.pallas_call(functools.partial(spread_kernel, half, outer, inner), in_s...]
    dot_general x0 -> x1, matrix products: none -> 2.78 us  [shards(): jnp.einsum('srt,stc->rc', turned, kv_low, preferred_element_type=F32)]
    all_to_all x5, waiting for transfers between devices: 53.3 us -> 55.1 us  [exchange(): return lax.all_to_all(parts, axis, 0, 0, tiled=True)]
    select_n x1, other arithmetic: 0.03 us -> 1.49 us  [shards(): jnp.where(first, own, other)]
  transfers between devices with their start and end apart: 6 -> 6, of which waited for: 5 -> 5; matrix products, arithmetic and copies ran while one was open for 2% -> 3% of each run, Pallas kernels for 18% -> 16%
where the time goes in v3:
time: 112 us
  waiting for transfers between devices  55.1 us (49%)
  starting transfers between devices  27.8 us (25%)
  Pallas kernels  20.5 us (18%)
  other arithmetic  3.22 us (3%)
  matrix products  2.78 us (2%)
  local copies, waits for them, and re-layouts  1.78 us (2%)
    all_to_all x5, waiting for transfers between devices, exchange(): return lax.all_to_all(parts, axis, 0, 0, tiled=True)  55.1 us
    all_to_all x5, starting transfers between devices, exchange(): return lax.all_to_all(parts, axis, 0, 0, tiled=True)  27.8 us
    pallas_call x1, Pallas kernels, attention(): pl.pallas_call(attention_kernel, grid=(heads // PAIR,), in_specs=[by_head...  14.4 us
    pallas_call x2, Pallas kernels, spread(): pl.pallas_call(functools.partial(spread_kernel, half, outer, inner), in_s...  4.07 us
    dot_general x1, matrix products, shards(): jnp.einsum('srt,stc->rc', turned, kv_low, preferred_element_type=F32)  2.78 us
  transfers between devices with their start and end apart: 6, of which 5 were waited for; matrix products, arithmetic and copies ran while one was open for 3% of the time, Pallas kernels for 16%

profile of v3, /device:TPU:6, one launch (start us, length us, event | category | flops | bytes accessed | tf_op | source)
XLA Modules:
  0.0 111.9 jit_solution(10214956080996167189)
XLA Ops:
  0.6 0.6 pad_add_fusion.turn_ref
  1.2 0.8 spread.2.refs_0_
  2.0 2.0 %pack.1 = bf16[8,272,256]{2,1,0:T(8,128)(2,1)} custom-call(bf16[256,128]{1,0:T(8,128)(2,1)} %bitcast.28, bf16[256,128]{1,0:T(8,128)(2,1)} %bitcast.29, s32[1,256]{1,0:T(1,128)} %pos_ref.3), custom_call_target="tpu_custom_call" | custom-call | tf_op jit(solution)/shard_map/pack/pallas_call | solution.py:51
  4.1 5.9 %all-to-all-start = ((bf16[8,272,256]{2,1,0:T(8,128)(2,1)}), bf16[8,272,256]{2,1,0:T(8,128)(2,1)S(1)}, u32[]{:S(2)}, u32[]{:S(2)}) async-start(bf16[8,272,256]{2,1,0:T(8,128)(2,1)} %pack.1), calls=%async_computation | async-start | bytes 2228224 | tf_op jit(solution)/shard_map/all_to_all | solution.py:219
  10.0 3.3 %spread.3 = bf16[8,8,80,128]{3,2,1,0:T(8,128)(2,1)} custom-call(s32[2]{0:T(128)} %pad_add_fusion.turn_ref, bf16[256,5120]{1,0:T(8,128)(2,1)} %bitcast.26, bf16[8,8,80,128]{3,2,1,0:T(8,128)(2,1)} %spread.2.refs_0_), custom_call_target="tpu_custom_call", output_to_operand_aliasing={{}: (2, {})} | custom-call | tf_op jit(solution)/shard_map/spread/pallas_call | solution.py:201
  13.3 12.7 %all-to-all-done.kv_ref = bf16[8,272,256]{2,1,0:T(8,128)(2,1)S(1)} async-done(((bf16[8,272,256]{2,1,0:T(8,128)(2,1)}), bf16[8,272,256]{2,1,0:T(8,128)(2,1)S(1)}, u32[]{:S(2)}, u32[]{:S(2)}) %all-to-all-start) | async-done | bytes 1114144 | tf_op jit(solution)/shard_map/all_to_all | solution.py:219
  26.0 0.0 copy-start
  26.0 4.5 %all-to-all-start.1 = ((bf16[8,8,80,128]{3,2,1,0:T(8,128)(2,1)}), bf16[8,8,80,128]{3,2,1,0:T(8,128)(2,1)S(1)}, u32[]{:S(2)}, u32[]{:S(2)}) async-start(bf16[8,8,80,128]{3,2,1,0:T(8,128)(2,1)} %spread.3), calls=%async_computation.1 | async-start | bytes 2621440 | tf_op jit(solution)/shard_map/all_to_all | solution.py:219
  30.5 0.0 copy-done
  30.5 14.4 %attention.1 = (f32[256,1024]{1,0:T(8,128)}, bf16[8,256,256]{2,1,0:T(8,128)(2,1)}) custom-call(bf16[256,1024]{1,0:T(8,128)(2,1)} %bitcast.30, bf16[256,1024]{1,0:T(8,128)(2,1)} %bitcast.31, bf16[256,1024]{1,0:T(8,128)(2,1)} %bitcast.32, f32[8,256]{1,0:T(8,128)} %bitcast.33, s32[1,256]{1,0:T(1,128)} %pos_ref.3, bf16[8,272,256]{2,1,0:T(8,128)(2,1)} %copy-done), custom_call_target="tpu_custom_call" | custom-call | flops 5368709120 | bytes 12582912 | tf_op jit(solution)/shard_map/attention/pallas_call | solution.py:134
  44.9 2.9 %all-to-all-done.1 = bf16[8,8,80,128]{3,2,1,0:T(8,128)(2,1)S(1)} async-done(((bf16[8,8,80,128]{3,2,1,0:T(8,128)(2,1)}), bf16[8,8,80,128]{3,2,1,0:T(8,128)(2,1)S(1)}, u32[]{:S(2)}, u32[]{:S(2)}) %all-to-all-start.1) | async-done | bytes 1310752 | tf_op jit(solution)/shard_map/all_to_all | solution.py:219
  47.8 4.2 %all-to-all-start.2 = ((bf16[8,256,256]{2,1,0:T(8,128)(2,1)}), bf16[8,256,256]{2,1,0:T(8,128)(2,1)S(1)}, u32[]{:S(2)}, u32[]{:S(2)}) async-start(bf16[8,256,256]{2,1,0:T(8,128)(2,1)} %get-tuple-element.20), calls=%async_computation.2 | async-start | bytes 2097152 | tf_op jit(solution)/shard_map/all_to_all | solution.py:219
  52.0 0.0 collective-permute-start
  52.0 14.4 %all-to-all-done.2 = bf16[8,256,256]{2,1,0:T(8,128)(2,1)S(1)} async-done(((bf16[8,256,256]{2,1,0:T(8,128)(2,1)}), bf16[8,256,256]{2,1,0:T(8,128)(2,1)S(1)}, u32[]{:S(2)}, u32[]{:S(2)}) %all-to-all-start.2) | async-done | bytes 1048608 | tf_op jit(solution)/shard_map/all_to_all | solution.py:219
  66.4 0.1 convert_reduce_fusion
  66.6 1.1 broadcast_in_dim.15
  67.6 4.7 %all-to-all-start.3 = ((bf16[8,256,256]{2,1,0:T(8,128)(2,1)}), bf16[8,256,256]{2,1,0:T(8,128)(2,1)}, u32[]{:S(2)}, u32[]{:S(2)}) async-start(bf16[8,256,256]{2,1,0:T(8,128)(2,1)} %broadcast_in_dim.15), calls=%async_computation.3 | async-start | bytes 2097152 | tf_op jit(solution)/shard_map/all_to_all | solution.py:219
  72.3 0.0 collective-permute-done
  72.3 1.5 %broadcast_select_fusion.1 = (bf16[8,640,128]{2,1,0:T(8,128)(2,1)S(1)}, bf16[8,640,128]{2,1,0:T(8,128)(2,1)S(1)}) fusion(bf16[8,640,128]{2,1,0:T(8,128)(2,1)} %collective-permute-done, pred[]{:T(512)S(6)} %eq.5, bf16[8,8,80,128]{3,2,1,0:T(8,128)(2,1)S(1)} %all-to-all-done.1), kind=kLoop, calls=%fused_computation.3 | loop fusion | flops 1310720 | bytes 5242881 | tf_op jit(solution)/shard_map/jit(_where)/select_n | solution.py:251
  73.8 0.3 pad_maximum_fusion
  74.1 12.7 %all-to-all-done.3 = bf16[8,256,256]{2,1,0:T(8,128)(2,1)} async-done(((bf16[8,256,256]{2,1,0:T(8,128)(2,1)}), bf16[8,256,256]{2,1,0:T(8,128)(2,1)}, u32[]{:S(2)}, u32[]{:S(2)}) %all-to-all-start.3) | async-done | bytes 1048608 | tf_op jit(solution)/shard_map/all_to_all | solution.py:219
  86.8 2.8 %fusion = bf16[640,256]{1,0:T(8,128)(2,1)} fusion(bf16[8,640,256]{2,1,0:T(8,128)(2,1)S(1)} %pad_maximum_fusion, bf16[8,256,256]{2,1,0:T(8,128)(2,1)} %all-to-all-done.3), kind=kOutput, calls=%fused_computation.5 | convolution fusion | flops 671252480 | bytes 3997696 | tf_op jit(solution)/shard_map/srt,stc->rc/dot_general | solution.py:254
  89.6 8.5 %all-to-all-start.4 = ((bf16[8,80,256]{2,1,0:T(8,128)(2,1)}), bf16[8,80,256]{2,1,0:T(8,128)(2,1)S(1)}, u32[]{:S(2)}, u32[]{:S(2)}) async-start(bf16[8,80,256]{2,1,0:T(8,128)(2,1)} %bitcast.14), calls=%async_computation.4 | async-start | bytes 655360 | tf_op jit(solution)/shard_map/all_to_all | solution.py:219
  98.1 0.7 slice_bitcast_fusion
  98.8 12.4 %all-to-all-done.4 = bf16[8,80,256]{2,1,0:T(8,128)(2,1)S(1)} async-done(((bf16[8,80,256]{2,1,0:T(8,128)(2,1)}), bf16[8,80,256]{2,1,0:T(8,128)(2,1)S(1)}, u32[]{:S(2)}, u32[]{:S(2)}) %all-to-all-start.4) | async-done | bytes 327712 | tf_op jit(solution)/shard_map/all_to_all | solution.py:219
  111.2 0.7 convert_reduce_fusion.1
  (1 shorter events, 0.0 us)
Async XLA Ops:
  4.1 21.9 %all-to-all-start = ((bf16[8,272,256]{2,1,0:T(8,128)(2,1)}), bf16[8,272,256]{2,1,0:T(8,128)(2,1)S(1)}, u32[]{:S(2)}, u32[]{:S(2)}) async-start(bf16[8,272,256]{2,1,0:T(8,128)(2,1)} %pack.1), calls=%async_computation | async-start | bytes 2228224 | tf_op jit(solution)/shard_map/all_to_all | solution.py:219
  26.0 4.5 %copy-start = (bf16[8,272,256]{2,1,0:T(8,128)(2,1)}, bf16[8,272,256]{2,1,0:T(8,128)(2,1)S(1)}, u32[]{:S(2)}) copy-start(bf16[8,272,256]{2,1,0:T(8,128)(2,1)S(1)} %all-to-all-done.kv_ref) | copy-start | bytes 3342340
  26.0 21.8 %all-to-all-start.1 = ((bf16[8,8,80,128]{3,2,1,0:T(8,128)(2,1)}), bf16[8,8,80,128]{3,2,1,0:T(8,128)(2,1)S(1)}, u32[]{:S(2)}, u32[]{:S(2)}) async-start(bf16[8,8,80,128]{3,2,1,0:T(8,128)(2,1)} %spread.3), calls=%async_computation.1 | async-start | bytes 2621440 | tf_op jit(solution)/shard_map/all_to_all | solution.py:219
  47.8 18.6 %all-to-all-start.2 = ((bf16[8,256,256]{2,1,0:T(8,128)(2,1)}), bf16[8,256,256]{2,1,0:T(8,128)(2,1)S(1)}, u32[]{:S(2)}, u32[]{:S(2)}) async-start(bf16[8,256,256]{2,1,0:T(8,128)(2,1)} %get-tuple-element.20), calls=%async_computation.2 | async-start | bytes 2097152 | tf_op jit(solution)/shard_map/all_to_all | solution.py:219
  52.0 20.3 %collective-permute-start = (bf16[8,640,128]{2,1,0:T(8,128)(2,1)S(1)}, bf16[8,640,128]{2,1,0:T(8,128)(2,1)}, u32[]{:S(2)}, u32[]{:S(2)}) collective-permute-start(bf16[8,640,128]{2,1,0:T(8,128)(2,1)S(1)} %bitcast.27), channel_id=1, source_target_pairs={{0,8},{8,0},{16,24},{24,16},{1,9},{9,1},{17,25},{25,17},{2,10},{10... | collective-permute-start | bytes 3932168 | tf_op jit(solution)/shard_map/ppermute | solution.py:224
  67.6 19.2 %all-to-all-start.3 = ((bf16[8,256,256]{2,1,0:T(8,128)(2,1)}), bf16[8,256,256]{2,1,0:T(8,128)(2,1)}, u32[]{:S(2)}, u32[]{:S(2)}) async-start(bf16[8,256,256]{2,1,0:T(8,128)(2,1)} %broadcast_in_dim.15), calls=%async_computation.3 | async-start | bytes 2097152 | tf_op jit(solution)/shard_map/all_to_all | solution.py:219
  89.6 21.6 %all-to-all-start.4 = ((bf16[8,80,256]{2,1,0:T(8,128)(2,1)}), bf16[8,80,256]{2,1,0:T(8,128)(2,1)S(1)}, u32[]{:S(2)}, u32[]{:S(2)}) async-start(bf16[8,80,256]{2,1,0:T(8,128)(2,1)} %bitcast.14), calls=%async_computation.4 | async-start | bytes 655360 | tf_op jit(solution)/shard_map/all_to_all | solution.py:219

commit v4 on v3

--- a/solution.py
+++ b/solution.py
@@ -14,6 +14,8 @@
 PAIR = 2
 CHUNK = 1024
 VMEM = 60 * 2**20
+CTX_ORDER = (0, 6)
+DP_ORDER = (2, 6)
 FACTOR = HD ** (-0.5)
 LOG2E = math.log2(math.e)
 BF16 = jnp.bfloat16
@@ -163,47 +165,46 @@
     )(query, grad, out, lse, pos, kv)
 
 
-def spread_kernel(half, outer, inner, turn_ref, in_ref, *refs):
-    out_ref, block, turned, in_sems, out_sems = refs[-5:]
+def spread_kernel(outer, inner, half_ref, in_ref, out_ref, block, turned, in_sems, out_sems):
+    half = half_ref[0]
+    mask = jnp.where(half == 0, CTX_ORDER[0], CTX_ORDER[1])
     tokens = block.shape[1]
     width = block.shape[2]
-
-    @pl.when(turn_ref[0] == half)
-    def _():
-        here = pl.ds(pl.multiple_of(turn_ref[1] * tokens, tokens), tokens)
-        loads = [
-            pltpu.make_async_copy(
-                in_ref.at[here, pl.ds(i * width, width)], block.at[i], in_sems.at[i]
-            )
-            for i in range(outer)
-        ]
-        stores = [
-            pltpu.make_async_copy(turned.at[:, i], out_ref.at[:, i], out_sems.at[i])
-            for i in range(outer)
-        ]
-        for load in loads:
-            load.start()
-        for i in range(outer):
-            loads[i].wait()
-            turned[:, i] = jnp.transpose(block[i]).reshape(inner, width // inner, tokens)
-            stores[i].start()
-        for store in stores:
-            store.wait()
-
-
-def spread(inputs, turn, half, outer, inner, before=None):
+    rows = width // inner
+    here = pl.ds(pl.multiple_of(half * tokens, tokens), tokens)
+    loads = [
+        pltpu.make_async_copy(
+            in_ref.at[here, pl.ds(i * width, width)], block.at[i], in_sems.at[i]
+        )
+        for i in range(outer)
+    ]
+    stores = [
+        pltpu.make_async_copy(turned.at[:, i], out_ref.at[:, i], out_sems.at[i])
+        for i in range(outer)
+    ]
+    for load in loads:
+        load.start()
+    for i in range(outer):
+        loads[i].wait()
+        columns = jnp.transpose(block[i])
+        for piece in range(inner):
+            turned[jnp.bitwise_xor(piece, mask), i] = columns[piece * rows : (piece + 1) * rows]
+        stores[i].start()
+    for store in stores:
+        store.wait()
+
+
+def spread(inputs, half, outer, inner):
     tokens, width = inputs.shape
     tokens = tokens // 2
     width = width // outer
     shape = (inner, outer, width // inner, tokens)
-    given = () if before is None else (before,)
     anywhere = pl.BlockSpec(memory_space=pl.ANY)
     return pl.pallas_call(
-        functools.partial(spread_kernel, half, outer, inner),
-        in_specs=[pl.BlockSpec(memory_space=pltpu.SMEM), anywhere] + [anywhere for _ in given],
+        functools.partial(spread_kernel, outer, inner),
+        in_specs=[pl.BlockSpec(memory_space=pltpu.SMEM), anywhere],
         out_specs=anywhere,
         out_shape=jax.ShapeDtypeStruct(shape, inputs.dtype),
-        input_output_aliases={2: 0} if given else {},
         scratch_shapes=[
             pltpu.VMEM((outer, tokens, width), inputs.dtype),
             pltpu.VMEM(shape, inputs.dtype),
@@ -212,11 +213,51 @@
         ],
         compiler_params=pltpu.CompilerParams(vmem_limit_bytes=VMEM),
         name="spread",
-    )(turn, inputs, *given)
-
-
-def exchange(parts, axis):
-    return lax.all_to_all(parts, axis, 0, 0, tiled=True)
+    )(half, inputs)
+
+
+def join_kernel(half_ref, own_ref, other_ref, out_ref):
+    first = half_ref[0] == 0
+    mask = jnp.where(first, DP_ORDER[0], DP_ORDER[1])
+    tokens = own_ref.shape[3]
+    for i in range(out_ref.shape[1]):
+        index = jnp.bitwise_xor(i, mask)
+        own = own_ref[0, index]
+        other = other_ref[0, index]
+        out_ref[0, i, :, :tokens] = jnp.where(first, own, other)
+        out_ref[0, i, :, tokens:] = jnp.where(first, other, own)
+
+
+def join(own, other, half):
+    inner, outer, rows, tokens = own.shape
+    swap = CTX_ORDER[0] ^ CTX_ORDER[1]
+    return pl.pallas_call(
+        join_kernel,
+        grid=(inner,),
+        in_specs=[
+            pl.BlockSpec(memory_space=pltpu.SMEM),
+            pl.BlockSpec((1, outer, rows, tokens), lambda i: (i, 0, 0, 0)),
+            pl.BlockSpec((1, outer, rows, tokens), lambda i: (jnp.bitwise_xor(i, swap), 0, 0, 0)),
+        ],
+        out_specs=pl.BlockSpec((1, outer, rows, 2 * tokens), lambda i: (i, 0, 0, 0)),
+        out_shape=jax.ShapeDtypeStruct((inner, outer, rows, 2 * tokens), own.dtype),
+        compiler_params=pltpu.CompilerParams(vmem_limit_bytes=16 * 2**20),
+        name="join",
+    )(half, own, other)
+
+
+def exchange_ctx(parts):
+    heads, ctx = lax.axis_size("heads"), lax.axis_size("ctx")
+    groups = [[h * ctx + (i ^ CTX_ORDER[h % 2]) for i in range(ctx)] for h in range(heads)]
+    return lax.all_to_all(
+        parts, ("heads", "ctx"), 0, 0, axis_index_groups=groups, tiled=True
+    )
+
+
+def exchange_dp(parts):
+    heads, dp = lax.axis_size("heads"), lax.axis_size("dp")
+    groups = [[(i ^ DP_ORDER[h % 2]) * heads + h for i in range(dp)] for h in range(heads)]
+    return lax.all_to_all(parts, ("dp", "heads"), 0, 0, axis_index_groups=groups, tiled=True)
 
 
 def with_neighbour(block):
@@ -225,35 +266,27 @@
 
 
 def shards(inputs, queries, keys, values, outputs, out_grad, lse, positions):
-    tokens = queries.shape[1]
     ctx = lax.axis_size("ctx")
     dp = lax.axis_size("dp")
-    half = lax.axis_index("heads") % 2
-    turn = jnp.stack([half, half])
-    kv = packed(keys[0], values[0], positions, ctx)
-    turned = spread(inputs[0], turn, 1, dp, ctx)
+    half = (lax.axis_index("heads") % 2).reshape(1)
+    kv = exchange_ctx(packed(keys[0], values[0], positions, ctx))
+    turned = spread(inputs[0], half, dp, ctx)
     kv, turned = lax.optimization_barrier((kv, turned))
-    kv = exchange(kv, "ctx")
-    turned = spread(inputs[0], turn, 0, dp, ctx, turned)
-    kv, turned = lax.optimization_barrier((kv, turned))
-    own = exchange(turned, "ctx")
+    own = exchange_ctx(turned)
     query_grad, partial = attention(
         queries[0], out_grad[0], outputs[0], jnp.transpose(lse[0]), positions, kv
     )
     partial, own = lax.optimization_barrier((partial, own))
-    own = own.reshape(ctx, -1, tokens // 2)
-    other = with_neighbour(own)
-    both = jnp.sum(exchange(partial, "ctx").astype(F32), axis=0)
+    turned = join(own, with_neighbour(own), half)
+    partial, turned = lax.optimization_barrier((exchange_ctx(partial), turned))
+    both = jnp.sum(partial.astype(F32), axis=0)
     kv_low = jnp.broadcast_to(both.astype(BF16), (ctx,) + both.shape)
-    kv_low = exchange(kv_low, "ctx")
-    first = half == 0
-    turned = jnp.concatenate(
-        [jnp.where(first, own, other), jnp.where(first, other, own)], axis=2
-    )
-    kv_low, turned = lax.optimization_barrier((kv_low, turned))
+    kv_low = exchange_ctx(kv_low)
+    turned = turned.reshape(ctx, -1, turned.shape[-1])
     terms = jnp.einsum("srt,stc->rc", turned, kv_low, preferred_element_type=F32)
-    terms = terms.astype(BF16).reshape(dp, -1, 2 * HD)
-    weight_grad = jnp.sum(exchange(terms, "dp").astype(F32), axis=0)
+    terms, both = lax.optimization_barrier((terms.astype(BF16), both))
+    terms = exchange_dp(terms.reshape(dp, -1, 2 * HD))
+    weight_grad = jnp.sum(terms.astype(F32), axis=0)
     return (query_grad[None], both[None, :, :HD], both[None, :, HD:], weight_grad)
 
 

time: 112 us -> 107 us (0.955)
  waiting for transfers between devices: 55.1 us -> 32.3 us
  blocking collectives: 0 us -> 19.1 us
  matrix products: 2.78 us -> 1.57 us
  other arithmetic: 3.22 us -> 2.08 us
    all_to_all x5 -> x4, waiting for transfers between devices: 55.1 us -> 32.3 us  [the longest x3 24 us: exchange_ctx(): lax.all_to_all(parts, ('heads', 'ctx'), 0, 0, axis_index_groups=groups, t...]
    all_to_all x0 -> x1, blocking collectives: none -> 19.1 us  [exchange_ctx(): lax.all_to_all(parts, ('heads', 'ctx'), 0, 0, axis_index_groups=groups, t...]
    unnamed x2 -> x6, local copies, waits for them, and re-layouts: 0.01 us -> 1.52 us
    select_n x1 -> x0, other arithmetic: 1.49 us -> none  [shards(): jnp.where(first, own, other)]
    reduce_sum x2, other arithmetic: 0.82 us -> 2.07 us  [the longest x1 1.39 us: shards(): both = jnp.sum(partial.astype(F32), axis=0)]
    dot_general x1, matrix products: 2.78 us -> 1.57 us  [shards(): jnp.einsum('srt,stc->rc', turned, kv_low, preferred_element_type=F32)]
    all_to_all x5 -> x4, starting transfers between devices: 27.8 us -> 28.3 us  [the longest x3 18.3 us: exchange_ctx(): lax.all_to_all(parts, ('heads', 'ctx'), 0, 0, axis_index_groups=groups, t...]
  transfers between devices with their start and end apart: 6 -> 5, of which waited for: 5 -> 4; matrix products, arithmetic and copies ran while one was open for 3% -> 1% of each run, Pallas kernels for 16% -> 17%
where the time goes in v4:
time: 107 us; the launch traced here: 106 us
  waiting for transfers between devices  32.3 us (30%)
  starting transfers between devices  28.3 us (26%)
  Pallas kernels  19.6 us (18%)
  blocking collectives  19.1 us (18%)
  local copies, waits for them, and re-layouts  2.3 us (2%)
  other arithmetic  2.08 us (2%)
  matrix products  1.57 us (1%)
    all_to_all x3, waiting for transfers between devices, exchange_ctx(): lax.all_to_all(parts, ('heads', 'ctx'), 0, 0, axis_index_groups=groups, t...  24 us
    all_to_all x1, blocking collectives, exchange_ctx(): lax.all_to_all(parts, ('heads', 'ctx'), 0, 0, axis_index_groups=groups, t...  19.1 us
    all_to_all x3, starting transfers between devices, exchange_ctx(): lax.all_to_all(parts, ('heads', 'ctx'), 0, 0, axis_index_groups=groups, t...  18.3 us
    pallas_call x1, Pallas kernels, attention(): pl.pallas_call(attention_kernel, grid=(heads // PAIR,), in_specs=[by_head...  14.4 us
    all_to_all x1, starting transfers between devices, exchange_dp(): lax.all_to_all(parts, ('dp', 'heads'), 0, 0, axis_index_groups=groups, ti...  9.93 us
    all_to_all x1, waiting for transfers between devices, exchange_dp(): lax.all_to_all(parts, ('dp', 'heads'), 0, 0, axis_index_groups=groups, ti...  8.25 us
    pallas_call x1, Pallas kernels, spread(): pl.pallas_call(functools.partial(spread_kernel, outer, inner), in_specs=[...  2.58 us
  transfers between devices with their start and end apart: 5, of which 4 were waited for; matrix products, arithmetic and copies ran while one was open for 1% of the time, Pallas kernels for 17%

profile of v4, /device:TPU:6, one launch (start us, length us, event | category | flops | bytes accessed | tf_op | source)
XLA Modules:
  0.0 105.9 jit_solution(14061537818940296598)
XLA Ops:
  0.6 2.0 %pack.1 = bf16[8,272,256]{2,1,0:T(8,128)(2,1)} custom-call(bf16[256,128]{1,0:T(8,128)(2,1)} %bitcast.25, bf16[256,128]{1,0:T(8,128)(2,1)} %bitcast.26, s32[1,256]{1,0:T(1,128)} %pos_ref.3), custom_call_target="tpu_custom_call" | custom-call | tf_op jit(solution)/shard_map/pack/pallas_call | solution.py:53
  2.6 5.9 %all-to-all-start = ((bf16[8,272,256]{2,1,0:T(8,128)(2,1)}), bf16[8,272,256]{2,1,0:T(8,128)(2,1)S(1)}, u32[]{:S(2)}, u32[]{:S(2)}) async-start(bf16[8,272,256]{2,1,0:T(8,128)(2,1)} %pack.1), calls=%async_computation | async-start | bytes 2228224 | tf_op jit(solution)/shard_map/all_to_all | solution.py:252
  8.6 2.6 %spread.1 = bf16[8,8,80,128]{3,2,1,0:T(8,128)(2,1)} custom-call(s32[1]{0:T(128)} %bitcast.7.half_ref, bf16[256,5120]{1,0:T(8,128)(2,1)} %bitcast.24), custom_call_target="tpu_custom_call" | custom-call | tf_op jit(solution)/shard_map/spread/pallas_call | solution.py:203
  11.2 11.7 %all-to-all-done.kv_ref = bf16[8,272,256]{2,1,0:T(8,128)(2,1)S(1)} async-done(((bf16[8,272,256]{2,1,0:T(8,128)(2,1)}), bf16[8,272,256]{2,1,0:T(8,128)(2,1)S(1)}, u32[]{:S(2)}, u32[]{:S(2)}) %all-to-all-start) | async-done | bytes 1114144 | tf_op jit(solution)/shard_map/all_to_all | solution.py:252
  22.9 0.0 copy-start.2
  22.9 5.9 %all-to-all-start.1 = ((bf16[8,8,80,128]{3,2,1,0:T(8,128)(2,1)}), bf16[8,8,80,128]{3,2,1,0:T(8,128)(2,1)S(1)}, u32[]{:S(2)}, u32[]{:S(2)}) async-start(bf16[8,8,80,128]{3,2,1,0:T(8,128)(2,1)} %spread.1), calls=%async_computation.1 | async-start | bytes 2621440 | tf_op jit(solution)/shard_map/all_to_all | solution.py:252
  28.8 0.0 copy-done.2
  28.8 14.4 %attention.1 = (f32[256,1024]{1,0:T(8,128)}, bf16[8,256,256]{2,1,0:T(8,128)(2,1)}) custom-call(bf16[256,1024]{1,0:T(8,128)(2,1)} %bitcast.27, bf16[256,1024]{1,0:T(8,128)(2,1)} %bitcast.28, bf16[256,1024]{1,0:T(8,128)(2,1)} %bitcast.29, f32[8,256]{1,0:T(8,128)} %bitcast.30, s32[1,256]{1,0:T(1,128)} %pos_ref.3, bf16[8,272,256]{2,1,0:T(8,128)(2,1)} %copy-done.2), custom_call_target="tpu_custom_call" | custom-call | flops 5368709120 | bytes 12582912 | tf_op jit(solution)/shard_map/attention/pallas_call | solution.py:136
  43.2 1.6 %all-to-all-done.1.own_ref = bf16[8,8,80,128]{3,2,1,0:T(8,128)(2,1)S(1)} async-done(((bf16[8,8,80,128]{3,2,1,0:T(8,128)(2,1)}), bf16[8,8,80,128]{3,2,1,0:T(8,128)(2,1)S(1)}, u32[]{:S(2)}, u32[]{:S(2)}) %all-to-all-start.1) | async-done | bytes 1310752 | tf_op jit(solution)/shard_map/all_to_all | solution.py:252
  44.8 0.0 collective-permute-start
  44.8 6.5 %all-to-all-start.2 = ((bf16[8,256,256]{2,1,0:T(8,128)(2,1)}), bf16[8,256,256]{2,1,0:T(8,128)(2,1)}, u32[]{:S(2)}, u32[]{:S(2)}) async-start(bf16[8,256,256]{2,1,0:T(8,128)(2,1)} %get-tuple-element.18), calls=%async_computation.2 | async-start | bytes 2097152 | tf_op jit(solution)/shard_map/all_to_all | solution.py:252
  51.3 0.0 collective-permute-done.other_ref
  51.3 0.6 join.1
  51.9 0.0 copy-start
  51.9 1.5 %copy-done = bf16[8,8,80,256]{3,2,1,0:T(8,128)(2,1)} copy-done((bf16[8,8,80,256]{3,2,1,0:T(8,128)(2,1)}, bf16[8,8,80,256]{3,2,1,0:T(8,128)(2,1)S(1)}, u32[]{:S(2)}) %copy-start) | copy-done | bytes 2621464
  53.4 10.7 %all-to-all-done.2 = bf16[8,256,256]{2,1,0:T(8,128)(2,1)} async-done(((bf16[8,256,256]{2,1,0:T(8,128)(2,1)}), bf16[8,256,256]{2,1,0:T(8,128)(2,1)}, u32[]{:S(2)}, u32[]{:S(2)}) %all-to-all-start.2) | async-done | bytes 1048608 | tf_op jit(solution)/shard_map/all_to_all | solution.py:252
  64.2 1.4 %convert_reduce_fusion = f32[256,256]{1,0:T(8,128)S(1)} fusion(bf16[8,256,256]{2,1,0:T(8,128)(2,1)} %all-to-all-done.2), kind=kLoop, calls=%fused_computation | loop fusion | flops 983040 | bytes 1310720 | tf_op jit(solution)/shard_map/reduce_sum | solution.py:282
  65.5 0.0 copy-start.1
  65.6 0.1 broadcast_in_dim.13
  65.7 19.1 %all_to_all.25 = bf16[8,256,256]{2,1,0:T(8,128)(2,1)S(1)} all-to-all(bf16[8,256,256]{2,1,0:T(8,128)(2,1)S(1)} %broadcast_in_dim.13), channel_id=1, replica_groups={{0,1,2,3,4,5,6,7},{14,15,12,13,10,11,8,9},{16,17,18,19,20,21,22,23},{30..., dimensions={0} | all-to-all | bytes 2097152 | tf_op jit(solution)/shard_map/all_to_all | solution.py:252
  84.7 0.0 copy-done.1
  84.7 1.6 %fusion = bf16[640,256]{1,0:T(8,128)(2,1)} fusion(bf16[8,640,256]{2,1,0:T(8,128)(2,1)S(1)} %bitcast.23, bf16[8,256,256]{2,1,0:T(8,128)(2,1)S(1)} %all_to_all.25), kind=kOutput, calls=%fused_computation.2 | convolution fusion | flops 671252480 | bytes 3997696 | tf_op jit(solution)/shard_map/srt,stc->rc/dot_general | solution.py:286
  86.3 9.9 %all-to-all-start.4 = ((bf16[8,80,256]{2,1,0:T(8,128)(2,1)}), bf16[8,80,256]{2,1,0:T(8,128)(2,1)S(1)}, u32[]{:S(2)}, u32[]{:S(2)}) async-start(bf16[8,80,256]{2,1,0:T(8,128)(2,1)} %bitcast.14), calls=%async_computation.4 | async-start | bytes 655360 | tf_op jit(solution)/shard_map/all_to_all | solution.py:260
  96.2 0.7 slice_bitcast_fusion
  97.0 8.2 %all-to-all-done.4 = bf16[8,80,256]{2,1,0:T(8,128)(2,1)S(1)} async-done(((bf16[8,80,256]{2,1,0:T(8,128)(2,1)}), bf16[8,80,256]{2,1,0:T(8,128)(2,1)S(1)}, u32[]{:S(2)}, u32[]{:S(2)}) %all-to-all-start.4) | async-done | bytes 327712 | tf_op jit(solution)/shard_map/all_to_all | solution.py:260
  105.2 0.7 convert_reduce_fusion.1
  (1 shorter events, 0.0 us)
Async XLA Ops:
  2.6 20.3 %all-to-all-start = ((bf16[8,272,256]{2,1,0:T(8,128)(2,1)}), bf16[8,272,256]{2,1,0:T(8,128)(2,1)S(1)}, u32[]{:S(2)}, u32[]{:S(2)}) async-start(bf16[8,272,256]{2,1,0:T(8,128)(2,1)} %pack.1), calls=%async_computation | async-start | bytes 2228224 | tf_op jit(solution)/shard_map/all_to_all | solution.py:252
  22.9 5.9 %copy-start.2 = (bf16[8,272,256]{2,1,0:T(8,128)(2,1)}, bf16[8,272,256]{2,1,0:T(8,128)(2,1)S(1)}, u32[]{:S(2)}) copy-start(bf16[8,272,256]{2,1,0:T(8,128)(2,1)S(1)} %all-to-all-done.kv_ref) | copy-start | bytes 3342340
  22.9 21.9 %all-to-all-start.1 = ((bf16[8,8,80,128]{3,2,1,0:T(8,128)(2,1)}), bf16[8,8,80,128]{3,2,1,0:T(8,128)(2,1)S(1)}, u32[]{:S(2)}, u32[]{:S(2)}) async-start(bf16[8,8,80,128]{3,2,1,0:T(8,128)(2,1)} %spread.1), calls=%async_computation.1 | async-start | bytes 2621440 | tf_op jit(solution)/shard_map/all_to_all | solution.py:252
  44.8 6.5 %collective-permute-start = (bf16[8,8,80,128]{3,2,1,0:T(8,128)(2,1)S(1)}, bf16[8,8,80,128]{3,2,1,0:T(8,128)(2,1)S(1)}, u32[]{:S(2)}, u32[]{:S(2)}) collective-permute-start(bf16[8,8,80,128]{3,2,1,0:T(8,128)(2,1)S(1)} %all-to-all-done.1.own_ref), channel_id=1, source_target_pairs={{0,8},{8,0},{16,24},{24,16},{1,9},{9,1},{17,25},{25,17},{2,10},{10... | collective-permute-start | bytes 3932168 | tf_op jit(solution)/shard_map/ppermute | solution.py:265
  44.8 19.4 %all-to-all-start.2 = ((bf16[8,256,256]{2,1,0:T(8,128)(2,1)}), bf16[8,256,256]{2,1,0:T(8,128)(2,1)}, u32[]{:S(2)}, u32[]{:S(2)}) async-start(bf16[8,256,256]{2,1,0:T(8,128)(2,1)} %get-tuple-element.18), calls=%async_computation.2 | async-start | bytes 2097152 | tf_op jit(solution)/shard_map/all_to_all | solution.py:252
  51.9 1.5 %copy-start = (bf16[8,8,80,256]{3,2,1,0:T(8,128)(2,1)}, bf16[8,8,80,256]{3,2,1,0:T(8,128)(2,1)S(1)}, u32[]{:S(2)}) copy-start(bf16[8,8,80,256]{3,2,1,0:T(8,128)(2,1)S(1)} %join.1) | copy-start | bytes 7864324
  65.5 19.2 %copy-start.1 = (bf16[8,8,80,256]{3,2,1,0:T(8,128)(2,1)S(1)}, bf16[8,8,80,256]{3,2,1,0:T(8,128)(2,1)}, u32[]{:S(2)}) copy-start(bf16[8,8,80,256]{3,2,1,0:T(8,128)(2,1)} %copy-done) | copy-start | bytes 7864324
  86.3 18.9 %all-to-all-start.4 = ((bf16[8,80,256]{2,1,0:T(8,128)(2,1)}), bf16[8,80,256]{2,1,0:T(8,128)(2,1)S(1)}, u32[]{:S(2)}, u32[]{:S(2)}) async-start(bf16[8,80,256]{2,1,0:T(8,128)(2,1)} %bitcast.14), calls=%async_computation.4 | async-start | bytes 655360 | tf_op jit(solution)/shard_map/all_to_all | solution.py:260

commit v5 on v4

--- a/solution.py
+++ b/solution.py
@@ -14,6 +14,8 @@
 PAIR = 2
 CHUNK = 1024
 VMEM = 60 * 2**20
+X = 2
+Y = 4
 CTX_ORDER = (0, 6)
 DP_ORDER = (2, 6)
 FACTOR = HD ** (-0.5)
@@ -165,85 +167,109 @@
     )(query, grad, out, lse, pos, kv)
 
 
-def spread_kernel(outer, inner, half_ref, in_ref, out_ref, block, turned, in_sems, out_sems):
-    half = half_ref[0]
-    mask = jnp.where(half == 0, CTX_ORDER[0], CTX_ORDER[1])
-    tokens = block.shape[1]
-    width = block.shape[2]
-    rows = width // inner
-    here = pl.ds(pl.multiple_of(half * tokens, tokens), tokens)
-    loads = [
-        pltpu.make_async_copy(
-            in_ref.at[here, pl.ds(i * width, width)], block.at[i], in_sems.at[i]
+def spread_kernel(place_ref, in_ref, *refs):
+    outs, block, turned, in_sems, out_sems = refs[:Y], *refs[Y:]
+    outer, tokens, width = block.shape
+    rows = outs[0].shape[1]
+    core, x, y = place_ref[0], place_ref[1], place_ref[2]
+    to_x = jnp.bitwise_xor(x, 1 - core)
+    shift = X * Y * rows - width
+    loads = []
+    stores = []
+    for i in range(outer):
+        start = pl.multiple_of(i * X * Y * rows + to_x * shift, 128)
+        loads.append(
+            pltpu.make_async_copy(in_ref.at[:, pl.ds(start, width)], block.at[i], in_sems.at[i])
         )
-        for i in range(outer)
-    ]
-    stores = [
-        pltpu.make_async_copy(turned.at[:, i], out_ref.at[:, i], out_sems.at[i])
-        for i in range(outer)
-    ]
+        for j in range(Y):
+            to_y = jnp.bitwise_and(y + j, Y - 1)
+            start = pl.multiple_of(to_x * (Y * rows - shift) + to_y * rows, 16)
+            stores.append(
+                pltpu.make_async_copy(
+                    turned.at[i, pl.ds(start, rows)], outs[j].at[i], out_sems.at[i, j]
+                )
+            )
     for load in loads:
         load.start()
     for i in range(outer):
         loads[i].wait()
-        columns = jnp.transpose(block[i])
-        for piece in range(inner):
-            turned[jnp.bitwise_xor(piece, mask), i] = columns[piece * rows : (piece + 1) * rows]
-        stores[i].start()
+        turned[i] = jnp.transpose(block[i])
+        for store in stores[i * Y : (i + 1) * Y]:
+            store.start()
     for store in stores:
         store.wait()
 
 
-def spread(inputs, half, outer, inner):
+def spread(inputs, place, outer):
     tokens, width = inputs.shape
-    tokens = tokens // 2
-    width = width // outer
-    shape = (inner, outer, width // inner, tokens)
+    rows = width // (outer * X * Y)
+    cols = -(-Y * rows // 128) * 128
     anywhere = pl.BlockSpec(memory_space=pl.ANY)
     return pl.pallas_call(
-        functools.partial(spread_kernel, outer, inner),
+        spread_kernel,
         in_specs=[pl.BlockSpec(memory_space=pltpu.SMEM), anywhere],
-        out_specs=anywhere,
-        out_shape=jax.ShapeDtypeStruct(shape, inputs.dtype),
+        out_specs=[anywhere] * Y,
+        out_shape=[jax.ShapeDtypeStruct((outer, rows, tokens), inputs.dtype)] * Y,
         scratch_shapes=[
-            pltpu.VMEM((outer, tokens, width), inputs.dtype),
-            pltpu.VMEM(shape, inputs.dtype),
+            pltpu.VMEM((outer, tokens, cols), inputs.dtype),
+            pltpu.VMEM((outer, cols, tokens), inputs.dtype),
             pltpu.SemaphoreType.DMA((outer,)),
-            pltpu.SemaphoreType.DMA((outer,)),
+            pltpu.SemaphoreType.DMA((outer, Y)),
         ],
         compiler_params=pltpu.CompilerParams(vmem_limit_bytes=VMEM),
         name="spread",
-    )(half, inputs)
-
-
-def join_kernel(half_ref, own_ref, other_ref, out_ref):
-    first = half_ref[0] == 0
-    mask = jnp.where(first, DP_ORDER[0], DP_ORDER[1])
-    tokens = own_ref.shape[3]
-    for i in range(out_ref.shape[1]):
-        index = jnp.bitwise_xor(i, mask)
-        own = own_ref[0, index]
-        other = other_ref[0, index]
-        out_ref[0, i, :, :tokens] = jnp.where(first, own, other)
-        out_ref[0, i, :, tokens:] = jnp.where(first, other, own)
-
-
-def join(own, other, half):
-    inner, outer, rows, tokens = own.shape
-    swap = CTX_ORDER[0] ^ CTX_ORDER[1]
+    )(place, inputs)
+
+
+def pass_along(pieces):
+    heads, ctx = lax.axis_size("heads"), lax.axis_size("ctx")
+    passed = []
+    for i, piece in enumerate(pieces):
+        route = []
+        for h in range(heads):
+            for c in range(ctx):
+                x, y = divmod(c, Y)
+                to_x = x if h % 2 else 1 - x
+                route.append((h * ctx + c, h * ctx + to_x * Y + (y + i) % Y))
+        passed.append(lax.ppermute(piece, ("heads", "ctx"), route))
+    return passed
+
+
+def join_kernel(place_ref, *refs):
+    blocks, out_ref, sems = refs[: 2 * Y], refs[2 * Y], refs[2 * Y + 1]
+    core, x, y = place_ref[0], place_ref[1], place_ref[2]
+    ctx_mask = jnp.where(core == 0, CTX_ORDER[0], CTX_ORDER[1])
+    dp_mask = jnp.where(core == 0, DP_ORDER[0], DP_ORDER[1])
+    copies = []
+    for k, block in enumerate(blocks):
+        at = core if k < Y else 1 - core
+        from_x = jnp.bitwise_xor(x, 1 - at)
+        from_y = jnp.bitwise_and(y - k % Y + Y, Y - 1)
+        place = jnp.bitwise_xor(from_x * Y + from_y, ctx_mask)
+        for i in range(block.shape[0]):
+            copies.append(
+                pltpu.make_async_copy(
+                    block.at[i], out_ref.at[place, jnp.bitwise_xor(i, dp_mask)], sems.at[k, i]
+                )
+            )
+    for copy in copies:
+        copy.start()
+    for copy in copies:
+        copy.wait()
+
+
+def join(own, other, place):
+    outer, rows, tokens = own[0].shape
+    anywhere = pl.BlockSpec(memory_space=pl.ANY)
     return pl.pallas_call(
         join_kernel,
-        grid=(inner,),
-        in_specs=[
-            pl.BlockSpec(memory_space=pltpu.SMEM),
-            pl.BlockSpec((1, outer, rows, tokens), lambda i: (i, 0, 0, 0)),
-            pl.BlockSpec((1, outer, rows, tokens), lambda i: (jnp.bitwise_xor(i, swap), 0, 0, 0)),
-        ],
-        out_specs=pl.BlockSpec((1, outer, rows, 2 * tokens), lambda i: (i, 0, 0, 0)),
-        out_shape=jax.ShapeDtypeStruct((inner, outer, rows, 2 * tokens), own.dtype),
+        in_specs=[pl.BlockSpec(memory_space=pltpu.SMEM)] + [anywhere] * (2 * Y),
+        out_specs=anywhere,
+        out_shape=jax.ShapeDtypeStruct((2 * Y, outer, rows, tokens), own[0].dtype),
+        scratch_shapes=[pltpu.SemaphoreType.DMA((2 * Y, outer))],
         compiler_params=pltpu.CompilerParams(vmem_limit_bytes=16 * 2**20),
         name="join",
-    )(half, own, other)
+    )(place, *own, *other)
 
 
 def exchange_ctx(parts):
@@ -268,16 +294,17 @@
 def shards(inputs, queries, keys, values, outputs, out_grad, lse, positions):
     ctx = lax.axis_size("ctx")
     dp = lax.axis_size("dp")
-    half = (lax.axis_index("heads") % 2).reshape(1)
+    index = lax.axis_index("ctx")
+    place = jnp.stack([lax.axis_index("heads") % 2, index // Y, index % Y])
     kv = exchange_ctx(packed(keys[0], values[0], positions, ctx))
-    turned = spread(inputs[0], half, dp, ctx)
-    kv, turned = lax.optimization_barrier((kv, turned))
-    own = exchange_ctx(turned)
+    pieces = spread(inputs[0], place, dp)
+    own = pass_along(pieces)
+    kv, _ = lax.optimization_barrier((kv, pieces))
     query_grad, partial = attention(
         queries[0], out_grad[0], outputs[0], jnp.transpose(lse[0]), positions, kv
     )
     partial, own = lax.optimization_barrier((partial, own))
-    turned = join(own, with_neighbour(own), half)
+    turned = join(own, [with_neighbour(block) for block in own], place)
     partial, turned = lax.optimization_barrier((exchange_ctx(partial), turned))
     both = jnp.sum(partial.astype(F32), axis=0)
     kv_low = jnp.broadcast_to(both.astype(BF16), (ctx,) + both.shape)

time: 107 us -> 103 us (0.963); the launches traced: 106 us -> 101 us
  waiting for transfers between devices: 32.3 us -> 16.1 us
  Pallas kernels: 19.6 us -> 25.1 us
  starting transfers between devices: 28.3 us -> 33.2 us
  local copies, waits for them, and re-layouts: 2.3 us -> 3.75 us
  blocking collectives: 19.1 us -> 17.7 us
    all_to_all x3 -> x2, waiting for transfers between devices: 24 us -> 6.35 us  [exchange_ctx(): lax.all_to_all(parts, ('heads', 'ctx'), 0, 0, axis_index_groups=groups, t...]
    ppermute x0 -> x4, starting transfers between devices: none -> 9.95 us  [pass_along(): passed.append(lax.ppermute(piece, ('heads', 'ctx'), route))]
    all_to_all x3 -> x2, starting transfers between devices: 18.3 us -> 12.3 us  [exchange_ctx(): lax.all_to_all(parts, ('heads', 'ctx'), 0, 0, axis_index_groups=groups, t...]
    pallas_call x2, Pallas kernels: 3.18 us -> 8.66 us  [the longest x1 5.16 us: join(): pl.pallas_call(join_kernel, in_specs=[pl.BlockSpec(memory_space=pltpu.SME...]
    ppermute x1 -> x4, waiting for transfers between devices: 0.01 us -> 2.01 us  [with_neighbour(): return lax.ppermute(block, 'heads', [(i, i ^ 1) for i in devices])]
    unnamed x6 -> x12, local copies, waits for them, and re-layouts: 1.52 us -> 2.96 us
    all_to_all x1, blocking collectives: 19.1 us -> 17.7 us  [exchange_ctx(): lax.all_to_all(parts, ('heads', 'ctx'), 0, 0, axis_index_groups=groups, t...]
  transfers between devices with their start and end apart: 5 -> 11, of which waited for: 4 -> 7; matrix products, arithmetic and copies ran while one was open for 1% -> 1% of each run, Pallas kernels for 17% -> 23%
where the time goes in v5:
time: 103 us; the launch traced here: 101 us
  starting transfers between devices  33.2 us (32%)
  Pallas kernels  25.1 us (24%)
  blocking collectives  17.7 us (17%)
  waiting for transfers between devices  16.1 us (16%)
  local copies, waits for them, and re-layouts  3.75 us (4%)
  other arithmetic  2.64 us (3%)
  matrix products  1.56 us (2%)
    all_to_all x1, blocking collectives, exchange_ctx(): lax.all_to_all(parts, ('heads', 'ctx'), 0, 0, axis_index_groups=groups, t...  17.7 us
    pallas_call x1, Pallas kernels, attention(): pl.pallas_call(attention_kernel, grid=(heads // PAIR,), in_specs=[by_head...  14.4 us
    all_to_all x2, starting transfers between devices, exchange_ctx(): lax.all_to_all(parts, ('heads', 'ctx'), 0, 0, axis_index_groups=groups, t...  12.3 us
    ppermute x4, starting transfers between devices, pass_along(): passed.append(lax.ppermute(piece, ('heads', 'ctx'), route))  9.95 us
    all_to_all x1, starting transfers between devices, exchange_dp(): lax.all_to_all(parts, ('dp', 'heads'), 0, 0, axis_index_groups=groups, ti...  9.94 us
    all_to_all x1, waiting for transfers between devices, exchange_dp(): lax.all_to_all(parts, ('dp', 'heads'), 0, 0, axis_index_groups=groups, ti...  7.7 us
    all_to_all x2, waiting for transfers between devices, exchange_ctx(): lax.all_to_all(parts, ('heads', 'ctx'), 0, 0, axis_index_groups=groups, t...  6.35 us
    pallas_call x1, Pallas kernels, join(): pl.pallas_call(join_kernel, in_specs=[pl.BlockSpec(memory_space=pltpu.SME...  5.16 us
  transfers between devices with their start and end apart: 11, of which 7 were waited for; matrix products, arithmetic and copies ran while one was open for 1% of the time, Pallas kernels for 23%

profile of v5, /device:TPU:6, one launch (start us, length us, event | category | flops | bytes accessed | tf_op | source)
XLA Modules:
  0.0 100.7 jit_solution(17447117253779813676)
XLA Ops:
  0.6 2.0 %pack.1 = bf16[8,272,256]{2,1,0:T(8,128)(2,1)} custom-call(bf16[256,128]{1,0:T(8,128)(2,1)} %bitcast.27, bf16[256,128]{1,0:T(8,128)(2,1)} %bitcast.28, s32[1,256]{1,0:T(1,128)} %pos_ref.3), custom_call_target="tpu_custom_call" | custom-call | tf_op jit(solution)/shard_map/pack/pallas_call | solution.py:55
  2.7 5.9 %all-to-all-start = ((bf16[8,272,256]{2,1,0:T(8,128)(2,1)}), bf16[8,272,256]{2,1,0:T(8,128)(2,1)S(1)}, u32[]{:S(2)}, u32[]{:S(2)}) async-start(bf16[8,272,256]{2,1,0:T(8,128)(2,1)} %pack.1), calls=%async_computation | async-start | bytes 2228224 | tf_op jit(solution)/shard_map/all_to_all | solution.py:278
  8.6 0.6 pad_add_fusion.place_ref
  9.2 3.5 %spread.1 = (bf16[8,80,256]{2,1,0:T(8,128)(2,1)}, bf16[8,80,256]{2,1,0:T(8,128)(2,1)}, bf16[8,80,256]{2,1,0:T(8,128)(2,1)}, bf16[8,80,256]{2,1,0:T(8,128)(2,1)}) custom-call(s32[3]{0:T(128)} %pad_add_fusion.place_ref, bf16[256,5120]{1,0:T(8,128)(2,1)} %bitcast.26), custom_call_target="tpu_custom_call" | custom-call | tf_op jit(solution)/shard_map/spread/pallas_call | solution.py:208
  12.7 1.9 %collective-permute-start = (bf16[8,80,256]{2,1,0:T(8,128)(2,1)}, bf16[8,80,256]{2,1,0:T(8,128)(2,1)S(1)}, u32[]{:S(2)}, u32[]{:S(2)}) collective-permute-start(bf16[8,80,256]{2,1,0:T(8,128)(2,1)} %get-tuple-element.20), channel_id=1, source_target_pairs={{0,4},{1,5},{2,6},{3,7},{4,0},{5,1},{6,2},{7,3},{8,8},{9,9},{10,10... | collective-permute-start | bytes 983048 | tf_op jit(solution)/shard_map/ppermute | solution.py:234
  14.6 3.0 %collective-permute-start.1 = (bf16[8,80,256]{2,1,0:T(8,128)(2,1)}, bf16[8,80,256]{2,1,0:T(8,128)(2,1)S(1)}, u32[]{:S(2)}, u32[]{:S(2)}) collective-permute-start(bf16[8,80,256]{2,1,0:T(8,128)(2,1)} %get-tuple-element.21), channel_id=1, source_target_pairs={{0,5},{1,6},{2,7},{3,4},{4,1},{5,2},{6,3},{7,0},{8,9},{9,10},{10,1... | collective-permute-start | bytes 983048 | tf_op jit(solution)/shard_map/ppermute | solution.py:234
  17.6 2.7 %collective-permute-start.2 = (bf16[8,80,256]{2,1,0:T(8,128)(2,1)}, bf16[8,80,256]{2,1,0:T(8,128)(2,1)S(1)}, u32[]{:S(2)}, u32[]{:S(2)}) collective-permute-start(bf16[8,80,256]{2,1,0:T(8,128)(2,1)} %get-tuple-element.22), channel_id=1, source_target_pairs={{0,6},{1,7},{2,4},{3,5},{4,2},{5,3},{6,0},{7,1},{8,10},{9,11},{10,... | collective-permute-start | bytes 983048 | tf_op jit(solution)/shard_map/ppermute | solution.py:234
  20.3 2.4 %collective-permute-start.3 = (bf16[8,80,256]{2,1,0:T(8,128)(2,1)}, bf16[8,80,256]{2,1,0:T(8,128)(2,1)S(1)}, u32[]{:S(2)}, u32[]{:S(2)}) collective-permute-start(bf16[8,80,256]{2,1,0:T(8,128)(2,1)} %get-tuple-element.23), channel_id=1, source_target_pairs={{0,7},{1,4},{2,5},{3,6},{4,3},{5,0},{6,1},{7,2},{8,11},{9,8},{10,9... | collective-permute-start | bytes 983048 | tf_op jit(solution)/shard_map/ppermute | solution.py:234
  22.6 2.3 %all-to-all-done.kv_ref = bf16[8,272,256]{2,1,0:T(8,128)(2,1)S(1)} async-done(((bf16[8,272,256]{2,1,0:T(8,128)(2,1)}), bf16[8,272,256]{2,1,0:T(8,128)(2,1)S(1)}, u32[]{:S(2)}, u32[]{:S(2)}) %all-to-all-start) | async-done | bytes 1114144 | tf_op jit(solution)/shard_map/all_to_all | solution.py:278
  24.9 0.0 copy-start.5
  24.9 1.0 copy-done.5
  25.9 0.0 copy-start.4
  25.9 14.4 %attention.1 = (f32[256,1024]{1,0:T(8,128)}, bf16[8,256,256]{2,1,0:T(8,128)(2,1)}) custom-call(bf16[256,1024]{1,0:T(8,128)(2,1)} %bitcast.29, bf16[256,1024]{1,0:T(8,128)(2,1)} %bitcast.30, bf16[256,1024]{1,0:T(8,128)(2,1)} %bitcast.31, f32[8,256]{1,0:T(8,128)} %bitcast.32, s32[1,256]{1,0:T(1,128)} %pos_ref.3, bf16[8,272,256]{2,1,0:T(8,128)(2,1)} %copy-done.5), custom_call_target="tpu_custom_call" | custom-call | flops 5368709120 | bytes 12582912 | tf_op jit(solution)/shard_map/attention/pallas_call | solution.py:138
  40.4 0.0 collective-permute-done.refs_0_
  40.4 0.0 collective-permute-done.1.refs_1_
  40.4 0.0 collective-permute-done.2.refs_2_
  40.4 0.0 copy-start
  40.4 0.0 collective-permute-done.3.refs_3_
  40.4 0.0 copy-start.2
  40.4 6.3 %all-to-all-start.1 = ((bf16[8,256,256]{2,1,0:T(8,128)(2,1)}), bf16[8,256,256]{2,1,0:T(8,128)(2,1)}, u32[]{:S(2)}, u32[]{:S(2)}) async-start(bf16[8,256,256]{2,1,0:T(8,128)(2,1)} %get-tuple-element.27), calls=%async_computation.1 | async-start | bytes 2097152 | tf_op jit(solution)/shard_map/all_to_all | solution.py:278
  46.7 0.0 collective-permute-start.4
  46.8 0.5 collective-permute-start.5
  47.3 0.0 collective-permute-start.6
  47.3 0.5 collective-permute-start.7
  47.8 0.6 collective-permute-done.4.refs_4_
  48.4 0.5 collective-permute-done.5.refs_5_
  48.8 0.5 collective-permute-done.6.refs_6_
  49.3 0.0 copy-done
  49.3 0.0 copy-done.2
  49.3 0.5 collective-permute-done.7.refs_7_
  49.8 0.0 copy-done.4
  49.8 0.0 copy-start.1
  49.8 1.0 copy-done.1
  50.8 0.0 copy-start.3
  50.8 1.0 copy-done.3
  51.7 5.2 %join.1 = bf16[8,8,80,256]{3,2,1,0:T(8,128)(2,1)S(1)} custom-call(s32[3]{0:T(128)S(1)} %copy-done.4, bf16[8,80,256]{2,1,0:T(8,128)(2,1)S(1)} %collective-permute-done.refs_0_, bf16[8,80,256]{2,1,0:T(8,128)(2,1)S(1)} %collective-permute-done.1.refs_1_, bf16[8,80,256]{2,1,0:T(8,128)(2,1)S(1)} %copy-done.1, bf16[8,80,256]{2,1,0:T(8,128)(2,1)S(1)} %copy-done.3, ...), custom_call_target="tpu_custom_call" | custom-call | tf_op jit(solution)/shard_map/join/pallas_call | solution.py:264
  56.9 4.1 %all-to-all-done.1 = bf16[8,256,256]{2,1,0:T(8,128)(2,1)} async-done(((bf16[8,256,256]{2,1,0:T(8,128)(2,1)}), bf16[8,256,256]{2,1,0:T(8,128)(2,1)}, u32[]{:S(2)}, u32[]{:S(2)}) %all-to-all-start.1) | async-done | bytes 1048608 | tf_op jit(solution)/shard_map/all_to_all | solution.py:278
  61.0 1.4 %convert_reduce_fusion = f32[256,256]{1,0:T(8,128)S(1)} fusion(bf16[8,256,256]{2,1,0:T(8,128)(2,1)} %all-to-all-done.1), kind=kLoop, calls=%fused_computation | loop fusion | flops 983040 | bytes 1310720 | tf_op jit(solution)/shard_map/reduce_sum | solution.py:309
  62.4 0.1 broadcast_in_dim.13
  62.4 17.7 %all_to_all.20 = bf16[8,256,256]{2,1,0:T(8,128)(2,1)S(1)} all-to-all(bf16[8,256,256]{2,1,0:T(8,128)(2,1)S(1)} %broadcast_in_dim.13), channel_id=1, replica_groups={{0,1,2,3,4,5,6,7},{14,15,12,13,10,11,8,9},{16,17,18,19,20,21,22,23},{30..., dimensions={0} | all-to-all | bytes 2097152 | tf_op jit(solution)/shard_map/all_to_all | solution.py:278
  80.1 1.6 %fusion = bf16[640,256]{1,0:T(8,128)(2,1)} fusion(bf16[8,640,256]{2,1,0:T(8,128)(2,1)S(1)} %bitcast.25, bf16[8,256,256]{2,1,0:T(8,128)(2,1)S(1)} %all_to_all.20), kind=kOutput, calls=%fused_computation.2 | convolution fusion | flops 671252480 | bytes 3997696 | tf_op jit(solution)/shard_map/srt,stc->rc/dot_general | solution.py:313
  81.7 9.9 %all-to-all-start.3 = ((bf16[8,80,256]{2,1,0:T(8,128)(2,1)}), bf16[8,80,256]{2,1,0:T(8,128)(2,1)S(1)}, u32[]{:S(2)}, u32[]{:S(2)}) async-start(bf16[8,80,256]{2,1,0:T(8,128)(2,1)} %bitcast.16), calls=%async_computation.3 | async-start | bytes 655360 | tf_op jit(solution)/shard_map/all_to_all | solution.py:286
  91.6 0.7 slice_bitcast_fusion
  92.4 7.7 %all-to-all-done.3 = bf16[8,80,256]{2,1,0:T(8,128)(2,1)S(1)} async-done(((bf16[8,80,256]{2,1,0:T(8,128)(2,1)}), bf16[8,80,256]{2,1,0:T(8,128)(2,1)S(1)}, u32[]{:S(2)}, u32[]{:S(2)}) %all-to-all-start.3) | async-done | bytes 327712 | tf_op jit(solution)/shard_map/all_to_all | solution.py:286
  100.1 0.7 convert_reduce_fusion.1
  (1 shorter events, 0.0 us)
Async XLA Ops:
  2.7 22.3 %all-to-all-start = ((bf16[8,272,256]{2,1,0:T(8,128)(2,1)}), bf16[8,272,256]{2,1,0:T(8,128)(2,1)S(1)}, u32[]{:S(2)}, u32[]{:S(2)}) async-start(bf16[8,272,256]{2,1,0:T(8,128)(2,1)} %pack.1), calls=%async_computation | async-start | bytes 2228224 | tf_op jit(solution)/shard_map/all_to_all | solution.py:278
  12.7 27.7 %collective-permute-start = (bf16[8,80,256]{2,1,0:T(8,128)(2,1)}, bf16[8,80,256]{2,1,0:T(8,128)(2,1)S(1)}, u32[]{:S(2)}, u32[]{:S(2)}) collective-permute-start(bf16[8,80,256]{2,1,0:T(8,128)(2,1)} %get-tuple-element.20), channel_id=1, source_target_pairs={{0,4},{1,5},{2,6},{3,7},{4,0},{5,1},{6,2},{7,3},{8,8},{9,9},{10,10... | collective-permute-start | bytes 983048 | tf_op jit(solution)/shard_map/ppermute | solution.py:234
  14.6 25.8 %collective-permute-start.1 = (bf16[8,80,256]{2,1,0:T(8,128)(2,1)}, bf16[8,80,256]{2,1,0:T(8,128)(2,1)S(1)}, u32[]{:S(2)}, u32[]{:S(2)}) collective-permute-start(bf16[8,80,256]{2,1,0:T(8,128)(2,1)} %get-tuple-element.21), channel_id=1, source_target_pairs={{0,5},{1,6},{2,7},{3,4},{4,1},{5,2},{6,3},{7,0},{8,9},{9,10},{10,1... | collective-permute-start | bytes 983048 | tf_op jit(solution)/shard_map/ppermute | solution.py:234
  17.6 22.8 %collective-permute-start.2 = (bf16[8,80,256]{2,1,0:T(8,128)(2,1)}, bf16[8,80,256]{2,1,0:T(8,128)(2,1)S(1)}, u32[]{:S(2)}, u32[]{:S(2)}) collective-permute-start(bf16[8,80,256]{2,1,0:T(8,128)(2,1)} %get-tuple-element.22), channel_id=1, source_target_pairs={{0,6},{1,7},{2,4},{3,5},{4,2},{5,3},{6,0},{7,1},{8,10},{9,11},{10,... | collective-permute-start | bytes 983048 | tf_op jit(solution)/shard_map/ppermute | solution.py:234
  20.3 20.1 %collective-permute-start.3 = (bf16[8,80,256]{2,1,0:T(8,128)(2,1)}, bf16[8,80,256]{2,1,0:T(8,128)(2,1)S(1)}, u32[]{:S(2)}, u32[]{:S(2)}) collective-permute-start(bf16[8,80,256]{2,1,0:T(8,128)(2,1)} %get-tuple-element.23), channel_id=1, source_target_pairs={{0,7},{1,4},{2,5},{3,6},{4,3},{5,0},{6,1},{7,2},{8,11},{9,8},{10,9... | collective-permute-start | bytes 983048 | tf_op jit(solution)/shard_map/ppermute | solution.py:234
  24.9 1.0 copy-start.5
  25.9 23.9 %copy-start.4 = (s32[3]{0:T(128)S(1)}, s32[3]{0:T(128)}, u32[]{:S(2)}) copy-start(s32[3]{0:T(128)} %pad_add_fusion.place_ref) | copy-start | bytes 40
  40.4 8.9 %copy-start = (bf16[8,80,256]{2,1,0:T(8,128)(2,1)}, bf16[8,80,256]{2,1,0:T(8,128)(2,1)S(1)}, u32[]{:S(2)}) copy-start(bf16[8,80,256]{2,1,0:T(8,128)(2,1)S(1)} %collective-permute-done.2.refs_2_) | copy-start | bytes 983044
  40.4 8.9 %copy-start.2 = (bf16[8,80,256]{2,1,0:T(8,128)(2,1)}, bf16[8,80,256]{2,1,0:T(8,128)(2,1)S(1)}, u32[]{:S(2)}) copy-start(bf16[8,80,256]{2,1,0:T(8,128)(2,1)S(1)} %collective-permute-done.3.refs_3_) | copy-start | bytes 983044
  40.4 20.5 %all-to-all-start.1 = ((bf16[8,256,256]{2,1,0:T(8,128)(2,1)}), bf16[8,256,256]{2,1,0:T(8,128)(2,1)}, u32[]{:S(2)}, u32[]{:S(2)}) async-start(bf16[8,256,256]{2,1,0:T(8,128)(2,1)} %get-tuple-element.27), calls=%async_computation.1 | async-start | bytes 2097152 | tf_op jit(solution)/shard_map/all_to_all | solution.py:278
  46.7 1.6 %collective-permute-start.4 = (bf16[8,80,256]{2,1,0:T(8,128)(2,1)S(1)}, bf16[8,80,256]{2,1,0:T(8,128)(2,1)S(1)}, u32[]{:S(2)}, u32[]{:S(2)}) collective-permute-start(bf16[8,80,256]{2,1,0:T(8,128)(2,1)S(1)} %collective-permute-done.refs_0_), channel_id=1, source_target_pairs={{0,8},{8,0},{16,24},{24,16},{1,9},{9,1},{17,25},{25,17},{2,10},{10... | collective-permute-start | bytes 983048 | tf_op jit(solution)/shard_map/ppermute | solution.py:291
  46.8 2.1 %collective-permute-start.5 = (bf16[8,80,256]{2,1,0:T(8,128)(2,1)S(1)}, bf16[8,80,256]{2,1,0:T(8,128)(2,1)S(1)}, u32[]{:S(2)}, u32[]{:S(2)}) collective-permute-start(bf16[8,80,256]{2,1,0:T(8,128)(2,1)S(1)} %collective-permute-done.1.refs_1_), channel_id=1, source_target_pairs={{0,8},{8,0},{16,24},{24,16},{1,9},{9,1},{17,25},{25,17},{2,10},{10... | collective-permute-start | bytes 983048 | tf_op jit(solution)/shard_map/ppermute | solution.py:291
  47.3 2.1 %collective-permute-start.6 = (bf16[8,80,256]{2,1,0:T(8,128)(2,1)S(1)}, bf16[8,80,256]{2,1,0:T(8,128)(2,1)S(1)}, u32[]{:S(2)}, u32[]{:S(2)}) collective-permute-start(bf16[8,80,256]{2,1,0:T(8,128)(2,1)S(1)} %collective-permute-done.2.refs_2_), channel_id=1, source_target_pairs={{0,8},{8,0},{16,24},{24,16},{1,9},{9,1},{17,25},{25,17},{2,10},{10... | collective-permute-start | bytes 983048 | tf_op jit(solution)/shard_map/ppermute | solution.py:291
  47.3 2.5 %collective-permute-start.7 = (bf16[8,80,256]{2,1,0:T(8,128)(2,1)S(1)}, bf16[8,80,256]{2,1,0:T(8,128)(2,1)S(1)}, u32[]{:S(2)}, u32[]{:S(2)}) collective-permute-start(bf16[8,80,256]{2,1,0:T(8,128)(2,1)S(1)} %collective-permute-done.3.refs_3_), channel_id=1, source_target_pairs={{0,8},{8,0},{16,24},{24,16},{1,9},{9,1},{17,25},{25,17},{2,10},{10... | collective-permute-start | bytes 983048 | tf_op jit(solution)/shard_map/ppermute | solution.py:291
  49.8 1.0 copy-start.1
  50.8 1.0 copy-start.3
  81.7 18.4 %all-to-all-start.3 = ((bf16[8,80,256]{2,1,0:T(8,128)(2,1)}), bf16[8,80,256]{2,1,0:T(8,128)(2,1)S(1)}, u32[]{:S(2)}, u32[]{:S(2)}) async-start(bf16[8,80,256]{2,1,0:T(8,128)(2,1)} %bitcast.16), calls=%async_computation.3 | async-start | bytes 655360 | tf_op jit(solution)/shard_map/all_to_all | solution.py:286

commit v6 on v5

--- a/solution.py
+++ b/solution.py
@@ -16,7 +16,8 @@
 VMEM = 60 * 2**20
 X = 2
 Y = 4
-CTX_ORDER = (0, 6)
+PART_ORDER = (0, 3)
+WHOLE_ORDER = (0, 6)
 DP_ORDER = (2, 6)
 FACTOR = HD ** (-0.5)
 LOG2E = math.log2(math.e)
@@ -62,21 +63,43 @@
     )(keys, values, pos)
 
 
+def delta_kernel(grad_ref, out_ref, query_ref, delta_ref):
+    del query_ref
+    for head in range(delta_ref.shape[0]):
+        cols = slice(head * HD, (head + 1) * HD)
+        product = grad_ref[:, cols].astype(F32) * out_ref[:, cols].astype(F32)
+        delta_ref[head : head + 1, :] = jnp.sum(jnp.transpose(product), axis=0, keepdims=True)
+
+
+def deltas(grad, out, query):
+    tokens, width = grad.shape
+    return pl.pallas_call(
+        delta_kernel,
+        out_shape=jax.ShapeDtypeStruct((width // HD, tokens), F32),
+        compiler_params=pltpu.CompilerParams(vmem_limit_bytes=16 * 2**20),
+        name="delta",
+    )(grad, out, query)
+
+
 def attention_kernel(
-    query_ref, grad_ref, out_ref, lse_ref, pos_ref, kv_ref, dq_ref, dkv_ref, key, key_t, value, acc
+    query_ref, grad_ref, delta_ref, lse_ref, pos_ref, kv_ref, dq_ref, dkv_ref, key_t, acc
 ):
     step = pl.program_id(0)
     blocks, rows, _ = kv_ref.shape
     keys = rows - PAD
     tokens = query_ref.shape[0]
 
+    def gathered(chunk, cols):
+        count = CHUNK // keys
+        return jnp.concatenate(
+            [kv_ref[chunk * count + i, :keys, cols] for i in range(count)], axis=0
+        )
+
     @pl.when(step == 0)
     def _():
         acc[...] = jnp.zeros_like(acc)
         for block in range(blocks):
             here = slice(block * keys, (block + 1) * keys)
-            key[here, :] = kv_ref[block, :keys, :HD]
-            value[here, :] = kv_ref[block, :keys, HD:]
             key_t[:, here] = jnp.transpose(kv_ref[block, :keys, :HD])
 
     query_pos = pos_ref[...].astype(F32)
@@ -89,21 +112,20 @@
             start = kv_ref[block, row : row + 1, :1].astype(F32) * RUN
             visible.append(offsets <= query_pos - start)
         visible = jnp.concatenate(visible, axis=0)
+        key = gathered(chunk, slice(0, HD))
+        value = gathered(chunk, slice(HD, 2 * HD))
         key_part = None
         value_part = None
         for i in range(PAIR):
             cols = slice(i * HD, (i + 1) * HD)
-            query = query_ref[:, cols]
-            grad = grad_ref[:, cols]
-            delta = jnp.sum(
-                jnp.transpose(grad.astype(F32) * out_ref[:, cols].astype(F32)),
-                axis=0,
-                keepdims=True,
-            )
+            wide = pl.ds(pl.multiple_of((step * PAIR + i) * HD, HD), HD)
+            query = query_ref[:, wide]
+            grad = grad_ref[:, wide]
+            delta = delta_ref[pl.ds(step * PAIR + i, 1), :]
             lse = lse_ref[pl.ds(step * PAIR + i, 1), :] * LOG2E
-            scores = dot(key[here, :], query, ROWS_ROWS)
+            scores = dot(key, query, ROWS_ROWS)
             probs = jnp.where(visible, jnp.exp2(scores * (FACTOR * LOG2E) - lse), 0.0)
-            dprobs = dot(value[here, :], grad, ROWS_ROWS)
+            dprobs = dot(value, grad, ROWS_ROWS)
             dscores = (probs * (dprobs - delta)).astype(BF16)
             dv = dot(probs.astype(BF16), grad, COLS_ROWS)
             dk = dot(dscores, query, COLS_ROWS)
@@ -125,7 +147,7 @@
             dkv_ref[block, :, HD:] = acc[here, HD:].astype(BF16)
 
 
-def attention(query, grad, out, lse, pos, kv):
+def attention(query, grad, delta, lse, pos, kv):
     tokens, width = query.shape
     heads = width // HD
     blocks, rows, cols = kv.shape
@@ -139,12 +161,12 @@
         attention_kernel,
         grid=(heads // PAIR,),
         in_specs=[
-            by_head,
-            by_head,
-            by_head,
+            pl.BlockSpec(memory_space=pltpu.VMEM),
+            pl.BlockSpec(memory_space=pltpu.VMEM),
+            whole(heads, tokens),
             whole(heads, tokens),
             whole(1, tokens),
-            whole(blocks, rows, cols),
+            pl.BlockSpec(memory_space=pltpu.VMEM),
         ],
         out_specs=[by_head, whole(blocks, keys, cols)],
         out_shape=[
@@ -152,19 +174,17 @@
             jax.ShapeDtypeStruct((blocks, keys, cols), BF16),
         ],
         scratch_shapes=[
-            pltpu.VMEM((blocks * keys, HD), BF16),
             pltpu.VMEM((HD, blocks * keys), BF16),
-            pltpu.VMEM((blocks * keys, HD), BF16),
             pltpu.VMEM((blocks * keys, cols), F32),
         ],
-        compiler_params=pltpu.CompilerParams(vmem_limit_bytes=VMEM),
+        compiler_params=pltpu.CompilerParams(vmem_limit_bytes=32 * 2**20),
         cost_estimate=pl.CostEstimate(
             flops=10 * blocks * keys * tokens * width,
             bytes_accessed=12 * 2**20,
             transcendentals=blocks * keys * tokens * heads,
         ),
         name="attention",
-    )(query, grad, out, lse, pos, kv)
+    )(query, grad, delta, lse, pos, kv)
 
 
 def spread_kernel(place_ref, in_ref, *refs):
@@ -236,45 +256,34 @@
 
 
 def join_kernel(place_ref, *refs):
-    blocks, out_ref, sems = refs[: 2 * Y], refs[2 * Y], refs[2 * Y + 1]
+    blocks, out_ref = refs[:-1], refs[-1]
     core, x, y = place_ref[0], place_ref[1], place_ref[2]
-    ctx_mask = jnp.where(core == 0, CTX_ORDER[0], CTX_ORDER[1])
+    ctx_mask = jnp.where(core == 0, WHOLE_ORDER[0], WHOLE_ORDER[1])
     dp_mask = jnp.where(core == 0, DP_ORDER[0], DP_ORDER[1])
-    copies = []
     for k, block in enumerate(blocks):
         at = core if k < Y else 1 - core
         from_x = jnp.bitwise_xor(x, 1 - at)
         from_y = jnp.bitwise_and(y - k % Y + Y, Y - 1)
         place = jnp.bitwise_xor(from_x * Y + from_y, ctx_mask)
         for i in range(block.shape[0]):
-            copies.append(
-                pltpu.make_async_copy(
-                    block.at[i], out_ref.at[place, jnp.bitwise_xor(i, dp_mask)], sems.at[k, i]
-                )
-            )
-    for copy in copies:
-        copy.start()
-    for copy in copies:
-        copy.wait()
+            out_ref[place, jnp.bitwise_xor(i, dp_mask)] = block[i]
 
 
 def join(own, other, place):
     outer, rows, tokens = own[0].shape
-    anywhere = pl.BlockSpec(memory_space=pl.ANY)
     return pl.pallas_call(
         join_kernel,
-        in_specs=[pl.BlockSpec(memory_space=pltpu.SMEM)] + [anywhere] * (2 * Y),
-        out_specs=anywhere,
+        in_specs=[pl.BlockSpec(memory_space=pltpu.SMEM)]
+        + [pl.BlockSpec(memory_space=pltpu.VMEM)] * (2 * Y),
         out_shape=jax.ShapeDtypeStruct((2 * Y, outer, rows, tokens), own[0].dtype),
-        scratch_shapes=[pltpu.SemaphoreType.DMA((2 * Y, outer))],
         compiler_params=pltpu.CompilerParams(vmem_limit_bytes=16 * 2**20),
         name="join",
     )(place, *own, *other)
 
 
-def exchange_ctx(parts):
+def exchange_ctx(parts, order):
     heads, ctx = lax.axis_size("heads"), lax.axis_size("ctx")
-    groups = [[h * ctx + (i ^ CTX_ORDER[h % 2]) for i in range(ctx)] for h in range(heads)]
+    groups = [[h * ctx + (i ^ order[h % 2]) for i in range(ctx)] for h in range(heads)]
     return lax.all_to_all(
         parts, ("heads", "ctx"), 0, 0, axis_index_groups=groups, tiled=True
     )
@@ -296,19 +305,19 @@
     dp = lax.axis_size("dp")
     index = lax.axis_index("ctx")
     place = jnp.stack([lax.axis_index("heads") % 2, index // Y, index % Y])
-    kv = exchange_ctx(packed(keys[0], values[0], positions, ctx))
+    kv = exchange_ctx(packed(keys[0], values[0], positions, ctx), PART_ORDER)
     pieces = spread(inputs[0], place, dp)
     own = pass_along(pieces)
-    kv, _ = lax.optimization_barrier((kv, pieces))
+    delta, _ = lax.optimization_barrier((deltas(out_grad[0], outputs[0], queries[0]), pieces))
     query_grad, partial = attention(
-        queries[0], out_grad[0], outputs[0], jnp.transpose(lse[0]), positions, kv
+        queries[0], out_grad[0], delta, jnp.transpose(lse[0]), positions, kv
     )
     partial, own = lax.optimization_barrier((partial, own))
     turned = join(own, [with_neighbour(block) for block in own], place)
-    partial, turned = lax.optimization_barrier((exchange_ctx(partial), turned))
-    both = jnp.sum(partial.astype(F32), axis=0)
+    both = jnp.sum(exchange_ctx(partial, PART_ORDER).astype(F32), axis=0)
+    both, turned = lax.optimization_barrier((both, turned))
     kv_low = jnp.broadcast_to(both.astype(BF16), (ctx,) + both.shape)
-    kv_low = exchange_ctx(kv_low)
+    kv_low = exchange_ctx(kv_low, WHOLE_ORDER)
     turned = turned.reshape(ctx, -1, turned.shape[-1])
     terms = jnp.einsum("srt,stc->rc", turned, kv_low, preferred_element_type=F32)
     terms, both = lax.optimization_barrier((terms.astype(BF16), both))

time: 103 us -> 97.8 us (0.950); the launches traced: 101 us -> 97.3 us
  Pallas kernels: 25.1 us -> 19.8 us
  waiting for transfers between devices: 16.1 us -> 19.9 us
  local copies, waits for them, and re-layouts: 3.75 us -> 0.82 us
    pallas_call x1, Pallas kernels: 5.16 us -> 1.3 us  [join(): pl.pallas_call(join_kernel, in_specs=[pl.BlockSpec(memory_space=pltpu.SME...]
    unnamed x12, local copies, waits for them, and re-layouts: 2.96 us -> 0.03 us
    pallas_call x1 -> x2, Pallas kernels: 14.4 us -> 13 us  [the longest x1 12.7 us: attention(): pl.pallas_call(attention_kernel, grid=(heads // PAIR,), in_specs=[pl.Bloc...]
    ppermute x4, waiting for transfers between devices: 0.01 us -> 1.31 us  [pass_along(): passed.append(lax.ppermute(piece, ('heads', 'ctx'), route))]
    all_to_all x1, waiting for transfers between devices: 7.7 us -> 8.96 us  [exchange_dp(): lax.all_to_all(parts, ('dp', 'heads'), 0, 0, axis_index_groups=groups, ti...]
    all_to_all x2, waiting for transfers between devices: 6.35 us -> 7.39 us  [exchange_ctx(): lax.all_to_all(parts, ('heads', 'ctx'), 0, 0, axis_index_groups=groups, t...]
  transfers between devices with their start and end apart: 11 -> 11, of which waited for: 7 -> 7; matrix products, arithmetic and copies ran while one was open for 1% -> 1% of each run, Pallas kernels for 23% -> 18%
where the time goes in v6:
time: 97.8 us; the launch traced here: 97.3 us
  starting transfers between devices  33.2 us (34%)
  waiting for transfers between devices  19.9 us (20%)
  Pallas kernels  19.8 us (20%)
  blocking collectives  18.6 us (19%)
  other arithmetic  2.68 us (3%)
  matrix products  1.56 us (2%)
    all_to_all x1, blocking collectives, exchange_ctx(): lax.all_to_all(parts, ('heads', 'ctx'), 0, 0, axis_index_groups=groups, t...  18.6 us
    pallas_call x1, Pallas kernels, attention(): pl.pallas_call(attention_kernel, grid=(heads // PAIR,), in_specs=[pl.Bloc...  12.7 us
    all_to_all x2, starting transfers between devices, exchange_ctx(): lax.all_to_all(parts, ('heads', 'ctx'), 0, 0, axis_index_groups=groups, t...  12.3 us
    ppermute x4, starting transfers between devices, pass_along(): passed.append(lax.ppermute(piece, ('heads', 'ctx'), route))  9.95 us
    all_to_all x1, starting transfers between devices, exchange_dp(): lax.all_to_all(parts, ('dp', 'heads'), 0, 0, axis_index_groups=groups, ti...  9.93 us
    all_to_all x1, waiting for transfers between devices, exchange_dp(): lax.all_to_all(parts, ('dp', 'heads'), 0, 0, axis_index_groups=groups, ti...  8.96 us
    all_to_all x2, waiting for transfers between devices, exchange_ctx(): lax.all_to_all(parts, ('heads', 'ctx'), 0, 0, axis_index_groups=groups, t...  7.39 us
    pallas_call x1, Pallas kernels, spread(): pl.pallas_call(spread_kernel, in_specs=[pl.BlockSpec(memory_space=pltpu.S...  3.49 us
  transfers between devices with their start and end apart: 11, of which 7 were waited for; matrix products, arithmetic and copies ran while one was open for 1% of the time, Pallas kernels for 18%

profile of v6, /device:TPU:6, one launch (start us, length us, event | category | flops | bytes accessed | tf_op | source)
XLA Modules:
  0.0 97.3 jit_solution(5583968734532631734)
XLA Ops:
  0.6 2.0 %pack.1 = bf16[8,272,256]{2,1,0:T(8,128)(2,1)} custom-call(bf16[256,128]{1,0:T(8,128)(2,1)} %bitcast.33, bf16[256,128]{1,0:T(8,128)(2,1)} %bitcast.34, s32[1,256]{1,0:T(1,128)} %pos_ref.3), custom_call_target="tpu_custom_call" | custom-call | tf_op jit(solution)/shard_map/pack/pallas_call | solution.py:56
  2.7 0.0 copy-start
  2.7 0.0 copy-start.1
  2.7 0.0 copy-start.2
  2.7 6.1 %all-to-all-start = ((bf16[8,272,256]{2,1,0:T(8,128)(2,1)}), bf16[8,272,256]{2,1,0:T(8,128)(2,1)S(1)}, u32[]{:S(2)}, u32[]{:S(2)}) async-start(bf16[8,272,256]{2,1,0:T(8,128)(2,1)} %pack.1), calls=%async_computation | async-start | bytes 2228224 | tf_op jit(solution)/shard_map/all_to_all | solution.py:287
  8.8 0.0 copy-start.4
  8.8 0.0 copy-start.5
  8.8 0.6 pad_add_fusion.place_ref
  9.4 3.5 %spread.1 = (bf16[8,80,256]{2,1,0:T(8,128)(2,1)}, bf16[8,80,256]{2,1,0:T(8,128)(2,1)}, bf16[8,80,256]{2,1,0:T(8,128)(2,1)}, bf16[8,80,256]{2,1,0:T(8,128)(2,1)}) custom-call(s32[3]{0:T(128)} %pad_add_fusion.place_ref, bf16[256,5120]{1,0:T(8,128)(2,1)} %bitcast.32), custom_call_target="tpu_custom_call" | custom-call | tf_op jit(solution)/shard_map/spread/pallas_call | solution.py:228
  12.9 2.0 %collective-permute-start = (bf16[8,80,256]{2,1,0:T(8,128)(2,1)}, bf16[8,80,256]{2,1,0:T(8,128)(2,1)S(1)}, u32[]{:S(2)}, u32[]{:S(2)}) collective-permute-start(bf16[8,80,256]{2,1,0:T(8,128)(2,1)} %get-tuple-element.20), channel_id=1, source_target_pairs={{0,4},{1,5},{2,6},{3,7},{4,0},{5,1},{6,2},{7,3},{8,8},{9,9},{10,10... | collective-permute-start | bytes 983048 | tf_op jit(solution)/shard_map/ppermute | solution.py:254
  14.8 3.0 %collective-permute-start.1 = (bf16[8,80,256]{2,1,0:T(8,128)(2,1)}, bf16[8,80,256]{2,1,0:T(8,128)(2,1)S(1)}, u32[]{:S(2)}, u32[]{:S(2)}) collective-permute-start(bf16[8,80,256]{2,1,0:T(8,128)(2,1)} %get-tuple-element.21), channel_id=1, source_target_pairs={{0,5},{1,6},{2,7},{3,4},{4,1},{5,2},{6,3},{7,0},{8,9},{9,10},{10,1... | collective-permute-start | bytes 983048 | tf_op jit(solution)/shard_map/ppermute | solution.py:254
  17.8 2.7 %collective-permute-start.2 = (bf16[8,80,256]{2,1,0:T(8,128)(2,1)}, bf16[8,80,256]{2,1,0:T(8,128)(2,1)}, u32[]{:S(2)}, u32[]{:S(2)}) collective-permute-start(bf16[8,80,256]{2,1,0:T(8,128)(2,1)} %get-tuple-element.22), channel_id=1, source_target_pairs={{0,6},{1,7},{2,4},{3,5},{4,2},{5,3},{6,0},{7,1},{8,10},{9,11},{10,... | collective-permute-start | bytes 983048 | tf_op jit(solution)/shard_map/ppermute | solution.py:254
  20.5 2.4 %collective-permute-start.3 = (bf16[8,80,256]{2,1,0:T(8,128)(2,1)}, bf16[8,80,256]{2,1,0:T(8,128)(2,1)}, u32[]{:S(2)}, u32[]{:S(2)}) collective-permute-start(bf16[8,80,256]{2,1,0:T(8,128)(2,1)} %get-tuple-element.23), channel_id=1, source_target_pairs={{0,7},{1,4},{2,5},{3,6},{4,3},{5,0},{6,1},{7,2},{8,11},{9,8},{10,9... | collective-permute-start | bytes 983048 | tf_op jit(solution)/shard_map/ppermute | solution.py:254
  22.8 0.0 copy-done
  22.8 0.0 copy-done.1
  22.8 0.0 copy-done.2
  22.8 0.4 delta.1.delta_ref
  23.2 0.0 all-to-all-done.kv_ref
  23.2 0.0 copy-done.4
  23.2 0.0 copy-done.5
  23.2 0.0 copy-start.3
  23.2 12.7 %attention.1 = (f32[256,1024]{1,0:T(8,128)}, bf16[8,256,256]{2,1,0:T(8,128)(2,1)}) custom-call(bf16[256,1024]{1,0:T(8,128)(2,1)S(1)} %bitcast.28, bf16[256,1024]{1,0:T(8,128)(2,1)S(1)} %bitcast.30, f32[8,256]{1,0:T(8,128)S(1)} %delta.1.delta_ref, f32[8,256]{1,0:T(8,128)S(1)} %bitcast.31, s32[1,256]{1,0:T(1,128)S(1)} %copy-done.4, ...), custom_call_target="tpu_custom_call" | custom-call | flops 5368709120 | bytes 12582912 | tf_op jit(solution)/shard_map/attention/pallas_call | solution.py:160
  35.9 0.0 collective-permute-done.refs_0_
  35.9 0.0 collective-permute-done.1.refs_1_
  35.9 0.0 collective-permute-done.2.refs_2_
  35.9 1.3 %collective-permute-done.3.refs_3_ = bf16[8,80,256]{2,1,0:T(8,128)(2,1)} collective-permute-done((bf16[8,80,256]{2,1,0:T(8,128)(2,1)}, bf16[8,80,256]{2,1,0:T(8,128)(2,1)}, u32[]{:S(2)}, u32[]{:S(2)}) %collective-permute-start.3) | collective-permute-done | bytes 327712 | tf_op jit(solution)/shard_map/ppermute | solution.py:254
  37.2 6.2 %all-to-all-start.1 = ((bf16[8,256,256]{2,1,0:T(8,128)(2,1)}), bf16[8,256,256]{2,1,0:T(8,128)(2,1)}, u32[]{:S(2)}, u32[]{:S(2)}) async-start(bf16[8,256,256]{2,1,0:T(8,128)(2,1)} %get-tuple-element.27), calls=%async_computation.1 | async-start | bytes 2097152 | tf_op jit(solution)/shard_map/all_to_all | solution.py:287
  43.4 0.0 collective-permute-start.4
  43.4 0.5 collective-permute-start.5
  43.9 0.0 collective-permute-start.6
  44.0 0.5 collective-permute-start.7
  44.5 0.6 collective-permute-done.4.refs_4_
  45.1 0.6 collective-permute-done.5.refs_5_
  45.6 0.6 collective-permute-done.6.refs_6_
  46.2 0.5 collective-permute-done.7.refs_7_
  46.7 0.0 copy-done.3
  46.7 1.3 %join.1 = bf16[8,8,80,256]{3,2,1,0:T(8,128)(2,1)S(1)} custom-call(s32[3]{0:T(128)S(1)} %copy-done.3, bf16[8,80,256]{2,1,0:T(8,128)(2,1)S(1)} %collective-permute-done.refs_0_, bf16[8,80,256]{2,1,0:T(8,128)(2,1)S(1)} %collective-permute-done.1.refs_1_, bf16[8,80,256]{2,1,0:T(8,128)(2,1)} %collective-permute-done.2.refs_2_, ...), custom_call_target="tpu_custom_call" | custom-call | tf_op jit(solution)/shard_map/join/pallas_call | solution.py:274
  48.0 7.4 %all-to-all-done.1 = bf16[8,256,256]{2,1,0:T(8,128)(2,1)} async-done(((bf16[8,256,256]{2,1,0:T(8,128)(2,1)}), bf16[8,256,256]{2,1,0:T(8,128)(2,1)}, u32[]{:S(2)}, u32[]{:S(2)}) %all-to-all-start.1) | async-done | bytes 1048608 | tf_op jit(solution)/shard_map/all_to_all | solution.py:287
  55.4 1.4 %convert_reduce_fusion = f32[256,256]{1,0:T(8,128)S(1)} fusion(bf16[8,256,256]{2,1,0:T(8,128)(2,1)} %all-to-all-done.1), kind=kLoop, calls=%fused_computation | loop fusion | flops 983040 | bytes 1310720 | tf_op jit(solution)/shard_map/reduce_sum | solution.py:317
  56.8 0.1 broadcast_in_dim.13
  56.9 18.6 %all_to_all.20 = bf16[8,256,256]{2,1,0:T(8,128)(2,1)S(1)} all-to-all(bf16[8,256,256]{2,1,0:T(8,128)(2,1)S(1)} %broadcast_in_dim.13), channel_id=1, replica_groups={{0,1,2,3,4,5,6,7},{14,15,12,13,10,11,8,9},{16,17,18,19,20,21,22,23},{30..., dimensions={0} | all-to-all | bytes 2097152 | tf_op jit(solution)/shard_map/all_to_all | solution.py:287
  75.4 1.6 %fusion = bf16[640,256]{1,0:T(8,128)(2,1)} fusion(bf16[8,640,256]{2,1,0:T(8,128)(2,1)S(1)} %bitcast.25, bf16[8,256,256]{2,1,0:T(8,128)(2,1)S(1)} %all_to_all.20), kind=kOutput, calls=%fused_computation.2 | convolution fusion | flops 671252480 | bytes 3997696 | tf_op jit(solution)/shard_map/srt,stc->rc/dot_general | solution.py:322
  77.0 9.9 %all-to-all-start.3 = ((bf16[8,80,256]{2,1,0:T(8,128)(2,1)}), bf16[8,80,256]{2,1,0:T(8,128)(2,1)S(1)}, u32[]{:S(2)}, u32[]{:S(2)}) async-start(bf16[8,80,256]{2,1,0:T(8,128)(2,1)} %bitcast.16), calls=%async_computation.3 | async-start | bytes 655360 | tf_op jit(solution)/shard_map/all_to_all | solution.py:295
  86.9 0.7 slice_bitcast_fusion
  87.6 9.0 %all-to-all-done.3 = bf16[8,80,256]{2,1,0:T(8,128)(2,1)S(1)} async-done(((bf16[8,80,256]{2,1,0:T(8,128)(2,1)}), bf16[8,80,256]{2,1,0:T(8,128)(2,1)S(1)}, u32[]{:S(2)}, u32[]{:S(2)}) %all-to-all-start.3) | async-done | bytes 327712 | tf_op jit(solution)/shard_map/all_to_all | solution.py:295
  96.6 0.7 convert_reduce_fusion.1
  (1 shorter events, 0.0 us)
Async XLA Ops:
  2.7 20.2 %copy-start = (bf16[1,256,1024]{2,1,0:T(8,128)(2,1)S(1)}, bf16[1,256,1024]{2,1,0:T(8,128)(2,1)}, u32[]{:S(2)}) copy-start(bf16[1,256,1024]{2,1,0:T(8,128)(2,1)} %param.12) | copy-start | bytes 1572868
  2.7 20.2 %copy-start.1 = (bf16[1,256,1024]{2,1,0:T(8,128)(2,1)S(1)}, bf16[1,256,1024]{2,1,0:T(8,128)(2,1)}, u32[]{:S(2)}) copy-start(bf16[1,256,1024]{2,1,0:T(8,128)(2,1)} %param.9) | copy-start | bytes 1572868
  2.7 20.1 %copy-start.2 = (bf16[1,256,1024]{2,1,0:T(8,128)(2,1)S(1)}, bf16[1,256,1024]{2,1,0:T(8,128)(2,1)}, u32[]{:S(2)}) copy-start(bf16[1,256,1024]{2,1,0:T(8,128)(2,1)} %param.13) | copy-start | bytes 1572868
  2.7 20.5 %all-to-all-start = ((bf16[8,272,256]{2,1,0:T(8,128)(2,1)}), bf16[8,272,256]{2,1,0:T(8,128)(2,1)S(1)}, u32[]{:S(2)}, u32[]{:S(2)}) async-start(bf16[8,272,256]{2,1,0:T(8,128)(2,1)} %pack.1), calls=%async_computation | async-start | bytes 2228224 | tf_op jit(solution)/shard_map/all_to_all | solution.py:287
  8.8 14.4 %copy-start.4 = (s32[1,256]{1,0:T(1,128)S(1)}, s32[1,256]{1,0:T(1,128)}, u32[]{:S(2)}) copy-start(s32[1,256]{1,0:T(1,128)} %pos_ref.3) | copy-start | bytes 3076
  8.8 14.4 %copy-start.5 = (f32[1,256,8]{1,2,0:T(8,128)S(1)}, f32[1,256,8]{1,2,0:T(8,128)}, u32[]{:S(2)}) copy-start(f32[1,256,8]{1,2,0:T(8,128)} %param.14) | copy-start | bytes 24580
  12.9 23.0 %collective-permute-start = (bf16[8,80,256]{2,1,0:T(8,128)(2,1)}, bf16[8,80,256]{2,1,0:T(8,128)(2,1)S(1)}, u32[]{:S(2)}, u32[]{:S(2)}) collective-permute-start(bf16[8,80,256]{2,1,0:T(8,128)(2,1)} %get-tuple-element.20), channel_id=1, source_target_pairs={{0,4},{1,5},{2,6},{3,7},{4,0},{5,1},{6,2},{7,3},{8,8},{9,9},{10,10... | collective-permute-start | bytes 983048 | tf_op jit(solution)/shard_map/ppermute | solution.py:254
  14.8 21.1 %collective-permute-start.1 = (bf16[8,80,256]{2,1,0:T(8,128)(2,1)}, bf16[8,80,256]{2,1,0:T(8,128)(2,1)S(1)}, u32[]{:S(2)}, u32[]{:S(2)}) collective-permute-start(bf16[8,80,256]{2,1,0:T(8,128)(2,1)} %get-tuple-element.21), channel_id=1, source_target_pairs={{0,5},{1,6},{2,7},{3,4},{4,1},{5,2},{6,3},{7,0},{8,9},{9,10},{10,1... | collective-permute-start | bytes 983048 | tf_op jit(solution)/shard_map/ppermute | solution.py:254
  17.8 18.1 %collective-permute-start.2 = (bf16[8,80,256]{2,1,0:T(8,128)(2,1)}, bf16[8,80,256]{2,1,0:T(8,128)(2,1)}, u32[]{:S(2)}, u32[]{:S(2)}) collective-permute-start(bf16[8,80,256]{2,1,0:T(8,128)(2,1)} %get-tuple-element.22), channel_id=1, source_target_pairs={{0,6},{1,7},{2,4},{3,5},{4,2},{5,3},{6,0},{7,1},{8,10},{9,11},{10,... | collective-permute-start | bytes 983048 | tf_op jit(solution)/shard_map/ppermute | solution.py:254
  20.5 16.8 %collective-permute-start.3 = (bf16[8,80,256]{2,1,0:T(8,128)(2,1)}, bf16[8,80,256]{2,1,0:T(8,128)(2,1)}, u32[]{:S(2)}, u32[]{:S(2)}) collective-permute-start(bf16[8,80,256]{2,1,0:T(8,128)(2,1)} %get-tuple-element.23), channel_id=1, source_target_pairs={{0,7},{1,4},{2,5},{3,6},{4,3},{5,0},{6,1},{7,2},{8,11},{9,8},{10,9... | collective-permute-start | bytes 983048 | tf_op jit(solution)/shard_map/ppermute | solution.py:254
  23.2 23.5 %copy-start.3 = (s32[3]{0:T(128)S(1)}, s32[3]{0:T(128)}, u32[]{:S(2)}) copy-start(s32[3]{0:T(128)} %pad_add_fusion.place_ref) | copy-start | bytes 40
  37.2 18.2 %all-to-all-start.1 = ((bf16[8,256,256]{2,1,0:T(8,128)(2,1)}), bf16[8,256,256]{2,1,0:T(8,128)(2,1)}, u32[]{:S(2)}, u32[]{:S(2)}) async-start(bf16[8,256,256]{2,1,0:T(8,128)(2,1)} %get-tuple-element.27), calls=%async_computation.1 | async-start | bytes 2097152 | tf_op jit(solution)/shard_map/all_to_all | solution.py:287
  43.4 1.6 %collective-permute-start.4 = (bf16[8,80,256]{2,1,0:T(8,128)(2,1)S(1)}, bf16[8,80,256]{2,1,0:T(8,128)(2,1)S(1)}, u32[]{:S(2)}, u32[]{:S(2)}) collective-permute-start(bf16[8,80,256]{2,1,0:T(8,128)(2,1)S(1)} %collective-permute-done.refs_0_), channel_id=1, source_target_pairs={{0,8},{8,0},{16,24},{24,16},{1,9},{9,1},{17,25},{25,17},{2,10},{10... | collective-permute-start | bytes 983048 | tf_op jit(solution)/shard_map/ppermute | solution.py:300
  43.4 2.2 %collective-permute-start.5 = (bf16[8,80,256]{2,1,0:T(8,128)(2,1)S(1)}, bf16[8,80,256]{2,1,0:T(8,128)(2,1)S(1)}, u32[]{:S(2)}, u32[]{:S(2)}) collective-permute-start(bf16[8,80,256]{2,1,0:T(8,128)(2,1)S(1)} %collective-permute-done.1.refs_1_), channel_id=1, source_target_pairs={{0,8},{8,0},{16,24},{24,16},{1,9},{9,1},{17,25},{25,17},{2,10},{10... | collective-permute-start | bytes 983048 | tf_op jit(solution)/shard_map/ppermute | solution.py:300
  43.9 2.3 %collective-permute-start.6 = (bf16[8,80,256]{2,1,0:T(8,128)(2,1)}, bf16[8,80,256]{2,1,0:T(8,128)(2,1)S(1)}, u32[]{:S(2)}, u32[]{:S(2)}) collective-permute-start(bf16[8,80,256]{2,1,0:T(8,128)(2,1)} %collective-permute-done.2.refs_2_), channel_id=1, source_target_pairs={{0,8},{8,0},{16,24},{24,16},{1,9},{9,1},{17,25},{25,17},{2,10},{10... | collective-permute-start | bytes 983048 | tf_op jit(solution)/shard_map/ppermute | solution.py:300
  44.0 2.7 %collective-permute-start.7 = (bf16[8,80,256]{2,1,0:T(8,128)(2,1)}, bf16[8,80,256]{2,1,0:T(8,128)(2,1)S(1)}, u32[]{:S(2)}, u32[]{:S(2)}) collective-permute-start(bf16[8,80,256]{2,1,0:T(8,128)(2,1)} %collective-permute-done.3.refs_3_), channel_id=1, source_target_pairs={{0,8},{8,0},{16,24},{24,16},{1,9},{9,1},{17,25},{25,17},{2,10},{10... | collective-permute-start | bytes 983048 | tf_op jit(solution)/shard_map/ppermute | solution.py:300
  77.0 19.6 %all-to-all-start.3 = ((bf16[8,80,256]{2,1,0:T(8,128)(2,1)}), bf16[8,80,256]{2,1,0:T(8,128)(2,1)S(1)}, u32[]{:S(2)}, u32[]{:S(2)}) async-start(bf16[8,80,256]{2,1,0:T(8,128)(2,1)} %bitcast.16), calls=%async_computation.3 | async-start | bytes 655360 | tf_op jit(solution)/shard_map/all_to_all | solution.py:295

commit v7 on v6

--- a/solution.py
+++ b/solution.py
@@ -13,6 +13,8 @@
 PAD = 16
 PAIR = 2
 CHUNK = 1024
+SLAB = 64
+GROUP = 8
 VMEM = 60 * 2**20
 X = 2
 Y = 4
@@ -281,6 +283,53 @@
     )(place, *own, *other)
 
 
+def finish_kernel(parts_ref, key_ref, value_ref, low_ref):
+    for start in range(0, parts_ref.shape[1], SLAB):
+        here = slice(start, start + SLAB)
+        total = parts_ref[0, here, :].astype(F32)
+        for i in range(1, parts_ref.shape[0]):
+            total = total + parts_ref[i, here, :].astype(F32)
+        key_ref[here, :] = total[:, :HD]
+        value_ref[here, :] = total[:, HD:]
+        low = total.astype(BF16)
+        for i in range(low_ref.shape[0]):
+            low_ref[i, here, :] = low
+
+
+def finish(parts):
+    _, tokens, cols = parts.shape
+    half = jax.ShapeDtypeStruct((tokens, cols // 2), F32)
+    return pl.pallas_call(
+        finish_kernel,
+        in_specs=[pl.BlockSpec(memory_space=pltpu.VMEM)],
+        out_shape=[half, half, jax.ShapeDtypeStruct(parts.shape, BF16)],
+        compiler_params=pltpu.CompilerParams(vmem_limit_bytes=16 * 2**20),
+        name="finish",
+    )(parts)
+
+
+def project_kernel(turned_ref, low_ref, out_ref):
+    outer, rows, cols = out_ref.shape
+    for start in range(0, outer, GROUP):
+        total = None
+        for block in range(turned_ref.shape[0]):
+            left = turned_ref[block, start : start + GROUP].reshape(GROUP * rows, -1)
+            term = dot(left, low_ref[block], COLS_ROWS)
+            total = term if total is None else total + term
+        out_ref[start : start + GROUP] = total.astype(BF16).reshape(GROUP, rows, cols)
+
+
+def project(turned, low):
+    _, outer, rows, _ = turned.shape
+    return pl.pallas_call(
+        project_kernel,
+        in_specs=[pl.BlockSpec(memory_space=pltpu.VMEM)] * 2,
+        out_shape=jax.ShapeDtypeStruct((outer, rows, low.shape[2]), BF16),
+        compiler_params=pltpu.CompilerParams(vmem_limit_bytes=24 * 2**20),
+        name="project",
+    )(turned, low)
+
+
 def exchange_ctx(parts, order):
     heads, ctx = lax.axis_size("heads"), lax.axis_size("ctx")
     groups = [[h * ctx + (i ^ order[h % 2]) for i in range(ctx)] for h in range(heads)]
@@ -314,16 +363,12 @@
     )
     partial, own = lax.optimization_barrier((partial, own))
     turned = join(own, [with_neighbour(block) for block in own], place)
-    both = jnp.sum(exchange_ctx(partial, PART_ORDER).astype(F32), axis=0)
-    both, turned = lax.optimization_barrier((both, turned))
-    kv_low = jnp.broadcast_to(both.astype(BF16), (ctx,) + both.shape)
-    kv_low = exchange_ctx(kv_low, WHOLE_ORDER)
-    turned = turned.reshape(ctx, -1, turned.shape[-1])
-    terms = jnp.einsum("srt,stc->rc", turned, kv_low, preferred_element_type=F32)
-    terms, both = lax.optimization_barrier((terms.astype(BF16), both))
-    terms = exchange_dp(terms.reshape(dp, -1, 2 * HD))
+    key_grad, value_grad, low = finish(exchange_ctx(partial, PART_ORDER))
+    low, turned = lax.optimization_barrier((low, turned))
+    low = exchange_ctx(low, WHOLE_ORDER)
+    terms = exchange_dp(project(turned, low))
     weight_grad = jnp.sum(terms.astype(F32), axis=0)
-    return (query_grad[None], both[None, :, :HD], both[None, :, HD:], weight_grad)
+    return (query_grad[None], key_grad[None], value_grad[None], weight_grad)
 
 
 def solution(mesh):

time: 97.8 us -> 96.8 us (0.990)
  blocking collectives: 18.6 us -> 37.3 us
  starting transfers between devices: 33.2 us -> 23.3 us
  waiting for transfers between devices: 19.9 us -> 10.9 us
  Pallas kernels: 19.8 us -> 22.7 us
  matrix products: 1.56 us -> 0 us
  other arithmetic: 2.68 us -> 1.32 us
    all_to_all x0 -> x1, blocking collectives: none -> 18.8 us  [exchange_dp(): lax.all_to_all(parts, ('dp', 'heads'), 0, 0, axis_index_groups=groups, ti...]
    all_to_all x1 -> x0, starting transfers between devices: 9.93 us -> none  [exchange_dp(): lax.all_to_all(parts, ('dp', 'heads'), 0, 0, axis_index_groups=groups, ti...]
    all_to_all x1 -> x0, waiting for transfers between devices: 8.96 us -> none  [exchange_dp(): lax.all_to_all(parts, ('dp', 'heads'), 0, 0, axis_index_groups=groups, ti...]
    pallas_call x0 -> x2, Pallas kernels: none -> 2.91 us  [the longest x1 2.07 us: finish(): pl.pallas_call(finish_kernel, in_specs=[pl.BlockSpec(memory_space=pltpu.V...]
    dot_general x1 -> x0, matrix products: 1.56 us -> none  [shards(): jnp.einsum('srt,stc->rc', turned, kv_low, preferred_element_type=F32)]
    reduce_sum x1 -> x0, other arithmetic: 1.39 us -> none  [shards(): both = jnp.sum(exchange_ctx(partial, PART_ORDER).astype(F32), axis=0)]
  transfers between devices with their start and end apart: 11 -> 10, of which waited for: 7 -> 6; matrix products, arithmetic and copies ran while one was open for 1% -> 1% of each run, Pallas kernels for 18% -> 18%
where the time goes in v7:
time: 96.8 us; the launch traced here: 96.3 us
  blocking collectives  37.3 us (39%)
  starting transfers between devices  23.3 us (24%)
  Pallas kernels  22.7 us (23%)
  waiting for transfers between devices  10.9 us (11%)
  other arithmetic  1.32 us (1%)
    all_to_all x1, blocking collectives, exchange_dp(): lax.all_to_all(parts, ('dp', 'heads'), 0, 0, axis_index_groups=groups, ti...  18.8 us
    all_to_all x1, blocking collectives, exchange_ctx(): lax.all_to_all(parts, ('heads', 'ctx'), 0, 0, axis_index_groups=groups, t...  18.6 us
    pallas_call x1, Pallas kernels, attention(): pl.pallas_call(attention_kernel, grid=(heads // PAIR,), in_specs=[pl.Bloc...  12.7 us
    all_to_all x2, starting transfers between devices, exchange_ctx(): lax.all_to_all(parts, ('heads', 'ctx'), 0, 0, axis_index_groups=groups, t...  12.3 us
    ppermute x4, starting transfers between devices, pass_along(): passed.append(lax.ppermute(piece, ('heads', 'ctx'), route))  9.95 us
    all_to_all x2, waiting for transfers between devices, exchange_ctx(): lax.all_to_all(parts, ('heads', 'ctx'), 0, 0, axis_index_groups=groups, t...  7.38 us
    pallas_call x1, Pallas kernels, spread(): pl.pallas_call(spread_kernel, in_specs=[pl.BlockSpec(memory_space=pltpu.S...  3.49 us
    ppermute x4, waiting for transfers between devices, with_neighbour(): return lax.ppermute(block, 'heads', [(i, i ^ 1) for i in devices])  2.22 us
  transfers between devices with their start and end apart: 10, of which 6 were waited for; matrix products, arithmetic and copies ran while one was open for 1% of the time, Pallas kernels for 18%

profile of v7, /device:TPU:6, one launch (start us, length us, event | category | flops | bytes accessed | tf_op | source)
XLA Modules:
  0.0 96.3 jit_solution(16205751764885864030)
XLA Ops:
  0.6 2.0 %pack.1 = bf16[8,272,256]{2,1,0:T(8,128)(2,1)} custom-call(bf16[256,128]{1,0:T(8,128)(2,1)} %bitcast.22, bf16[256,128]{1,0:T(8,128)(2,1)} %bitcast.23, s32[1,256]{1,0:T(1,128)} %pos_ref.3), custom_call_target="tpu_custom_call" | custom-call | tf_op jit(solution)/shard_map/pack/pallas_call | solution.py:58
  2.7 0.0 copy-start
  2.7 0.0 copy-start.1
  2.7 0.0 copy-start.2
  2.7 6.1 %all-to-all-start = ((bf16[8,272,256]{2,1,0:T(8,128)(2,1)}), bf16[8,272,256]{2,1,0:T(8,128)(2,1)S(1)}, u32[]{:S(2)}, u32[]{:S(2)}) async-start(bf16[8,272,256]{2,1,0:T(8,128)(2,1)} %pack.1), calls=%async_computation | async-start | bytes 2228224 | tf_op jit(solution)/shard_map/all_to_all | solution.py:336
  8.8 0.0 copy-start.4
  8.8 0.0 copy-start.5
  8.8 0.6 pad_add_fusion.place_ref
  9.4 3.5 %spread.1 = (bf16[8,80,256]{2,1,0:T(8,128)(2,1)}, bf16[8,80,256]{2,1,0:T(8,128)(2,1)}, bf16[8,80,256]{2,1,0:T(8,128)(2,1)}, bf16[8,80,256]{2,1,0:T(8,128)(2,1)}) custom-call(s32[3]{0:T(128)} %pad_add_fusion.place_ref, bf16[256,5120]{1,0:T(8,128)(2,1)} %bitcast.21), custom_call_target="tpu_custom_call" | custom-call | tf_op jit(solution)/shard_map/spread/pallas_call | solution.py:230
  12.9 2.0 %collective-permute-start = (bf16[8,80,256]{2,1,0:T(8,128)(2,1)}, bf16[8,80,256]{2,1,0:T(8,128)(2,1)S(1)}, u32[]{:S(2)}, u32[]{:S(2)}) collective-permute-start(bf16[8,80,256]{2,1,0:T(8,128)(2,1)} %get-tuple-element.21), channel_id=1, source_target_pairs={{0,4},{1,5},{2,6},{3,7},{4,0},{5,1},{6,2},{7,3},{8,8},{9,9},{10,10... | collective-permute-start | bytes 983048 | tf_op jit(solution)/shard_map/ppermute | solution.py:256
  14.9 3.0 %collective-permute-start.1 = (bf16[8,80,256]{2,1,0:T(8,128)(2,1)}, bf16[8,80,256]{2,1,0:T(8,128)(2,1)S(1)}, u32[]{:S(2)}, u32[]{:S(2)}) collective-permute-start(bf16[8,80,256]{2,1,0:T(8,128)(2,1)} %get-tuple-element.22), channel_id=1, source_target_pairs={{0,5},{1,6},{2,7},{3,4},{4,1},{5,2},{6,3},{7,0},{8,9},{9,10},{10,1... | collective-permute-start | bytes 983048 | tf_op jit(solution)/shard_map/ppermute | solution.py:256
  17.9 2.7 %collective-permute-start.2 = (bf16[8,80,256]{2,1,0:T(8,128)(2,1)}, bf16[8,80,256]{2,1,0:T(8,128)(2,1)}, u32[]{:S(2)}, u32[]{:S(2)}) collective-permute-start(bf16[8,80,256]{2,1,0:T(8,128)(2,1)} %get-tuple-element.23), channel_id=1, source_target_pairs={{0,6},{1,7},{2,4},{3,5},{4,2},{5,3},{6,0},{7,1},{8,10},{9,11},{10,... | collective-permute-start | bytes 983048 | tf_op jit(solution)/shard_map/ppermute | solution.py:256
  20.5 2.4 %collective-permute-start.3 = (bf16[8,80,256]{2,1,0:T(8,128)(2,1)}, bf16[8,80,256]{2,1,0:T(8,128)(2,1)}, u32[]{:S(2)}, u32[]{:S(2)}) collective-permute-start(bf16[8,80,256]{2,1,0:T(8,128)(2,1)} %get-tuple-element.24), channel_id=1, source_target_pairs={{0,7},{1,4},{2,5},{3,6},{4,3},{5,0},{6,1},{7,2},{8,11},{9,8},{10,9... | collective-permute-start | bytes 983048 | tf_op jit(solution)/shard_map/ppermute | solution.py:256
  22.9 0.0 copy-done
  22.9 0.0 copy-done.1
  22.9 0.0 copy-done.2
  22.9 0.4 delta.1.delta_ref
  23.2 0.0 all-to-all-done.kv_ref
  23.3 0.0 copy-done.4
  23.3 0.0 copy-done.5
  23.3 0.0 copy-start.3
  23.3 12.7 %attention.1 = (f32[256,1024]{1,0:T(8,128)}, bf16[8,256,256]{2,1,0:T(8,128)(2,1)}) custom-call(bf16[256,1024]{1,0:T(8,128)(2,1)S(1)} %bitcast.17, bf16[256,1024]{1,0:T(8,128)(2,1)S(1)} %bitcast.19, f32[8,256]{1,0:T(8,128)S(1)} %delta.1.delta_ref, f32[8,256]{1,0:T(8,128)S(1)} %bitcast.20, s32[1,256]{1,0:T(1,128)S(1)} %copy-done.4, ...), custom_call_target="tpu_custom_call" | custom-call | flops 5368709120 | bytes 12582912 | tf_op jit(solution)/shard_map/attention/pallas_call | solution.py:162
  35.9 0.0 collective-permute-done.refs_0_
  36.0 0.0 collective-permute-done.1.refs_1_
  36.0 0.0 collective-permute-done.2.refs_2_
  36.0 1.3 %collective-permute-done.3.refs_3_ = bf16[8,80,256]{2,1,0:T(8,128)(2,1)} collective-permute-done((bf16[8,80,256]{2,1,0:T(8,128)(2,1)}, bf16[8,80,256]{2,1,0:T(8,128)(2,1)}, u32[]{:S(2)}, u32[]{:S(2)}) %collective-permute-start.3) | collective-permute-done | bytes 327712 | tf_op jit(solution)/shard_map/ppermute | solution.py:256
  37.2 6.2 %all-to-all-start.1 = ((bf16[8,256,256]{2,1,0:T(8,128)(2,1)}), bf16[8,256,256]{2,1,0:T(8,128)(2,1)}, u32[]{:S(2)}, u32[]{:S(2)}) async-start(bf16[8,256,256]{2,1,0:T(8,128)(2,1)} %get-tuple-element.28), calls=%async_computation.1 | async-start | bytes 2097152 | tf_op jit(solution)/shard_map/all_to_all | solution.py:336
  43.5 0.0 collective-permute-start.4
  43.5 0.5 collective-permute-start.5
  44.0 0.0 collective-permute-start.6
  44.0 0.5 collective-permute-start.7
  44.5 0.6 collective-permute-done.4.refs_4_
  45.1 0.6 collective-permute-done.5.refs_5_
  45.7 0.6 collective-permute-done.6.refs_6_
  46.2 0.5 collective-permute-done.7.refs_7_
  46.7 0.0 copy-done.3
  46.7 1.3 %join.1.turned_ref = bf16[8,8,80,256]{3,2,1,0:T(8,128)(2,1)S(1)} custom-call(s32[3]{0:T(128)S(1)} %copy-done.3, bf16[8,80,256]{2,1,0:T(8,128)(2,1)S(1)} %collective-permute-done.refs_0_, bf16[8,80,256]{2,1,0:T(8,128)(2,1)S(1)} %collective-permute-done.1.refs_1_, bf16[8,80,256]{2,1,0:T(8,128)(2,1)} %collective-permute-done.2.refs_2_, ...), custom_call_target="tpu_custom_call" | custom-call | tf_op jit(solution)/shard_map/join/pallas_call | solution.py:276
  48.0 7.4 %all-to-all-done.1.parts_ref = bf16[8,256,256]{2,1,0:T(8,128)(2,1)} async-done(((bf16[8,256,256]{2,1,0:T(8,128)(2,1)}), bf16[8,256,256]{2,1,0:T(8,128)(2,1)}, u32[]{:S(2)}, u32[]{:S(2)}) %all-to-all-start.1) | async-done | bytes 1048608 | tf_op jit(solution)/shard_map/all_to_all | solution.py:336
  55.4 2.1 %finish.1 = (f32[256,128]{1,0:T(8,128)}, f32[256,128]{1,0:T(8,128)}, bf16[8,256,256]{2,1,0:T(8,128)(2,1)S(1)}) custom-call(bf16[8,256,256]{2,1,0:T(8,128)(2,1)} %all-to-all-done.1.parts_ref), custom_call_target="tpu_custom_call" | custom-call | tf_op jit(solution)/shard_map/finish/pallas_call | solution.py:302
  57.5 18.6 %all_to_all.20.low_ref = bf16[8,256,256]{2,1,0:T(8,128)(2,1)S(1)} all-to-all(bf16[8,256,256]{2,1,0:T(8,128)(2,1)S(1)} %get-tuple-element.37), channel_id=1, replica_groups={{0,1,2,3,4,5,6,7},{14,15,12,13,10,11,8,9},{16,17,18,19,20,21,22,23},{30..., dimensions={0} | all-to-all | bytes 2097152 | tf_op jit(solution)/shard_map/all_to_all | solution.py:336
  76.0 0.8 project.1
  76.9 18.8 %all_to_all.21 = bf16[8,80,256]{2,1,0:T(8,128)(2,1)S(1)} all-to-all(bf16[8,80,256]{2,1,0:T(8,128)(2,1)S(1)} %project.1), channel_id=1, replica_groups={{64,96,0,32,192,224,128,160},{200,232,136,168,72,104,8,40},{80,112,16,4..., dimensions={0} | all-to-all | bytes 655360 | tf_op jit(solution)/shard_map/all_to_all | solution.py:344
  95.6 0.7 convert_reduce_fusion
Async XLA Ops:
  2.7 20.2 %copy-start = (bf16[1,256,1024]{2,1,0:T(8,128)(2,1)S(1)}, bf16[1,256,1024]{2,1,0:T(8,128)(2,1)}, u32[]{:S(2)}) copy-start(bf16[1,256,1024]{2,1,0:T(8,128)(2,1)} %param.12) | copy-start | bytes 1572868
  2.7 20.2 %copy-start.1 = (bf16[1,256,1024]{2,1,0:T(8,128)(2,1)S(1)}, bf16[1,256,1024]{2,1,0:T(8,128)(2,1)}, u32[]{:S(2)}) copy-start(bf16[1,256,1024]{2,1,0:T(8,128)(2,1)} %param.9) | copy-start | bytes 1572868
  2.7 20.2 %copy-start.2 = (bf16[1,256,1024]{2,1,0:T(8,128)(2,1)S(1)}, bf16[1,256,1024]{2,1,0:T(8,128)(2,1)}, u32[]{:S(2)}) copy-start(bf16[1,256,1024]{2,1,0:T(8,128)(2,1)} %param.13) | copy-start | bytes 1572868
  2.7 20.5 %all-to-all-start = ((bf16[8,272,256]{2,1,0:T(8,128)(2,1)}), bf16[8,272,256]{2,1,0:T(8,128)(2,1)S(1)}, u32[]{:S(2)}, u32[]{:S(2)}) async-start(bf16[8,272,256]{2,1,0:T(8,128)(2,1)} %pack.1), calls=%async_computation | async-start | bytes 2228224 | tf_op jit(solution)/shard_map/all_to_all | solution.py:336
  8.8 14.5 %copy-start.4 = (s32[1,256]{1,0:T(1,128)S(1)}, s32[1,256]{1,0:T(1,128)}, u32[]{:S(2)}) copy-start(s32[1,256]{1,0:T(1,128)} %pos_ref.3) | copy-start | bytes 3076
  8.8 14.5 %copy-start.5 = (f32[1,256,8]{1,2,0:T(8,128)S(1)}, f32[1,256,8]{1,2,0:T(8,128)}, u32[]{:S(2)}) copy-start(f32[1,256,8]{1,2,0:T(8,128)} %param.14) | copy-start | bytes 24580
  12.9 23.0 %collective-permute-start = (bf16[8,80,256]{2,1,0:T(8,128)(2,1)}, bf16[8,80,256]{2,1,0:T(8,128)(2,1)S(1)}, u32[]{:S(2)}, u32[]{:S(2)}) collective-permute-start(bf16[8,80,256]{2,1,0:T(8,128)(2,1)} %get-tuple-element.21), channel_id=1, source_target_pairs={{0,4},{1,5},{2,6},{3,7},{4,0},{5,1},{6,2},{7,3},{8,8},{9,9},{10,10... | collective-permute-start | bytes 983048 | tf_op jit(solution)/shard_map/ppermute | solution.py:256
  14.9 21.1 %collective-permute-start.1 = (bf16[8,80,256]{2,1,0:T(8,128)(2,1)}, bf16[8,80,256]{2,1,0:T(8,128)(2,1)S(1)}, u32[]{:S(2)}, u32[]{:S(2)}) collective-permute-start(bf16[8,80,256]{2,1,0:T(8,128)(2,1)} %get-tuple-element.22), channel_id=1, source_target_pairs={{0,5},{1,6},{2,7},{3,4},{4,1},{5,2},{6,3},{7,0},{8,9},{9,10},{10,1... | collective-permute-start | bytes 983048 | tf_op jit(solution)/shard_map/ppermute | solution.py:256
  17.9 18.1 %collective-permute-start.2 = (bf16[8,80,256]{2,1,0:T(8,128)(2,1)}, bf16[8,80,256]{2,1,0:T(8,128)(2,1)}, u32[]{:S(2)}, u32[]{:S(2)}) collective-permute-start(bf16[8,80,256]{2,1,0:T(8,128)(2,1)} %get-tuple-element.23), channel_id=1, source_target_pairs={{0,6},{1,7},{2,4},{3,5},{4,2},{5,3},{6,0},{7,1},{8,10},{9,11},{10,... | collective-permute-start | bytes 983048 | tf_op jit(solution)/shard_map/ppermute | solution.py:256
  20.5 16.7 %collective-permute-start.3 = (bf16[8,80,256]{2,1,0:T(8,128)(2,1)}, bf16[8,80,256]{2,1,0:T(8,128)(2,1)}, u32[]{:S(2)}, u32[]{:S(2)}) collective-permute-start(bf16[8,80,256]{2,1,0:T(8,128)(2,1)} %get-tuple-element.24), channel_id=1, source_target_pairs={{0,7},{1,4},{2,5},{3,6},{4,3},{5,0},{6,1},{7,2},{8,11},{9,8},{10,9... | collective-permute-start | bytes 983048 | tf_op jit(solution)/shard_map/ppermute | solution.py:256
  23.3 23.4 %copy-start.3 = (s32[3]{0:T(128)S(1)}, s32[3]{0:T(128)}, u32[]{:S(2)}) copy-start(s32[3]{0:T(128)} %pad_add_fusion.place_ref) | copy-start | bytes 40
  37.2 18.2 %all-to-all-start.1 = ((bf16[8,256,256]{2,1,0:T(8,128)(2,1)}), bf16[8,256,256]{2,1,0:T(8,128)(2,1)}, u32[]{:S(2)}, u32[]{:S(2)}) async-start(bf16[8,256,256]{2,1,0:T(8,128)(2,1)} %get-tuple-element.28), calls=%async_computation.1 | async-start | bytes 2097152 | tf_op jit(solution)/shard_map/all_to_all | solution.py:336
  43.5 1.6 %collective-permute-start.4 = (bf16[8,80,256]{2,1,0:T(8,128)(2,1)S(1)}, bf16[8,80,256]{2,1,0:T(8,128)(2,1)S(1)}, u32[]{:S(2)}, u32[]{:S(2)}) collective-permute-start(bf16[8,80,256]{2,1,0:T(8,128)(2,1)S(1)} %collective-permute-done.refs_0_), channel_id=1, source_target_pairs={{0,8},{8,0},{16,24},{24,16},{1,9},{9,1},{17,25},{25,17},{2,10},{10... | collective-permute-start | bytes 983048 | tf_op jit(solution)/shard_map/ppermute | solution.py:349
  43.5 2.2 %collective-permute-start.5 = (bf16[8,80,256]{2,1,0:T(8,128)(2,1)S(1)}, bf16[8,80,256]{2,1,0:T(8,128)(2,1)S(1)}, u32[]{:S(2)}, u32[]{:S(2)}) collective-permute-start(bf16[8,80,256]{2,1,0:T(8,128)(2,1)S(1)} %collective-permute-done.1.refs_1_), channel_id=1, source_target_pairs={{0,8},{8,0},{16,24},{24,16},{1,9},{9,1},{17,25},{25,17},{2,10},{10... | collective-permute-start | bytes 983048 | tf_op jit(solution)/shard_map/ppermute | solution.py:349
  44.0 2.3 %collective-permute-start.6 = (bf16[8,80,256]{2,1,0:T(8,128)(2,1)}, bf16[8,80,256]{2,1,0:T(8,128)(2,1)S(1)}, u32[]{:S(2)}, u32[]{:S(2)}) collective-permute-start(bf16[8,80,256]{2,1,0:T(8,128)(2,1)} %collective-permute-done.2.refs_2_), channel_id=1, source_target_pairs={{0,8},{8,0},{16,24},{24,16},{1,9},{9,1},{17,25},{25,17},{2,10},{10... | collective-permute-start | bytes 983048 | tf_op jit(solution)/shard_map/ppermute | solution.py:349
  44.0 2.7 %collective-permute-start.7 = (bf16[8,80,256]{2,1,0:T(8,128)(2,1)}, bf16[8,80,256]{2,1,0:T(8,128)(2,1)S(1)}, u32[]{:S(2)}, u32[]{:S(2)}) collective-permute-start(bf16[8,80,256]{2,1,0:T(8,128)(2,1)} %collective-permute-done.3.refs_3_), channel_id=1, source_target_pairs={{0,8},{8,0},{16,24},{24,16},{1,9},{9,1},{17,25},{25,17},{2,10},{10... | collective-permute-start | bytes 983048 | tf_op jit(solution)/shard_map/ppermute | solution.py:349

commit v8 on v7

--- a/solution.py
+++ b/solution.py
@@ -12,8 +12,8 @@
 RUN = 128
 PAD = 16
 PAIR = 2
-CHUNK = 1024
-SLAB = 64
+CHUNK = 4
+SLAB = 128
 GROUP = 8
 VMEM = 60 * 2**20
 X = 2
@@ -84,69 +84,67 @@
 
 
 def attention_kernel(
-    query_ref, grad_ref, delta_ref, lse_ref, pos_ref, kv_ref, dq_ref, dkv_ref, key_t, acc
+    query_ref, grad_ref, delta_ref, lse_ref, pos_ref, kv_ref, dq_ref, dkv_ref, key_t, dq, dkv, *sems
 ):
-    step = pl.program_id(0)
+    dq_sems, dkv_sems = sems
     blocks, rows, _ = kv_ref.shape
     keys = rows - PAD
-    tokens = query_ref.shape[0]
-
-    def gathered(chunk, cols):
-        count = CHUNK // keys
-        return jnp.concatenate(
-            [kv_ref[chunk * count + i, :keys, cols] for i in range(count)], axis=0
+    tokens, width = query_ref.shape
+    wide = PAIR * HD
+    dq_stores = [
+        pltpu.make_async_copy(
+            dq.at[:, pl.ds(i * wide, wide)], dq_ref.at[:, pl.ds(i * wide, wide)], dq_sems.at[i]
         )
-
-    @pl.when(step == 0)
-    def _():
-        acc[...] = jnp.zeros_like(acc)
-        for block in range(blocks):
+        for i in range(width // wide)
+    ]
+    dkv_stores = [
+        pltpu.make_async_copy(dkv.at[i], dkv_ref.at[i], dkv_sems.at[i]) for i in range(blocks)
+    ]
+    query_pos = pos_ref[...].astype(F32)
+    offsets = lax.broadcasted_iota(jnp.int32, (RUN, tokens), 0).astype(F32)
+    for first in range(0, blocks, CHUNK):
+        chunk = range(first, first + CHUNK)
+        visible = []
+        for block in chunk:
             here = slice(block * keys, (block + 1) * keys)
             key_t[:, here] = jnp.transpose(kv_ref[block, :keys, :HD])
-
-    query_pos = pos_ref[...].astype(F32)
-    offsets = lax.broadcasted_iota(jnp.int32, (RUN, tokens), 0).astype(F32)
-    for chunk in range(blocks * keys // CHUNK):
-        here = slice(chunk * CHUNK, (chunk + 1) * CHUNK)
-        visible = []
-        for run in range(chunk * CHUNK // RUN, (chunk + 1) * CHUNK // RUN):
-            block, row = run // (keys // RUN), keys + run % (keys // RUN)
-            start = kv_ref[block, row : row + 1, :1].astype(F32) * RUN
-            visible.append(offsets <= query_pos - start)
+            for run in range(keys // RUN):
+                start = kv_ref[block, keys + run : keys + run + 1, :1].astype(F32) * RUN
+                visible.append(offsets <= query_pos - start)
         visible = jnp.concatenate(visible, axis=0)
-        key = gathered(chunk, slice(0, HD))
-        value = gathered(chunk, slice(HD, 2 * HD))
-        key_part = None
-        value_part = None
-        for i in range(PAIR):
-            cols = slice(i * HD, (i + 1) * HD)
-            wide = pl.ds(pl.multiple_of((step * PAIR + i) * HD, HD), HD)
-            query = query_ref[:, wide]
-            grad = grad_ref[:, wide]
-            delta = delta_ref[pl.ds(step * PAIR + i, 1), :]
-            lse = lse_ref[pl.ds(step * PAIR + i, 1), :] * LOG2E
+        key = jnp.concatenate([kv_ref[block, :keys, :HD] for block in chunk], axis=0)
+        value = jnp.concatenate([kv_ref[block, :keys, HD:] for block in chunk], axis=0)
+        here = slice(first * keys, (first + CHUNK) * keys)
+        key_total = None
+        value_total = None
+        for head in range(width // HD):
+            cols = slice(head * HD, (head + 1) * HD)
+            query = query_ref[:, cols]
+            grad = grad_ref[:, cols]
+            delta = delta_ref[head : head + 1, :]
+            lse = lse_ref[head : head + 1, :] * LOG2E
             scores = dot(key, query, ROWS_ROWS)
             probs = jnp.where(visible, jnp.exp2(scores * (FACTOR * LOG2E) - lse), 0.0)
             dprobs = dot(value, grad, ROWS_ROWS)
             dscores = (probs * (dprobs - delta)).astype(BF16)
             dv = dot(probs.astype(BF16), grad, COLS_ROWS)
             dk = dot(dscores, query, COLS_ROWS)
-            dq = jnp.transpose(dot(key_t[:, here], dscores, COLS_ROWS)) * FACTOR
-            if chunk == 0:
-                dq_ref[:, cols] = dq
+            part = jnp.transpose(dot(key_t[:, here], dscores, COLS_ROWS)) * FACTOR
+            if first == 0:
+                dq[:, cols] = part
             else:
-                dq_ref[:, cols] += dq
-            key_part = dk if key_part is None else key_part + dk
-            value_part = dv if value_part is None else value_part + dv
-        acc[here, :HD] += key_part
-        acc[here, HD:] += value_part
-
-    @pl.when(step == pl.num_programs(0) - 1)
-    def _():
-        for block in range(blocks):
-            here = slice(block * keys, (block + 1) * keys)
-            dkv_ref[block, :, :HD] = (acc[here, :HD] * FACTOR).astype(BF16)
-            dkv_ref[block, :, HD:] = acc[here, HD:].astype(BF16)
+                dq[:, cols] += part
+            if first + CHUNK == blocks and head % PAIR == PAIR - 1:
+                dq_stores[head // PAIR].start()
+            key_total = dk if key_total is None else key_total + dk
+            value_total = dv if value_total is None else value_total + dv
+        for i, block in enumerate(chunk):
+            part = slice(i * keys, (i + 1) * keys)
+            dkv[block, :, :HD] = (key_total[part] * FACTOR).astype(BF16)
+            dkv[block, :, HD:] = value_total[part].astype(BF16)
+            dkv_stores[block].start()
+    for store in dq_stores + dkv_stores:
+        store.wait()
 
 
 def attention(query, grad, delta, lse, pos, kv):
@@ -154,30 +152,20 @@
     heads = width // HD
     blocks, rows, cols = kv.shape
     keys = rows - PAD
-    by_head = pl.BlockSpec((tokens, PAIR * HD), lambda h: (0, h))
-
-    def whole(*shape):
-        return pl.BlockSpec(shape, lambda h: (0,) * len(shape))
-
     return pl.pallas_call(
         attention_kernel,
-        grid=(heads // PAIR,),
-        in_specs=[
-            pl.BlockSpec(memory_space=pltpu.VMEM),
-            pl.BlockSpec(memory_space=pltpu.VMEM),
-            whole(heads, tokens),
-            whole(heads, tokens),
-            whole(1, tokens),
-            pl.BlockSpec(memory_space=pltpu.VMEM),
-        ],
-        out_specs=[by_head, whole(blocks, keys, cols)],
+        in_specs=[pl.BlockSpec(memory_space=pltpu.VMEM)] * 6,
+        out_specs=[pl.BlockSpec(memory_space=pl.ANY)] * 2,
         out_shape=[
             jax.ShapeDtypeStruct((tokens, width), F32),
             jax.ShapeDtypeStruct((blocks, keys, cols), BF16),
         ],
         scratch_shapes=[
             pltpu.VMEM((HD, blocks * keys), BF16),
-            pltpu.VMEM((blocks * keys, cols), F32),
+            pltpu.VMEM((tokens, width), F32),
+            pltpu.VMEM((blocks, keys, cols), BF16),
+            pltpu.SemaphoreType.DMA((heads // PAIR,)),
+            pltpu.SemaphoreType.DMA((blocks,)),
         ],
         compiler_params=pltpu.CompilerParams(vmem_limit_bytes=32 * 2**20),
         cost_estimate=pl.CostEstimate(
@@ -283,12 +271,22 @@
     )(place, *own, *other)
 
 
-def finish_kernel(parts_ref, key_ref, value_ref, low_ref):
-    for start in range(0, parts_ref.shape[1], SLAB):
+def finish_kernel(parts_ref, key_ref, value_ref, low_ref, parts, sems):
+    slabs = range(0, parts.shape[1], SLAB)
+    loads = [
+        pltpu.make_async_copy(
+            parts_ref.at[:, pl.ds(start, SLAB)], parts.at[:, pl.ds(start, SLAB)], sems.at[i]
+        )
+        for i, start in enumerate(slabs)
+    ]
+    for load in loads:
+        load.start()
+    for load, start in zip(loads, slabs):
+        load.wait()
         here = slice(start, start + SLAB)
-        total = parts_ref[0, here, :].astype(F32)
-        for i in range(1, parts_ref.shape[0]):
-            total = total + parts_ref[i, here, :].astype(F32)
+        total = parts[0, here, :].astype(F32)
+        for i in range(1, parts.shape[0]):
+            total = total + parts[i, here, :].astype(F32)
         key_ref[here, :] = total[:, :HD]
         value_ref[here, :] = total[:, HD:]
         low = total.astype(BF16)
@@ -297,12 +295,16 @@
 
 
 def finish(parts):
-    _, tokens, cols = parts.shape
+    count, tokens, cols = parts.shape
     half = jax.ShapeDtypeStruct((tokens, cols // 2), F32)
     return pl.pallas_call(
         finish_kernel,
-        in_specs=[pl.BlockSpec(memory_space=pltpu.VMEM)],
+        in_specs=[pl.BlockSpec(memory_space=pl.ANY)],
         out_shape=[half, half, jax.ShapeDtypeStruct(parts.shape, BF16)],
+        scratch_shapes=[
+            pltpu.VMEM((count, tokens, cols), BF16),
+            pltpu.SemaphoreType.DMA((tokens // SLAB,)),
+        ],
         compiler_params=pltpu.CompilerParams(vmem_limit_bytes=16 * 2**20),
         name="finish",
     )(parts)

time: 96.8 us -> 96.6 us (level)
  Pallas kernels: 22.7 us -> 21.6 us
    pallas_call x2, Pallas kernels: 14.7 us -> 13.6 us  [the longest x1 11.7 us: attention(): pl.pallas_call(attention_kernel, in_specs=[pl.BlockSpec(memory_space=pltp...]
    ppermute x4, waiting for transfers between devices: 1.28 us -> 2.25 us  [pass_along(): passed.append(lax.ppermute(piece, ('heads', 'ctx'), route))]
  transfers between devices with their start and end apart: 10 -> 10, of which waited for: 6 -> 6; matrix products, arithmetic and copies ran while one was open for 1% -> 1% of each run, Pallas kernels for 18% -> 17%
where the time goes in v8:
time: 96.6 us; the launch traced here: 96.2 us
  blocking collectives  37.3 us (39%)
  starting transfers between devices  23.3 us (24%)
  Pallas kernels  21.6 us (22%)
  waiting for transfers between devices  11.8 us (12%)
  other arithmetic  1.32 us (1%)
    all_to_all x1, blocking collectives, exchange_dp(): lax.all_to_all(parts, ('dp', 'heads'), 0, 0, axis_index_groups=groups, ti...  18.8 us
    all_to_all x1, blocking collectives, exchange_ctx(): lax.all_to_all(parts, ('heads', 'ctx'), 0, 0, axis_index_groups=groups, t...  18.6 us
    all_to_all x2, starting transfers between devices, exchange_ctx(): lax.all_to_all(parts, ('heads', 'ctx'), 0, 0, axis_index_groups=groups, t...  12.3 us
    pallas_call x1, Pallas kernels, attention(): pl.pallas_call(attention_kernel, in_specs=[pl.BlockSpec(memory_space=pltp...  11.7 us
    ppermute x4, starting transfers between devices, pass_along(): passed.append(lax.ppermute(piece, ('heads', 'ctx'), route))  9.95 us
    all_to_all x2, waiting for transfers between devices, exchange_ctx(): lax.all_to_all(parts, ('heads', 'ctx'), 0, 0, axis_index_groups=groups, t...  7.38 us
    pallas_call x1, Pallas kernels, spread(): pl.pallas_call(spread_kernel, in_specs=[pl.BlockSpec(memory_space=pltpu.S...  3.49 us
    ppermute x4, waiting for transfers between devices, pass_along(): passed.append(lax.ppermute(piece, ('heads', 'ctx'), route))  2.25 us
  transfers between devices with their start and end apart: 10, of which 6 were waited for; matrix products, arithmetic and copies ran while one was open for 1% of the time, Pallas kernels for 17%

profile of v8, /device:TPU:6, one launch (start us, length us, event | category | flops | bytes accessed | tf_op | source)
XLA Modules:
  0.0 96.2 jit_solution(100945047300161856)
XLA Ops:
  0.6 2.0 %pack.1 = bf16[8,272,256]{2,1,0:T(8,128)(2,1)} custom-call(bf16[256,128]{1,0:T(8,128)(2,1)} %bitcast.22, bf16[256,128]{1,0:T(8,128)(2,1)} %bitcast.23, s32[1,256]{1,0:T(1,128)} %pos_ref.3), custom_call_target="tpu_custom_call" | custom-call | tf_op jit(solution)/shard_map/pack/pallas_call | solution.py:58
  2.7 0.0 copy-start
  2.7 0.0 copy-start.1
  2.7 0.0 copy-start.2
  2.7 6.1 %all-to-all-start = ((bf16[8,272,256]{2,1,0:T(8,128)(2,1)}), bf16[8,272,256]{2,1,0:T(8,128)(2,1)S(1)}, u32[]{:S(2)}, u32[]{:S(2)}) async-start(bf16[8,272,256]{2,1,0:T(8,128)(2,1)} %pack.1), calls=%async_computation | async-start | bytes 2228224 | tf_op jit(solution)/shard_map/all_to_all | solution.py:338
  8.8 0.0 copy-start.4
  8.8 0.0 copy-start.5
  8.8 0.6 pad_add_fusion.place_ref
  9.4 3.5 %spread.1 = (bf16[8,80,256]{2,1,0:T(8,128)(2,1)}, bf16[8,80,256]{2,1,0:T(8,128)(2,1)}, bf16[8,80,256]{2,1,0:T(8,128)(2,1)}, bf16[8,80,256]{2,1,0:T(8,128)(2,1)}) custom-call(s32[3]{0:T(128)} %pad_add_fusion.place_ref, bf16[256,5120]{1,0:T(8,128)(2,1)} %bitcast.21), custom_call_target="tpu_custom_call" | custom-call | tf_op jit(solution)/shard_map/spread/pallas_call | solution.py:218
  12.9 2.0 %collective-permute-start = (bf16[8,80,256]{2,1,0:T(8,128)(2,1)}, bf16[8,80,256]{2,1,0:T(8,128)(2,1)S(1)}, u32[]{:S(2)}, u32[]{:S(2)}) collective-permute-start(bf16[8,80,256]{2,1,0:T(8,128)(2,1)} %get-tuple-element.21), channel_id=1, source_target_pairs={{0,4},{1,5},{2,6},{3,7},{4,0},{5,1},{6,2},{7,3},{8,8},{9,9},{10,10... | collective-permute-start | bytes 983048 | tf_op jit(solution)/shard_map/ppermute | solution.py:244
  14.9 3.0 %collective-permute-start.1 = (bf16[8,80,256]{2,1,0:T(8,128)(2,1)}, bf16[8,80,256]{2,1,0:T(8,128)(2,1)S(1)}, u32[]{:S(2)}, u32[]{:S(2)}) collective-permute-start(bf16[8,80,256]{2,1,0:T(8,128)(2,1)} %get-tuple-element.22), channel_id=1, source_target_pairs={{0,5},{1,6},{2,7},{3,4},{4,1},{5,2},{6,3},{7,0},{8,9},{9,10},{10,1... | collective-permute-start | bytes 983048 | tf_op jit(solution)/shard_map/ppermute | solution.py:244
  17.9 2.7 %collective-permute-start.2 = (bf16[8,80,256]{2,1,0:T(8,128)(2,1)}, bf16[8,80,256]{2,1,0:T(8,128)(2,1)}, u32[]{:S(2)}, u32[]{:S(2)}) collective-permute-start(bf16[8,80,256]{2,1,0:T(8,128)(2,1)} %get-tuple-element.23), channel_id=1, source_target_pairs={{0,6},{1,7},{2,4},{3,5},{4,2},{5,3},{6,0},{7,1},{8,10},{9,11},{10,... | collective-permute-start | bytes 983048 | tf_op jit(solution)/shard_map/ppermute | solution.py:244
  20.5 2.4 %collective-permute-start.3 = (bf16[8,80,256]{2,1,0:T(8,128)(2,1)}, bf16[8,80,256]{2,1,0:T(8,128)(2,1)}, u32[]{:S(2)}, u32[]{:S(2)}) collective-permute-start(bf16[8,80,256]{2,1,0:T(8,128)(2,1)} %get-tuple-element.24), channel_id=1, source_target_pairs={{0,7},{1,4},{2,5},{3,6},{4,3},{5,0},{6,1},{7,2},{8,11},{9,8},{10,9... | collective-permute-start | bytes 983048 | tf_op jit(solution)/shard_map/ppermute | solution.py:244
  22.9 0.0 copy-done
  22.9 0.0 copy-done.1
  22.9 0.0 copy-done.2
  22.9 0.4 delta.1.delta_ref
  23.2 0.0 all-to-all-done.kv_ref
  23.3 0.0 copy-done.4
  23.3 0.0 copy-done.5
  23.3 0.0 copy-start.3
  23.3 11.7 %attention.1 = (f32[256,1024]{1,0:T(8,128)}, bf16[8,256,256]{2,1,0:T(8,128)(2,1)}) custom-call(bf16[256,1024]{1,0:T(8,128)(2,1)S(1)} %bitcast.17, bf16[256,1024]{1,0:T(8,128)(2,1)S(1)} %bitcast.19, f32[8,256]{1,0:T(8,128)S(1)} %delta.1.delta_ref, f32[8,256]{1,0:T(8,128)S(1)} %bitcast.20, s32[1,256]{1,0:T(1,128)S(1)} %copy-done.4, ...), custom_call_target="tpu_custom_call" | custom-call | flops 5368709120 | bytes 12582912 | tf_op jit(solution)/shard_map/attention/pallas_call | solution.py:155
  35.0 0.0 collective-permute-done.refs_0_
  35.0 0.0 collective-permute-done.1.refs_1_
  35.0 0.0 collective-permute-done.2.refs_2_
  35.0 2.2 %collective-permute-done.3.refs_3_ = bf16[8,80,256]{2,1,0:T(8,128)(2,1)} collective-permute-done((bf16[8,80,256]{2,1,0:T(8,128)(2,1)}, bf16[8,80,256]{2,1,0:T(8,128)(2,1)}, u32[]{:S(2)}, u32[]{:S(2)}) %collective-permute-start.3) | collective-permute-done | bytes 327712 | tf_op jit(solution)/shard_map/ppermute | solution.py:244
  37.2 6.2 %all-to-all-start.1 = ((bf16[8,256,256]{2,1,0:T(8,128)(2,1)}), bf16[8,256,256]{2,1,0:T(8,128)(2,1)}, u32[]{:S(2)}, u32[]{:S(2)}) async-start(bf16[8,256,256]{2,1,0:T(8,128)(2,1)} %get-tuple-element.28), calls=%async_computation.1 | async-start | bytes 2097152 | tf_op jit(solution)/shard_map/all_to_all | solution.py:338
  43.5 0.0 collective-permute-start.4
  43.5 0.5 collective-permute-start.5
  44.0 0.0 collective-permute-start.6
  44.0 0.5 collective-permute-start.7
  44.5 0.6 collective-permute-done.4.refs_4_
  45.1 0.6 collective-permute-done.5.refs_5_
  45.7 0.6 collective-permute-done.6.refs_6_
  46.2 0.5 collective-permute-done.7.refs_7_
  46.7 0.0 copy-done.3
  46.7 1.3 %join.1.turned_ref = bf16[8,8,80,256]{3,2,1,0:T(8,128)(2,1)S(1)} custom-call(s32[3]{0:T(128)S(1)} %copy-done.3, bf16[8,80,256]{2,1,0:T(8,128)(2,1)S(1)} %collective-permute-done.refs_0_, bf16[8,80,256]{2,1,0:T(8,128)(2,1)S(1)} %collective-permute-done.1.refs_1_, bf16[8,80,256]{2,1,0:T(8,128)(2,1)} %collective-permute-done.2.refs_2_, ...), custom_call_target="tpu_custom_call" | custom-call | tf_op jit(solution)/shard_map/join/pallas_call | solution.py:264
  48.0 7.4 %all-to-all-done.1.parts_ref = bf16[8,256,256]{2,1,0:T(8,128)(2,1)} async-done(((bf16[8,256,256]{2,1,0:T(8,128)(2,1)}), bf16[8,256,256]{2,1,0:T(8,128)(2,1)}, u32[]{:S(2)}, u32[]{:S(2)}) %all-to-all-start.1) | async-done | bytes 1048608 | tf_op jit(solution)/shard_map/all_to_all | solution.py:338
  55.4 2.0 %finish.1 = (f32[256,128]{1,0:T(8,128)}, f32[256,128]{1,0:T(8,128)}, bf16[8,256,256]{2,1,0:T(8,128)(2,1)S(1)}) custom-call(bf16[8,256,256]{2,1,0:T(8,128)(2,1)} %all-to-all-done.1.parts_ref), custom_call_target="tpu_custom_call" | custom-call | tf_op jit(solution)/shard_map/finish/pallas_call | solution.py:300
  57.4 18.6 %all_to_all.20.low_ref = bf16[8,256,256]{2,1,0:T(8,128)(2,1)S(1)} all-to-all(bf16[8,256,256]{2,1,0:T(8,128)(2,1)S(1)} %get-tuple-element.37), channel_id=1, replica_groups={{0,1,2,3,4,5,6,7},{14,15,12,13,10,11,8,9},{16,17,18,19,20,21,22,23},{30..., dimensions={0} | all-to-all | bytes 2097152 | tf_op jit(solution)/shard_map/all_to_all | solution.py:338
  75.9 0.8 project.1
  76.8 18.8 %all_to_all.21 = bf16[8,80,256]{2,1,0:T(8,128)(2,1)S(1)} all-to-all(bf16[8,80,256]{2,1,0:T(8,128)(2,1)S(1)} %project.1), channel_id=1, replica_groups={{64,96,0,32,192,224,128,160},{200,232,136,168,72,104,8,40},{80,112,16,4..., dimensions={0} | all-to-all | bytes 655360 | tf_op jit(solution)/shard_map/all_to_all | solution.py:346
  95.5 0.7 convert_reduce_fusion
Async XLA Ops:
  2.7 20.2 %copy-start = (bf16[1,256,1024]{2,1,0:T(8,128)(2,1)S(1)}, bf16[1,256,1024]{2,1,0:T(8,128)(2,1)}, u32[]{:S(2)}) copy-start(bf16[1,256,1024]{2,1,0:T(8,128)(2,1)} %param.12) | copy-start | bytes 1572868
  2.7 20.2 %copy-start.1 = (bf16[1,256,1024]{2,1,0:T(8,128)(2,1)S(1)}, bf16[1,256,1024]{2,1,0:T(8,128)(2,1)}, u32[]{:S(2)}) copy-start(bf16[1,256,1024]{2,1,0:T(8,128)(2,1)} %param.9) | copy-start | bytes 1572868
  2.7 20.2 %copy-start.2 = (bf16[1,256,1024]{2,1,0:T(8,128)(2,1)S(1)}, bf16[1,256,1024]{2,1,0:T(8,128)(2,1)}, u32[]{:S(2)}) copy-start(bf16[1,256,1024]{2,1,0:T(8,128)(2,1)} %param.13) | copy-start | bytes 1572868
  2.7 20.5 %all-to-all-start = ((bf16[8,272,256]{2,1,0:T(8,128)(2,1)}), bf16[8,272,256]{2,1,0:T(8,128)(2,1)S(1)}, u32[]{:S(2)}, u32[]{:S(2)}) async-start(bf16[8,272,256]{2,1,0:T(8,128)(2,1)} %pack.1), calls=%async_computation | async-start | bytes 2228224 | tf_op jit(solution)/shard_map/all_to_all | solution.py:338
  8.8 14.5 %copy-start.4 = (s32[1,256]{1,0:T(1,128)S(1)}, s32[1,256]{1,0:T(1,128)}, u32[]{:S(2)}) copy-start(s32[1,256]{1,0:T(1,128)} %pos_ref.3) | copy-start | bytes 3076
  8.8 14.5 %copy-start.5 = (f32[1,256,8]{1,2,0:T(8,128)S(1)}, f32[1,256,8]{1,2,0:T(8,128)}, u32[]{:S(2)}) copy-start(f32[1,256,8]{1,2,0:T(8,128)} %param.14) | copy-start | bytes 24580
  12.9 22.0 %collective-permute-start = (bf16[8,80,256]{2,1,0:T(8,128)(2,1)}, bf16[8,80,256]{2,1,0:T(8,128)(2,1)S(1)}, u32[]{:S(2)}, u32[]{:S(2)}) collective-permute-start(bf16[8,80,256]{2,1,0:T(8,128)(2,1)} %get-tuple-element.21), channel_id=1, source_target_pairs={{0,4},{1,5},{2,6},{3,7},{4,0},{5,1},{6,2},{7,3},{8,8},{9,9},{10,10... | collective-permute-start | bytes 983048 | tf_op jit(solution)/shard_map/ppermute | solution.py:244
  14.9 20.1 %collective-permute-start.1 = (bf16[8,80,256]{2,1,0:T(8,128)(2,1)}, bf16[8,80,256]{2,1,0:T(8,128)(2,1)S(1)}, u32[]{:S(2)}, u32[]{:S(2)}) collective-permute-start(bf16[8,80,256]{2,1,0:T(8,128)(2,1)} %get-tuple-element.22), channel_id=1, source_target_pairs={{0,5},{1,6},{2,7},{3,4},{4,1},{5,2},{6,3},{7,0},{8,9},{9,10},{10,1... | collective-permute-start | bytes 983048 | tf_op jit(solution)/shard_map/ppermute | solution.py:244
  17.9 17.1 %collective-permute-start.2 = (bf16[8,80,256]{2,1,0:T(8,128)(2,1)}, bf16[8,80,256]{2,1,0:T(8,128)(2,1)}, u32[]{:S(2)}, u32[]{:S(2)}) collective-permute-start(bf16[8,80,256]{2,1,0:T(8,128)(2,1)} %get-tuple-element.23), channel_id=1, source_target_pairs={{0,6},{1,7},{2,4},{3,5},{4,2},{5,3},{6,0},{7,1},{8,10},{9,11},{10,... | collective-permute-start | bytes 983048 | tf_op jit(solution)/shard_map/ppermute | solution.py:244
  20.5 16.7 %collective-permute-start.3 = (bf16[8,80,256]{2,1,0:T(8,128)(2,1)}, bf16[8,80,256]{2,1,0:T(8,128)(2,1)}, u32[]{:S(2)}, u32[]{:S(2)}) collective-permute-start(bf16[8,80,256]{2,1,0:T(8,128)(2,1)} %get-tuple-element.24), channel_id=1, source_target_pairs={{0,7},{1,4},{2,5},{3,6},{4,3},{5,0},{6,1},{7,2},{8,11},{9,8},{10,9... | collective-permute-start | bytes 983048 | tf_op jit(solution)/shard_map/ppermute | solution.py:244
  23.3 23.4 %copy-start.3 = (s32[3]{0:T(128)S(1)}, s32[3]{0:T(128)}, u32[]{:S(2)}) copy-start(s32[3]{0:T(128)} %pad_add_fusion.place_ref) | copy-start | bytes 40
  37.2 18.2 %all-to-all-start.1 = ((bf16[8,256,256]{2,1,0:T(8,128)(2,1)}), bf16[8,256,256]{2,1,0:T(8,128)(2,1)}, u32[]{:S(2)}, u32[]{:S(2)}) async-start(bf16[8,256,256]{2,1,0:T(8,128)(2,1)} %get-tuple-element.28), calls=%async_computation.1 | async-start | bytes 2097152 | tf_op jit(solution)/shard_map/all_to_all | solution.py:338
  43.5 1.6 %collective-permute-start.4 = (bf16[8,80,256]{2,1,0:T(8,128)(2,1)S(1)}, bf16[8,80,256]{2,1,0:T(8,128)(2,1)S(1)}, u32[]{:S(2)}, u32[]{:S(2)}) collective-permute-start(bf16[8,80,256]{2,1,0:T(8,128)(2,1)S(1)} %collective-permute-done.refs_0_), channel_id=1, source_target_pairs={{0,8},{8,0},{16,24},{24,16},{1,9},{9,1},{17,25},{25,17},{2,10},{10... | collective-permute-start | bytes 983048 | tf_op jit(solution)/shard_map/ppermute | solution.py:351
  43.5 2.2 %collective-permute-start.5 = (bf16[8,80,256]{2,1,0:T(8,128)(2,1)S(1)}, bf16[8,80,256]{2,1,0:T(8,128)(2,1)S(1)}, u32[]{:S(2)}, u32[]{:S(2)}) collective-permute-start(bf16[8,80,256]{2,1,0:T(8,128)(2,1)S(1)} %collective-permute-done.1.refs_1_), channel_id=1, source_target_pairs={{0,8},{8,0},{16,24},{24,16},{1,9},{9,1},{17,25},{25,17},{2,10},{10... | collective-permute-start | bytes 983048 | tf_op jit(solution)/shard_map/ppermute | solution.py:351
  44.0 2.3 %collective-permute-start.6 = (bf16[8,80,256]{2,1,0:T(8,128)(2,1)}, bf16[8,80,256]{2,1,0:T(8,128)(2,1)S(1)}, u32[]{:S(2)}, u32[]{:S(2)}) collective-permute-start(bf16[8,80,256]{2,1,0:T(8,128)(2,1)} %collective-permute-done.2.refs_2_), channel_id=1, source_target_pairs={{0,8},{8,0},{16,24},{24,16},{1,9},{9,1},{17,25},{25,17},{2,10},{10... | collective-permute-start | bytes 983048 | tf_op jit(solution)/shard_map/ppermute | solution.py:351
  44.0 2.7 %collective-permute-start.7 = (bf16[8,80,256]{2,1,0:T(8,128)(2,1)}, bf16[8,80,256]{2,1,0:T(8,128)(2,1)S(1)}, u32[]{:S(2)}, u32[]{:S(2)}) collective-permute-start(bf16[8,80,256]{2,1,0:T(8,128)(2,1)} %collective-permute-done.3.refs_3_), channel_id=1, source_target_pairs={{0,8},{8,0},{16,24},{24,16},{1,9},{9,1},{17,25},{25,17},{2,10},{10... | collective-permute-start | bytes 983048 | tf_op jit(solution)/shard_map/ppermute | solution.py:351

commit v9 on v8

--- a/solution.py
+++ b/solution.py
@@ -363,7 +363,8 @@
     query_grad, partial = attention(
         queries[0], out_grad[0], delta, jnp.transpose(lse[0]), positions, kv
     )
-    partial, own = lax.optimization_barrier((partial, own))
+    partial, *early = lax.optimization_barrier((partial, *own[1:]))
+    own = own[:1] + early
     turned = join(own, [with_neighbour(block) for block in own], place)
     key_grad, value_grad, low = finish(exchange_ctx(partial, PART_ORDER))
     low, turned = lax.optimization_barrier((low, turned))

time: 96.6 us -> 106 us (1.097)
  waiting for transfers between devices: 11.8 us -> 17.1 us
  starting transfers between devices: 23.3 us -> 27 us
    ppermute x4, waiting for transfers between devices: 2.25 us -> 12 us  [pass_along(): passed.append(lax.ppermute(piece, ('heads', 'ctx'), route))]
    all_to_all x2, starting transfers between devices: 12.3 us -> 17.5 us  [exchange_ctx(): lax.all_to_all(parts, ('heads', 'ctx'), 0, 0, axis_index_groups=groups, t...]
    all_to_all x2, waiting for transfers between devices: 7.38 us -> 2.82 us  [exchange_ctx(): lax.all_to_all(parts, ('heads', 'ctx'), 0, 0, axis_index_groups=groups, t...]
    ppermute x4, starting transfers between devices: 9.95 us -> 8.49 us  [pass_along(): passed.append(lax.ppermute(piece, ('heads', 'ctx'), route))]
  transfers between devices with their start and end apart: 10 -> 10, of which waited for: 6 -> 6; matrix products, arithmetic and copies ran while one was open for 1% -> 1% of each run, Pallas kernels for 17% -> 16%
where the time goes in v9:
time: 106 us; the launch traced here: 105 us
  blocking collectives  36.9 us (35%)
  starting transfers between devices  27 us (25%)
  Pallas kernels  21.6 us (20%)
  waiting for transfers between devices  17.1 us (16%)
  other arithmetic  1.27 us (1%)
    all_to_all x1, blocking collectives, exchange_ctx(): lax.all_to_all(parts, ('heads', 'ctx'), 0, 0, axis_index_groups=groups, t...  18.5 us
    all_to_all x1, blocking collectives, exchange_dp(): lax.all_to_all(parts, ('dp', 'heads'), 0, 0, axis_index_groups=groups, ti...  18.4 us
    all_to_all x2, starting transfers between devices, exchange_ctx(): lax.all_to_all(parts, ('heads', 'ctx'), 0, 0, axis_index_groups=groups, t...  17.5 us
    ppermute x4, waiting for transfers between devices, pass_along(): passed.append(lax.ppermute(piece, ('heads', 'ctx'), route))  12 us
    pallas_call x1, Pallas kernels, attention(): pl.pallas_call(attention_kernel, in_specs=[pl.BlockSpec(memory_space=pltp...  11.7 us
    ppermute x4, starting transfers between devices, pass_along(): passed.append(lax.ppermute(piece, ('heads', 'ctx'), route))  8.49 us
    pallas_call x1, Pallas kernels, spread(): pl.pallas_call(spread_kernel, in_specs=[pl.BlockSpec(memory_space=pltpu.S...  3.5 us
    all_to_all x2, waiting for transfers between devices, exchange_ctx(): lax.all_to_all(parts, ('heads', 'ctx'), 0, 0, axis_index_groups=groups, t...  2.82 us
  transfers between devices with their start and end apart: 10, of which 6 were waited for; matrix products, arithmetic and copies ran while one was open for 1% of the time, Pallas kernels for 16%

profile of v9, /device:TPU:6, one launch (start us, length us, event | category | flops | bytes accessed | tf_op | source)
XLA Modules:
  0.0 104.6 jit_solution(4401027745251928097)
XLA Ops:
  0.6 2.0 %pack.1 = bf16[8,272,256]{2,1,0:T(8,128)(2,1)} custom-call(bf16[256,128]{1,0:T(8,128)(2,1)} %bitcast.22, bf16[256,128]{1,0:T(8,128)(2,1)} %bitcast.23, s32[1,256]{1,0:T(1,128)} %pos_ref.3), custom_call_target="tpu_custom_call" | custom-call | tf_op jit(solution)/shard_map/pack/pallas_call | solution.py:58
  2.7 0.0 copy-start
  2.7 0.0 copy-start.1
  2.7 0.0 copy-start.2
  2.7 6.1 %all-to-all-start = ((bf16[8,272,256]{2,1,0:T(8,128)(2,1)}), bf16[8,272,256]{2,1,0:T(8,128)(2,1)S(1)}, u32[]{:S(2)}, u32[]{:S(2)}) async-start(bf16[8,272,256]{2,1,0:T(8,128)(2,1)} %pack.1), calls=%async_computation | async-start | bytes 2228224 | tf_op jit(solution)/shard_map/all_to_all | solution.py:338
  8.8 0.0 copy-start.4
  8.8 0.0 copy-start.5
  8.8 0.6 pad_add_fusion.place_ref
  9.4 3.5 %spread.1 = (bf16[8,80,256]{2,1,0:T(8,128)(2,1)}, bf16[8,80,256]{2,1,0:T(8,128)(2,1)}, bf16[8,80,256]{2,1,0:T(8,128)(2,1)}, bf16[8,80,256]{2,1,0:T(8,128)(2,1)}) custom-call(s32[3]{0:T(128)} %pad_add_fusion.place_ref, bf16[256,5120]{1,0:T(8,128)(2,1)} %bitcast.21), custom_call_target="tpu_custom_call" | custom-call | tf_op jit(solution)/shard_map/spread/pallas_call | solution.py:218
  12.9 1.5 %collective-permute-start = (bf16[8,80,256]{2,1,0:T(8,128)(2,1)}, bf16[8,80,256]{2,1,0:T(8,128)(2,1)S(1)}, u32[]{:S(2)}, u32[]{:S(2)}) collective-permute-start(bf16[8,80,256]{2,1,0:T(8,128)(2,1)} %get-tuple-element.21), channel_id=1, source_target_pairs={{0,5},{1,6},{2,7},{3,4},{4,1},{5,2},{6,3},{7,0},{8,9},{9,10},{10,1... | collective-permute-start | bytes 983048 | tf_op jit(solution)/shard_map/ppermute | solution.py:244
  14.4 3.6 %collective-permute-start.1 = (bf16[8,80,256]{2,1,0:T(8,128)(2,1)}, bf16[8,80,256]{2,1,0:T(8,128)(2,1)S(1)}, u32[]{:S(2)}, u32[]{:S(2)}) collective-permute-start(bf16[8,80,256]{2,1,0:T(8,128)(2,1)} %get-tuple-element.22), channel_id=1, source_target_pairs={{0,6},{1,7},{2,4},{3,5},{4,2},{5,3},{6,0},{7,1},{8,10},{9,11},{10,... | collective-permute-start | bytes 983048 | tf_op jit(solution)/shard_map/ppermute | solution.py:244
  18.0 1.5 %collective-permute-start.2 = (bf16[8,80,256]{2,1,0:T(8,128)(2,1)}, bf16[8,80,256]{2,1,0:T(8,128)(2,1)}, u32[]{:S(2)}, u32[]{:S(2)}) collective-permute-start(bf16[8,80,256]{2,1,0:T(8,128)(2,1)} %get-tuple-element.23), channel_id=1, source_target_pairs={{0,7},{1,4},{2,5},{3,6},{4,3},{5,0},{6,1},{7,2},{8,11},{9,8},{10,9... | collective-permute-start | bytes 983048 | tf_op jit(solution)/shard_map/ppermute | solution.py:244
  19.5 0.0 copy-done
  19.5 0.0 copy-done.1
  19.5 0.0 copy-done.2
  19.5 0.4 delta.1.delta_ref
  19.8 2.8 %all-to-all-done.kv_ref = bf16[8,272,256]{2,1,0:T(8,128)(2,1)S(1)} async-done(((bf16[8,272,256]{2,1,0:T(8,128)(2,1)}), bf16[8,272,256]{2,1,0:T(8,128)(2,1)S(1)}, u32[]{:S(2)}, u32[]{:S(2)}) %all-to-all-start) | async-done | bytes 1114144 | tf_op jit(solution)/shard_map/all_to_all | solution.py:338
  22.6 0.0 copy-done.4
  22.6 0.0 copy-done.5
  22.7 0.0 copy-start.6
  22.7 0.0 copy-start.3
  22.7 11.7 %attention.1 = (f32[256,1024]{1,0:T(8,128)}, bf16[8,256,256]{2,1,0:T(8,128)(2,1)}) custom-call(bf16[256,1024]{1,0:T(8,128)(2,1)S(1)} %bitcast.17, bf16[256,1024]{1,0:T(8,128)(2,1)S(1)} %bitcast.19, f32[8,256]{1,0:T(8,128)S(1)} %delta.1.delta_ref, f32[8,256]{1,0:T(8,128)S(1)} %bitcast.20, s32[1,256]{1,0:T(1,128)S(1)} %copy-done.4, ...), custom_call_target="tpu_custom_call" | custom-call | flops 5368709120 | bytes 12582912 | tf_op jit(solution)/shard_map/attention/pallas_call | solution.py:155
  34.3 0.0 collective-permute-done.refs_1_
  34.3 0.0 collective-permute-done.1.refs_2_
  34.4 0.0 collective-permute-done.2.refs_3_
  34.4 11.5 %all-to-all-start.1 = ((bf16[8,256,256]{2,1,0:T(8,128)(2,1)}), bf16[8,256,256]{2,1,0:T(8,128)(2,1)}, u32[]{:S(2)}, u32[]{:S(2)}) async-start(bf16[8,256,256]{2,1,0:T(8,128)(2,1)} %get-tuple-element.27), calls=%async_computation.1 | async-start | bytes 2097152 | tf_op jit(solution)/shard_map/all_to_all | solution.py:338
  45.8 0.0 copy-done.6
  45.8 1.9 %collective-permute-start.3 = (bf16[8,80,256]{2,1,0:T(8,128)(2,1)S(1)}, bf16[8,80,256]{2,1,0:T(8,128)(2,1)S(1)}, u32[]{:S(2)}, u32[]{:S(2)}) collective-permute-start(bf16[8,80,256]{2,1,0:T(8,128)(2,1)S(1)} %copy-done.6), channel_id=1, source_target_pairs={{0,4},{1,5},{2,6},{3,7},{4,0},{5,1},{6,2},{7,3},{8,8},{9,9},{10,10... | collective-permute-start | bytes 983048 | tf_op jit(solution)/shard_map/ppermute | solution.py:244
  47.7 12.0 %collective-permute-done.3.refs_0_ = bf16[8,80,256]{2,1,0:T(8,128)(2,1)S(1)} collective-permute-done((bf16[8,80,256]{2,1,0:T(8,128)(2,1)S(1)}, bf16[8,80,256]{2,1,0:T(8,128)(2,1)S(1)}, u32[]{:S(2)}, u32[]{:S(2)}) %collective-permute-start.3) | collective-permute-done | bytes 327712 | tf_op jit(solution)/shard_map/ppermute | solution.py:244
  59.8 0.0 collective-permute-start.4
  59.8 0.5 collective-permute-start.5
  60.3 0.0 collective-permute-start.6
  60.3 0.5 collective-permute-start.7
  60.8 0.6 collective-permute-done.4.refs_4_
  61.4 0.5 collective-permute-done.5.refs_5_
  61.9 0.9 collective-permute-done.6.refs_6_
  62.8 0.2 collective-permute-done.7.refs_7_
  63.0 0.0 copy-done.3
  63.0 1.2 %join.1.turned_ref = bf16[8,8,80,256]{3,2,1,0:T(8,128)(2,1)S(1)} custom-call(s32[3]{0:T(128)S(1)} %copy-done.3, bf16[8,80,256]{2,1,0:T(8,128)(2,1)S(1)} %collective-permute-done.3.refs_0_, bf16[8,80,256]{2,1,0:T(8,128)(2,1)S(1)} %collective-permute-done.refs_1_, bf16[8,80,256]{2,1,0:T(8,128)(2,1)S(1)} %collective-permute-done.1.refs_2_, ...), custom_call_target="tpu_custom_call" | custom-call | tf_op jit(solution)/shard_map/join/pallas_call | solution.py:264
  64.2 0.0 all-to-all-done.1.parts_ref
  64.2 2.0 %finish.1 = (f32[256,128]{1,0:T(8,128)}, f32[256,128]{1,0:T(8,128)}, bf16[8,256,256]{2,1,0:T(8,128)(2,1)S(1)}) custom-call(bf16[8,256,256]{2,1,0:T(8,128)(2,1)} %all-to-all-done.1.parts_ref), custom_call_target="tpu_custom_call" | custom-call | tf_op jit(solution)/shard_map/finish/pallas_call | solution.py:300
  66.2 18.5 %all_to_all.20.low_ref = bf16[8,256,256]{2,1,0:T(8,128)(2,1)S(1)} all-to-all(bf16[8,256,256]{2,1,0:T(8,128)(2,1)S(1)} %get-tuple-element.35), channel_id=1, replica_groups={{0,1,2,3,4,5,6,7},{14,15,12,13,10,11,8,9},{16,17,18,19,20,21,22,23},{30..., dimensions={0} | all-to-all | bytes 2097152 | tf_op jit(solution)/shard_map/all_to_all | solution.py:338
  84.7 0.8 project.1
  85.5 18.4 %all_to_all.21 = bf16[8,80,256]{2,1,0:T(8,128)(2,1)S(1)} all-to-all(bf16[8,80,256]{2,1,0:T(8,128)(2,1)S(1)} %project.1), channel_id=1, replica_groups={{64,96,0,32,192,224,128,160},{200,232,136,168,72,104,8,40},{80,112,16,4..., dimensions={0} | all-to-all | bytes 655360 | tf_op jit(solution)/shard_map/all_to_all | solution.py:346
  103.9 0.7 convert_reduce_fusion
Async XLA Ops:
  2.7 16.8 %copy-start = (bf16[1,256,1024]{2,1,0:T(8,128)(2,1)S(1)}, bf16[1,256,1024]{2,1,0:T(8,128)(2,1)}, u32[]{:S(2)}) copy-start(bf16[1,256,1024]{2,1,0:T(8,128)(2,1)} %param.12) | copy-start | bytes 1572868
  2.7 16.8 %copy-start.1 = (bf16[1,256,1024]{2,1,0:T(8,128)(2,1)S(1)}, bf16[1,256,1024]{2,1,0:T(8,128)(2,1)}, u32[]{:S(2)}) copy-start(bf16[1,256,1024]{2,1,0:T(8,128)(2,1)} %param.9) | copy-start | bytes 1572868
  2.7 16.8 %copy-start.2 = (bf16[1,256,1024]{2,1,0:T(8,128)(2,1)S(1)}, bf16[1,256,1024]{2,1,0:T(8,128)(2,1)}, u32[]{:S(2)}) copy-start(bf16[1,256,1024]{2,1,0:T(8,128)(2,1)} %param.13) | copy-start | bytes 1572868
  2.7 19.9 %all-to-all-start = ((bf16[8,272,256]{2,1,0:T(8,128)(2,1)}), bf16[8,272,256]{2,1,0:T(8,128)(2,1)S(1)}, u32[]{:S(2)}, u32[]{:S(2)}) async-start(bf16[8,272,256]{2,1,0:T(8,128)(2,1)} %pack.1), calls=%async_computation | async-start | bytes 2228224 | tf_op jit(solution)/shard_map/all_to_all | solution.py:338
  8.8 13.9 %copy-start.4 = (s32[1,256]{1,0:T(1,128)S(1)}, s32[1,256]{1,0:T(1,128)}, u32[]{:S(2)}) copy-start(s32[1,256]{1,0:T(1,128)} %pos_ref.3) | copy-start | bytes 3076
  8.8 13.9 %copy-start.5 = (f32[1,256,8]{1,2,0:T(8,128)S(1)}, f32[1,256,8]{1,2,0:T(8,128)}, u32[]{:S(2)}) copy-start(f32[1,256,8]{1,2,0:T(8,128)} %param.14) | copy-start | bytes 24580
  12.9 21.4 %collective-permute-start = (bf16[8,80,256]{2,1,0:T(8,128)(2,1)}, bf16[8,80,256]{2,1,0:T(8,128)(2,1)S(1)}, u32[]{:S(2)}, u32[]{:S(2)}) collective-permute-start(bf16[8,80,256]{2,1,0:T(8,128)(2,1)} %get-tuple-element.21), channel_id=1, source_target_pairs={{0,5},{1,6},{2,7},{3,4},{4,1},{5,2},{6,3},{7,0},{8,9},{9,10},{10,1... | collective-permute-start | bytes 983048 | tf_op jit(solution)/shard_map/ppermute | solution.py:244
  14.4 19.9 %collective-permute-start.1 = (bf16[8,80,256]{2,1,0:T(8,128)(2,1)}, bf16[8,80,256]{2,1,0:T(8,128)(2,1)S(1)}, u32[]{:S(2)}, u32[]{:S(2)}) collective-permute-start(bf16[8,80,256]{2,1,0:T(8,128)(2,1)} %get-tuple-element.22), channel_id=1, source_target_pairs={{0,6},{1,7},{2,4},{3,5},{4,2},{5,3},{6,0},{7,1},{8,10},{9,11},{10,... | collective-permute-start | bytes 983048 | tf_op jit(solution)/shard_map/ppermute | solution.py:244
  18.0 16.4 %collective-permute-start.2 = (bf16[8,80,256]{2,1,0:T(8,128)(2,1)}, bf16[8,80,256]{2,1,0:T(8,128)(2,1)}, u32[]{:S(2)}, u32[]{:S(2)}) collective-permute-start(bf16[8,80,256]{2,1,0:T(8,128)(2,1)} %get-tuple-element.23), channel_id=1, source_target_pairs={{0,7},{1,4},{2,5},{3,6},{4,3},{5,0},{6,1},{7,2},{8,11},{9,8},{10,9... | collective-permute-start | bytes 983048 | tf_op jit(solution)/shard_map/ppermute | solution.py:244
  22.7 23.2 %copy-start.6 = (bf16[8,80,256]{2,1,0:T(8,128)(2,1)S(1)}, bf16[8,80,256]{2,1,0:T(8,128)(2,1)}, u32[]{:S(2)}) copy-start(bf16[8,80,256]{2,1,0:T(8,128)(2,1)} %get-tuple-element.20) | copy-start | bytes 983044
  22.7 40.4 %copy-start.3 = (s32[3]{0:T(128)S(1)}, s32[3]{0:T(128)}, u32[]{:S(2)}) copy-start(s32[3]{0:T(128)} %pad_add_fusion.place_ref) | copy-start | bytes 40
  34.4 29.9 %all-to-all-start.1 = ((bf16[8,256,256]{2,1,0:T(8,128)(2,1)}), bf16[8,256,256]{2,1,0:T(8,128)(2,1)}, u32[]{:S(2)}, u32[]{:S(2)}) async-start(bf16[8,256,256]{2,1,0:T(8,128)(2,1)} %get-tuple-element.27), calls=%async_computation.1 | async-start | bytes 2097152 | tf_op jit(solution)/shard_map/all_to_all | solution.py:338
  45.8 13.9 %collective-permute-start.3 = (bf16[8,80,256]{2,1,0:T(8,128)(2,1)S(1)}, bf16[8,80,256]{2,1,0:T(8,128)(2,1)S(1)}, u32[]{:S(2)}, u32[]{:S(2)}) collective-permute-start(bf16[8,80,256]{2,1,0:T(8,128)(2,1)S(1)} %copy-done.6), channel_id=1, source_target_pairs={{0,4},{1,5},{2,6},{3,7},{4,0},{5,1},{6,2},{7,3},{8,8},{9,9},{10,10... | collective-permute-start | bytes 983048 | tf_op jit(solution)/shard_map/ppermute | solution.py:244
  59.8 1.6 %collective-permute-start.4 = (bf16[8,80,256]{2,1,0:T(8,128)(2,1)S(1)}, bf16[8,80,256]{2,1,0:T(8,128)(2,1)S(1)}, u32[]{:S(2)}, u32[]{:S(2)}) collective-permute-start(bf16[8,80,256]{2,1,0:T(8,128)(2,1)S(1)} %collective-permute-done.3.refs_0_), channel_id=1, source_target_pairs={{0,8},{8,0},{16,24},{24,16},{1,9},{9,1},{17,25},{25,17},{2,10},{10... | collective-permute-start | bytes 983048 | tf_op jit(solution)/shard_map/ppermute | solution.py:351
  59.8 2.1 %collective-permute-start.5 = (bf16[8,80,256]{2,1,0:T(8,128)(2,1)S(1)}, bf16[8,80,256]{2,1,0:T(8,128)(2,1)S(1)}, u32[]{:S(2)}, u32[]{:S(2)}) collective-permute-start(bf16[8,80,256]{2,1,0:T(8,128)(2,1)S(1)} %collective-permute-done.refs_1_), channel_id=1, source_target_pairs={{0,8},{8,0},{16,24},{24,16},{1,9},{9,1},{17,25},{25,17},{2,10},{10... | collective-permute-start | bytes 983048 | tf_op jit(solution)/shard_map/ppermute | solution.py:351
  60.3 2.5 %collective-permute-start.6 = (bf16[8,80,256]{2,1,0:T(8,128)(2,1)S(1)}, bf16[8,80,256]{2,1,0:T(8,128)(2,1)S(1)}, u32[]{:S(2)}, u32[]{:S(2)}) collective-permute-start(bf16[8,80,256]{2,1,0:T(8,128)(2,1)S(1)} %collective-permute-done.1.refs_2_), channel_id=1, source_target_pairs={{0,8},{8,0},{16,24},{24,16},{1,9},{9,1},{17,25},{25,17},{2,10},{10... | collective-permute-start | bytes 983048 | tf_op jit(solution)/shard_map/ppermute | solution.py:351
  60.3 2.7 %collective-permute-start.7 = (bf16[8,80,256]{2,1,0:T(8,128)(2,1)}, bf16[8,80,256]{2,1,0:T(8,128)(2,1)S(1)}, u32[]{:S(2)}, u32[]{:S(2)}) collective-permute-start(bf16[8,80,256]{2,1,0:T(8,128)(2,1)} %collective-permute-done.2.refs_3_), channel_id=1, source_target_pairs={{0,8},{8,0},{16,24},{24,16},{1,9},{9,1},{17,25},{25,17},{2,10},{10... | collective-permute-start | bytes 983048 | tf_op jit(solution)/shard_map/ppermute | solution.py:351

commit v10 on v8

--- a/solution.py
+++ b/solution.py
@@ -177,11 +177,16 @@
     )(query, grad, delta, lse, pos, kv)
 
 
-def spread_kernel(place_ref, in_ref, *refs):
+def position():
+    index = lax.axis_index("ctx")
+    return jnp.bitwise_and(lax.axis_index("heads"), 1), index // Y, jnp.bitwise_and(index, Y - 1)
+
+
+def spread_kernel(in_ref, *refs):
     outs, block, turned, in_sems, out_sems = refs[:Y], *refs[Y:]
     outer, tokens, width = block.shape
     rows = outs[0].shape[1]
-    core, x, y = place_ref[0], place_ref[1], place_ref[2]
+    core, x, y = position()
     to_x = jnp.bitwise_xor(x, 1 - core)
     shift = X * Y * rows - width
     loads = []
@@ -210,14 +215,14 @@
         store.wait()
 
 
-def spread(inputs, place, outer):
+def spread(inputs, outer):
     tokens, width = inputs.shape
     rows = width // (outer * X * Y)
     cols = -(-Y * rows // 128) * 128
     anywhere = pl.BlockSpec(memory_space=pl.ANY)
     return pl.pallas_call(
         spread_kernel,
-        in_specs=[pl.BlockSpec(memory_space=pltpu.SMEM), anywhere],
+        in_specs=[anywhere],
         out_specs=[anywhere] * Y,
         out_shape=[jax.ShapeDtypeStruct((outer, rows, tokens), inputs.dtype)] * Y,
         scratch_shapes=[
@@ -228,7 +233,7 @@
         ],
         compiler_params=pltpu.CompilerParams(vmem_limit_bytes=VMEM),
         name="spread",
-    )(place, inputs)
+    )(inputs)
 
 
 def pass_along(pieces):
@@ -245,9 +250,9 @@
     return passed
 
 
-def join_kernel(place_ref, *refs):
+def join_kernel(*refs):
     blocks, out_ref = refs[:-1], refs[-1]
-    core, x, y = place_ref[0], place_ref[1], place_ref[2]
+    core, x, y = position()
     ctx_mask = jnp.where(core == 0, WHOLE_ORDER[0], WHOLE_ORDER[1])
     dp_mask = jnp.where(core == 0, DP_ORDER[0], DP_ORDER[1])
     for k, block in enumerate(blocks):
@@ -259,16 +264,15 @@
             out_ref[place, jnp.bitwise_xor(i, dp_mask)] = block[i]
 
 
-def join(own, other, place):
+def join(own, other):
     outer, rows, tokens = own[0].shape
     return pl.pallas_call(
         join_kernel,
-        in_specs=[pl.BlockSpec(memory_space=pltpu.SMEM)]
-        + [pl.BlockSpec(memory_space=pltpu.VMEM)] * (2 * Y),
+        in_specs=[pl.BlockSpec(memory_space=pltpu.VMEM)] * (2 * Y),
         out_shape=jax.ShapeDtypeStruct((2 * Y, outer, rows, tokens), own[0].dtype),
         compiler_params=pltpu.CompilerParams(vmem_limit_bytes=16 * 2**20),
         name="join",
-    )(place, *own, *other)
+    )(*own, *other)
 
 
 def finish_kernel(parts_ref, key_ref, value_ref, low_ref, parts, sems):
@@ -354,17 +358,15 @@
 def shards(inputs, queries, keys, values, outputs, out_grad, lse, positions):
     ctx = lax.axis_size("ctx")
     dp = lax.axis_size("dp")
-    index = lax.axis_index("ctx")
-    place = jnp.stack([lax.axis_index("heads") % 2, index // Y, index % Y])
     kv = exchange_ctx(packed(keys[0], values[0], positions, ctx), PART_ORDER)
-    pieces = spread(inputs[0], place, dp)
+    pieces = spread(inputs[0], dp)
     own = pass_along(pieces)
     delta, _ = lax.optimization_barrier((deltas(out_grad[0], outputs[0], queries[0]), pieces))
     query_grad, partial = attention(
         queries[0], out_grad[0], delta, jnp.transpose(lse[0]), positions, kv
     )
     partial, own = lax.optimization_barrier((partial, own))
-    turned = join(own, [with_neighbour(block) for block in own], place)
+    turned = join(own, [with_neighbour(block) for block in own])
     key_grad, value_grad, low = finish(exchange_ctx(partial, PART_ORDER))
     low, turned = lax.optimization_barrier((low, turned))
     low = exchange_ctx(low, WHOLE_ORDER)

time: 96.6 us -> 96.6 us (level)
  waiting for transfers between devices: 11.8 us -> 13.2 us
  transfers between devices with their start and end apart: 10 -> 10, of which waited for: 6 -> 8; matrix products, arithmetic and copies ran while one was open for 1% -> 0% of each run, Pallas kernels for 17% -> 17%
where the time goes in v10:
time: 96.6 us; the launch traced here: 96.2 us
  blocking collectives  37.3 us (39%)
  starting transfers between devices  23.3 us (24%)
  Pallas kernels  20.9 us (22%)
  waiting for transfers between devices  13.2 us (14%)
    all_to_all x1, blocking collectives, exchange_dp(): lax.all_to_all(parts, ('dp', 'heads'), 0, 0, axis_index_groups=groups, ti...  18.8 us
    all_to_all x1, blocking collectives, exchange_ctx(): lax.all_to_all(parts, ('heads', 'ctx'), 0, 0, axis_index_groups=groups, t...  18.6 us
    all_to_all x2, starting transfers between devices, exchange_ctx(): lax.all_to_all(parts, ('heads', 'ctx'), 0, 0, axis_index_groups=groups, t...  12.3 us
    pallas_call x1, Pallas kernels, attention(): pl.pallas_call(attention_kernel, in_specs=[pl.BlockSpec(memory_space=pltp...  11.7 us
    ppermute x4, starting transfers between devices, pass_along(): passed.append(lax.ppermute(piece, ('heads', 'ctx'), route))  9.95 us
    all_to_all x2, waiting for transfers between devices, exchange_ctx(): lax.all_to_all(parts, ('heads', 'ctx'), 0, 0, axis_index_groups=groups, t...  7.94 us
    ppermute x4, waiting for transfers between devices, pass_along(): passed.append(lax.ppermute(piece, ('heads', 'ctx'), route))  3.07 us
    pallas_call x1, Pallas kernels, spread(): pl.pallas_call(spread_kernel, in_specs=[anywhere], out_specs=[anywhere] *...  2.84 us
  transfers between devices with their start and end apart: 10, of which 8 were waited for; matrix products, arithmetic and copies ran while one was open for 0% of the time, Pallas kernels for 17%

profile of v10, /device:TPU:6, one launch (start us, length us, event | category | flops | bytes accessed | tf_op | source)
XLA Modules:
  0.0 96.2 jit_solution(11293082983581499444)
XLA Ops:
  0.6 2.0 %pack.1 = bf16[8,272,256]{2,1,0:T(8,128)(2,1)} custom-call(bf16[256,128]{1,0:T(8,128)(2,1)} %bitcast.19, bf16[256,128]{1,0:T(8,128)(2,1)} %bitcast.20, s32[1,256]{1,0:T(1,128)} %pos_ref.3), custom_call_target="tpu_custom_call" | custom-call | tf_op jit(solution)/shard_map/pack/pallas_call | solution.py:58
  2.7 0.0 copy-start
  2.7 0.0 copy-start.1
  2.7 0.0 copy-start.2
  2.7 6.1 %all-to-all-start = ((bf16[8,272,256]{2,1,0:T(8,128)(2,1)}), bf16[8,272,256]{2,1,0:T(8,128)(2,1)S(1)}, u32[]{:S(2)}, u32[]{:S(2)}) async-start(bf16[8,272,256]{2,1,0:T(8,128)(2,1)} %pack.1), calls=%async_computation | async-start | bytes 2228224 | tf_op jit(solution)/shard_map/all_to_all | solution.py:342
  8.8 0.0 copy-start.3
  8.8 0.0 copy-start.4
  8.8 2.8 %spread.1 = (bf16[8,80,256]{2,1,0:T(8,128)(2,1)}, bf16[8,80,256]{2,1,0:T(8,128)(2,1)}, bf16[8,80,256]{2,1,0:T(8,128)(2,1)}, bf16[8,80,256]{2,1,0:T(8,128)(2,1)}) custom-call(bf16[256,5120]{1,0:T(8,128)(2,1)} %bitcast.18), custom_call_target="tpu_custom_call" | custom-call | tf_op jit(solution)/shard_map/spread/pallas_call | solution.py:223
  11.6 1.9 %collective-permute-start = (bf16[8,80,256]{2,1,0:T(8,128)(2,1)}, bf16[8,80,256]{2,1,0:T(8,128)(2,1)S(1)}, u32[]{:S(2)}, u32[]{:S(2)}) collective-permute-start(bf16[8,80,256]{2,1,0:T(8,128)(2,1)} %get-tuple-element.21), channel_id=1, source_target_pairs={{0,4},{1,5},{2,6},{3,7},{4,0},{5,1},{6,2},{7,3},{8,8},{9,9},{10,10... | collective-permute-start | bytes 983048 | tf_op jit(solution)/shard_map/ppermute | solution.py:249
  13.6 3.0 %collective-permute-start.1 = (bf16[8,80,256]{2,1,0:T(8,128)(2,1)}, bf16[8,80,256]{2,1,0:T(8,128)(2,1)S(1)}, u32[]{:S(2)}, u32[]{:S(2)}) collective-permute-start(bf16[8,80,256]{2,1,0:T(8,128)(2,1)} %get-tuple-element.22), channel_id=1, source_target_pairs={{0,5},{1,6},{2,7},{3,4},{4,1},{5,2},{6,3},{7,0},{8,9},{9,10},{10,1... | collective-permute-start | bytes 983048 | tf_op jit(solution)/shard_map/ppermute | solution.py:249
  16.5 2.7 %collective-permute-start.2 = (bf16[8,80,256]{2,1,0:T(8,128)(2,1)}, bf16[8,80,256]{2,1,0:T(8,128)(2,1)}, u32[]{:S(2)}, u32[]{:S(2)}) collective-permute-start(bf16[8,80,256]{2,1,0:T(8,128)(2,1)} %get-tuple-element.23), channel_id=1, source_target_pairs={{0,6},{1,7},{2,4},{3,5},{4,2},{5,3},{6,0},{7,1},{8,10},{9,11},{10,... | collective-permute-start | bytes 983048 | tf_op jit(solution)/shard_map/ppermute | solution.py:249
  19.2 2.4 %collective-permute-start.3 = (bf16[8,80,256]{2,1,0:T(8,128)(2,1)}, bf16[8,80,256]{2,1,0:T(8,128)(2,1)}, u32[]{:S(2)}, u32[]{:S(2)}) collective-permute-start(bf16[8,80,256]{2,1,0:T(8,128)(2,1)} %get-tuple-element.24), channel_id=1, source_target_pairs={{0,7},{1,4},{2,5},{3,6},{4,3},{5,0},{6,1},{7,2},{8,11},{9,8},{10,9... | collective-permute-start | bytes 983048 | tf_op jit(solution)/shard_map/ppermute | solution.py:249
  21.6 0.0 copy-done
  21.6 0.0 copy-done.1
  21.6 0.0 copy-done.2
  21.6 0.4 delta.1.delta_ref
  21.9 0.5 all-to-all-done.kv_ref
  22.4 0.0 copy-done.3
  22.4 0.0 copy-done.4
  22.4 11.7 %attention.1 = (f32[256,1024]{1,0:T(8,128)}, bf16[8,256,256]{2,1,0:T(8,128)(2,1)}) custom-call(bf16[256,1024]{1,0:T(8,128)(2,1)S(1)} %bitcast.14, bf16[256,1024]{1,0:T(8,128)(2,1)S(1)} %bitcast.16, f32[8,256]{1,0:T(8,128)S(1)} %delta.1.delta_ref, f32[8,256]{1,0:T(8,128)S(1)} %bitcast.17, s32[1,256]{1,0:T(1,128)S(1)} %copy-done.3, ...), custom_call_target="tpu_custom_call" | custom-call | flops 5368709120 | bytes 12582912 | tf_op jit(solution)/shard_map/attention/pallas_call | solution.py:155
  34.1 0.0 collective-permute-done.refs_0_
  34.1 0.0 collective-permute-done.1.refs_1_
  34.2 0.2 collective-permute-done.2.refs_2_
  34.4 2.9 %collective-permute-done.3.refs_3_ = bf16[8,80,256]{2,1,0:T(8,128)(2,1)} collective-permute-done((bf16[8,80,256]{2,1,0:T(8,128)(2,1)}, bf16[8,80,256]{2,1,0:T(8,128)(2,1)}, u32[]{:S(2)}, u32[]{:S(2)}) %collective-permute-start.3) | collective-permute-done | bytes 327712 | tf_op jit(solution)/shard_map/ppermute | solution.py:249
  37.2 6.2 %all-to-all-start.1 = ((bf16[8,256,256]{2,1,0:T(8,128)(2,1)}), bf16[8,256,256]{2,1,0:T(8,128)(2,1)}, u32[]{:S(2)}, u32[]{:S(2)}) async-start(bf16[8,256,256]{2,1,0:T(8,128)(2,1)} %get-tuple-element.28), calls=%async_computation.1 | async-start | bytes 2097152 | tf_op jit(solution)/shard_map/all_to_all | solution.py:342
  43.4 0.0 collective-permute-start.4
  43.4 0.5 collective-permute-start.5
  43.9 0.0 collective-permute-start.6
  44.0 0.5 collective-permute-start.7
  44.5 0.6 collective-permute-done.4.refs_4_
  45.1 0.6 collective-permute-done.5.refs_5_
  45.6 0.6 collective-permute-done.6.refs_6_
  46.2 0.5 collective-permute-done.7.refs_7_
  46.7 1.2 %join.1.turned_ref = bf16[8,8,80,256]{3,2,1,0:T(8,128)(2,1)S(1)} custom-call(bf16[8,80,256]{2,1,0:T(8,128)(2,1)S(1)} %collective-permute-done.refs_0_, bf16[8,80,256]{2,1,0:T(8,128)(2,1)S(1)} %collective-permute-done.1.refs_1_, bf16[8,80,256]{2,1,0:T(8,128)(2,1)} %collective-permute-done.2.refs_2_, bf16[8,80,256]{2,1,0:T(8,128)(2,1)} %collective-permute-done.3.refs_3_, ...), custom_call_target="tpu_custom_call" | custom-call | tf_op jit(solution)/shard_map/join/pallas_call | solution.py:269
  47.9 7.4 %all-to-all-done.1.parts_ref = bf16[8,256,256]{2,1,0:T(8,128)(2,1)} async-done(((bf16[8,256,256]{2,1,0:T(8,128)(2,1)}), bf16[8,256,256]{2,1,0:T(8,128)(2,1)}, u32[]{:S(2)}, u32[]{:S(2)}) %all-to-all-start.1) | async-done | bytes 1048608 | tf_op jit(solution)/shard_map/all_to_all | solution.py:342
  55.4 2.0 %finish.1 = (f32[256,128]{1,0:T(8,128)}, f32[256,128]{1,0:T(8,128)}, bf16[8,256,256]{2,1,0:T(8,128)(2,1)S(1)}) custom-call(bf16[8,256,256]{2,1,0:T(8,128)(2,1)} %all-to-all-done.1.parts_ref), custom_call_target="tpu_custom_call" | custom-call | tf_op jit(solution)/shard_map/finish/pallas_call | solution.py:304
  57.3 18.6 %all_to_all.20.low_ref = bf16[8,256,256]{2,1,0:T(8,128)(2,1)S(1)} all-to-all(bf16[8,256,256]{2,1,0:T(8,128)(2,1)S(1)} %get-tuple-element.37), channel_id=1, replica_groups={{0,1,2,3,4,5,6,7},{14,15,12,13,10,11,8,9},{16,17,18,19,20,21,22,23},{30..., dimensions={0} | all-to-all | bytes 2097152 | tf_op jit(solution)/shard_map/all_to_all | solution.py:342
  75.9 0.8 project.1
  76.7 18.8 %all_to_all.21 = bf16[8,80,256]{2,1,0:T(8,128)(2,1)S(1)} all-to-all(bf16[8,80,256]{2,1,0:T(8,128)(2,1)S(1)} %project.1), channel_id=1, replica_groups={{64,96,0,32,192,224,128,160},{200,232,136,168,72,104,8,40},{80,112,16,4..., dimensions={0} | all-to-all | bytes 655360 | tf_op jit(solution)/shard_map/all_to_all | solution.py:350
  95.5 0.7 convert_reduce_fusion
Async XLA Ops:
  2.7 18.9 %copy-start = (bf16[1,256,1024]{2,1,0:T(8,128)(2,1)S(1)}, bf16[1,256,1024]{2,1,0:T(8,128)(2,1)}, u32[]{:S(2)}) copy-start(bf16[1,256,1024]{2,1,0:T(8,128)(2,1)} %param.12) | copy-start | bytes 1572868
  2.7 18.9 %copy-start.1 = (bf16[1,256,1024]{2,1,0:T(8,128)(2,1)S(1)}, bf16[1,256,1024]{2,1,0:T(8,128)(2,1)}, u32[]{:S(2)}) copy-start(bf16[1,256,1024]{2,1,0:T(8,128)(2,1)} %param.9) | copy-start | bytes 1572868
  2.7 18.9 %copy-start.2 = (bf16[1,256,1024]{2,1,0:T(8,128)(2,1)S(1)}, bf16[1,256,1024]{2,1,0:T(8,128)(2,1)}, u32[]{:S(2)}) copy-start(bf16[1,256,1024]{2,1,0:T(8,128)(2,1)} %param.13) | copy-start | bytes 1572868
  2.7 19.7 %all-to-all-start = ((bf16[8,272,256]{2,1,0:T(8,128)(2,1)}), bf16[8,272,256]{2,1,0:T(8,128)(2,1)S(1)}, u32[]{:S(2)}, u32[]{:S(2)}) async-start(bf16[8,272,256]{2,1,0:T(8,128)(2,1)} %pack.1), calls=%async_computation | async-start | bytes 2228224 | tf_op jit(solution)/shard_map/all_to_all | solution.py:342
  8.8 13.7 %copy-start.3 = (s32[1,256]{1,0:T(1,128)S(1)}, s32[1,256]{1,0:T(1,128)}, u32[]{:S(2)}) copy-start(s32[1,256]{1,0:T(1,128)} %pos_ref.3) | copy-start | bytes 3076
  8.8 13.7 %copy-start.4 = (f32[1,256,8]{1,2,0:T(8,128)S(1)}, f32[1,256,8]{1,2,0:T(8,128)}, u32[]{:S(2)}) copy-start(f32[1,256,8]{1,2,0:T(8,128)} %param.14) | copy-start | bytes 24580
  11.6 22.5 %collective-permute-start = (bf16[8,80,256]{2,1,0:T(8,128)(2,1)}, bf16[8,80,256]{2,1,0:T(8,128)(2,1)S(1)}, u32[]{:S(2)}, u32[]{:S(2)}) collective-permute-start(bf16[8,80,256]{2,1,0:T(8,128)(2,1)} %get-tuple-element.21), channel_id=1, source_target_pairs={{0,4},{1,5},{2,6},{3,7},{4,0},{5,1},{6,2},{7,3},{8,8},{9,9},{10,10... | collective-permute-start | bytes 983048 | tf_op jit(solution)/shard_map/ppermute | solution.py:249
  13.6 20.6 %collective-permute-start.1 = (bf16[8,80,256]{2,1,0:T(8,128)(2,1)}, bf16[8,80,256]{2,1,0:T(8,128)(2,1)S(1)}, u32[]{:S(2)}, u32[]{:S(2)}) collective-permute-start(bf16[8,80,256]{2,1,0:T(8,128)(2,1)} %get-tuple-element.22), channel_id=1, source_target_pairs={{0,5},{1,6},{2,7},{3,4},{4,1},{5,2},{6,3},{7,0},{8,9},{9,10},{10,1... | collective-permute-start | bytes 983048 | tf_op jit(solution)/shard_map/ppermute | solution.py:249
  16.5 17.8 %collective-permute-start.2 = (bf16[8,80,256]{2,1,0:T(8,128)(2,1)}, bf16[8,80,256]{2,1,0:T(8,128)(2,1)}, u32[]{:S(2)}, u32[]{:S(2)}) collective-permute-start(bf16[8,80,256]{2,1,0:T(8,128)(2,1)} %get-tuple-element.23), channel_id=1, source_target_pairs={{0,6},{1,7},{2,4},{3,5},{4,2},{5,3},{6,0},{7,1},{8,10},{9,11},{10,... | collective-permute-start | bytes 983048 | tf_op jit(solution)/shard_map/ppermute | solution.py:249
  19.2 18.0 %collective-permute-start.3 = (bf16[8,80,256]{2,1,0:T(8,128)(2,1)}, bf16[8,80,256]{2,1,0:T(8,128)(2,1)}, u32[]{:S(2)}, u32[]{:S(2)}) collective-permute-start(bf16[8,80,256]{2,1,0:T(8,128)(2,1)} %get-tuple-element.24), channel_id=1, source_target_pairs={{0,7},{1,4},{2,5},{3,6},{4,3},{5,0},{6,1},{7,2},{8,11},{9,8},{10,9... | collective-permute-start | bytes 983048 | tf_op jit(solution)/shard_map/ppermute | solution.py:249
  37.2 18.2 %all-to-all-start.1 = ((bf16[8,256,256]{2,1,0:T(8,128)(2,1)}), bf16[8,256,256]{2,1,0:T(8,128)(2,1)}, u32[]{:S(2)}, u32[]{:S(2)}) async-start(bf16[8,256,256]{2,1,0:T(8,128)(2,1)} %get-tuple-element.28), calls=%async_computation.1 | async-start | bytes 2097152 | tf_op jit(solution)/shard_map/all_to_all | solution.py:342
  43.4 1.6 %collective-permute-start.4 = (bf16[8,80,256]{2,1,0:T(8,128)(2,1)S(1)}, bf16[8,80,256]{2,1,0:T(8,128)(2,1)S(1)}, u32[]{:S(2)}, u32[]{:S(2)}) collective-permute-start(bf16[8,80,256]{2,1,0:T(8,128)(2,1)S(1)} %collective-permute-done.refs_0_), channel_id=1, source_target_pairs={{0,8},{8,0},{16,24},{24,16},{1,9},{9,1},{17,25},{25,17},{2,10},{10... | collective-permute-start | bytes 983048 | tf_op jit(solution)/shard_map/ppermute | solution.py:355
  43.4 2.2 %collective-permute-start.5 = (bf16[8,80,256]{2,1,0:T(8,128)(2,1)S(1)}, bf16[8,80,256]{2,1,0:T(8,128)(2,1)S(1)}, u32[]{:S(2)}, u32[]{:S(2)}) collective-permute-start(bf16[8,80,256]{2,1,0:T(8,128)(2,1)S(1)} %collective-permute-done.1.refs_1_), channel_id=1, source_target_pairs={{0,8},{8,0},{16,24},{24,16},{1,9},{9,1},{17,25},{25,17},{2,10},{10... | collective-permute-start | bytes 983048 | tf_op jit(solution)/shard_map/ppermute | solution.py:355
  43.9 2.3 %collective-permute-start.6 = (bf16[8,80,256]{2,1,0:T(8,128)(2,1)}, bf16[8,80,256]{2,1,0:T(8,128)(2,1)S(1)}, u32[]{:S(2)}, u32[]{:S(2)}) collective-permute-start(bf16[8,80,256]{2,1,0:T(8,128)(2,1)} %collective-permute-done.2.refs_2_), channel_id=1, source_target_pairs={{0,8},{8,0},{16,24},{24,16},{1,9},{9,1},{17,25},{25,17},{2,10},{10... | collective-permute-start | bytes 983048 | tf_op jit(solution)/shard_map/ppermute | solution.py:355
  44.0 2.7 %collective-permute-start.7 = (bf16[8,80,256]{2,1,0:T(8,128)(2,1)}, bf16[8,80,256]{2,1,0:T(8,128)(2,1)S(1)}, u32[]{:S(2)}, u32[]{:S(2)}) collective-permute-start(bf16[8,80,256]{2,1,0:T(8,128)(2,1)} %collective-permute-done.3.refs_3_), channel_id=1, source_target_pairs={{0,8},{8,0},{16,24},{24,16},{1,9},{9,1},{17,25},{25,17},{2,10},{10... | collective-permute-start | bytes 983048 | tf_op jit(solution)/shard_map/ppermute | solution.py:355

commit v11 on v10

--- a/solution.py
+++ b/solution.py
@@ -14,7 +14,7 @@
 PAIR = 2
 CHUNK = 4
 SLAB = 128
-GROUP = 8
+LATE = 2
 VMEM = 60 * 2**20
 X = 2
 Y = 4
@@ -251,7 +251,7 @@
 
 
 def join_kernel(*refs):
-    blocks, out_ref = refs[:-1], refs[-1]
+    blocks, outs = refs[: 2 * Y], refs[2 * Y :]
     core, x, y = position()
     ctx_mask = jnp.where(core == 0, WHOLE_ORDER[0], WHOLE_ORDER[1])
     dp_mask = jnp.where(core == 0, DP_ORDER[0], DP_ORDER[1])
@@ -260,8 +260,11 @@
         from_x = jnp.bitwise_xor(x, 1 - at)
         from_y = jnp.bitwise_and(y - k % Y + Y, Y - 1)
         place = jnp.bitwise_xor(from_x * Y + from_y, ctx_mask)
-        for i in range(block.shape[0]):
-            out_ref[place, jnp.bitwise_xor(i, dp_mask)] = block[i]
+        at = 0
+        for out_ref in outs:
+            for i in range(out_ref.shape[1]):
+                out_ref[place, i] = block[jnp.bitwise_xor(at + i, dp_mask)]
+            at += out_ref.shape[1]
 
 
 def join(own, other):
@@ -269,7 +272,10 @@
     return pl.pallas_call(
         join_kernel,
         in_specs=[pl.BlockSpec(memory_space=pltpu.VMEM)] * (2 * Y),
-        out_shape=jax.ShapeDtypeStruct((2 * Y, outer, rows, tokens), own[0].dtype),
+        out_shape=[
+            jax.ShapeDtypeStruct((2 * Y, count, rows, tokens), own[0].dtype)
+            for count in (outer - LATE, LATE)
+        ],
         compiler_params=pltpu.CompilerParams(vmem_limit_bytes=16 * 2**20),
         name="join",
     )(*own, *other)
@@ -314,26 +320,31 @@
     )(parts)
 
 
-def project_kernel(turned_ref, low_ref, out_ref):
-    outer, rows, cols = out_ref.shape
-    for start in range(0, outer, GROUP):
+def project_kernel(*refs):
+    *turned, low_ref, out_ref = refs
+    rows, cols = out_ref.shape[1:]
+    at = 0
+    for ref in turned:
+        blocks, count = ref.shape[:2]
         total = None
-        for block in range(turned_ref.shape[0]):
-            left = turned_ref[block, start : start + GROUP].reshape(GROUP * rows, -1)
+        for block in range(blocks):
+            left = ref[block].reshape(count * rows, -1)
             term = dot(left, low_ref[block], COLS_ROWS)
             total = term if total is None else total + term
-        out_ref[start : start + GROUP] = total.astype(BF16).reshape(GROUP, rows, cols)
+        out_ref[at : at + count] = total.astype(BF16).reshape(count, rows, cols)
+        at += count
 
 
 def project(turned, low):
-    _, outer, rows, _ = turned.shape
+    rows = turned[0].shape[2]
+    outer = sum(part.shape[1] for part in turned)
     return pl.pallas_call(
         project_kernel,
-        in_specs=[pl.BlockSpec(memory_space=pltpu.VMEM)] * 2,
+        in_specs=[pl.BlockSpec(memory_space=pltpu.VMEM)] * (len(turned) + 1),
         out_shape=jax.ShapeDtypeStruct((outer, rows, low.shape[2]), BF16),
         compiler_params=pltpu.CompilerParams(vmem_limit_bytes=24 * 2**20),
         name="project",
-    )(turned, low)
+    )(*turned, low)
 
 
 def exchange_ctx(parts, order):

time: 96.6 us -> 95.5 us (0.989)
  local copies, waits for them, and re-layouts: 0.03 us -> 1.88 us
  waiting for transfers between devices: 13.2 us -> 11.4 us
    all_to_all x2, waiting for transfers between devices: 7.94 us -> 6.07 us  [exchange_ctx(): lax.all_to_all(parts, ('heads', 'ctx'), 0, 0, axis_index_groups=groups, t...]
    unnamed x10 -> x18, local copies, waits for them, and re-layouts: 0.03 us -> 1.88 us
    pallas_call x1, Pallas kernels: 1.96 us -> 0.92 us  [finish(): pl.pallas_call(finish_kernel, in_specs=[pl.BlockSpec(memory_space=pl.ANY)...]
where the time goes in v11:
time: 95.5 us; the launch traced here: 95 us
  blocking collectives  37.2 us (39%)
  starting transfers between devices  23.1 us (24%)
  Pallas kernels  20 us (21%)
  waiting for transfers between devices  11.4 us (12%)
  local copies, waits for them, and re-layouts  1.88 us (2%)
    all_to_all x1, blocking collectives, exchange_dp(): lax.all_to_all(parts, ('dp', 'heads'), 0, 0, axis_index_groups=groups, ti...  18.7 us
    all_to_all x1, blocking collectives, exchange_ctx(): lax.all_to_all(parts, ('heads', 'ctx'), 0, 0, axis_index_groups=groups, t...  18.5 us
    all_to_all x2, starting transfers between devices, exchange_ctx(): lax.all_to_all(parts, ('heads', 'ctx'), 0, 0, axis_index_groups=groups, t...  12.1 us
    pallas_call x1, Pallas kernels, attention(): pl.pallas_call(attention_kernel, in_specs=[pl.BlockSpec(memory_space=pltp...  11.7 us
    ppermute x4, starting transfers between devices, pass_along(): passed.append(lax.ppermute(piece, ('heads', 'ctx'), route))  9.95 us
    all_to_all x2, waiting for transfers between devices, exchange_ctx(): lax.all_to_all(parts, ('heads', 'ctx'), 0, 0, axis_index_groups=groups, t...  6.07 us
    ppermute x4, waiting for transfers between devices, pass_along(): passed.append(lax.ppermute(piece, ('heads', 'ctx'), route))  3.08 us
    pallas_call x1, Pallas kernels, spread(): pl.pallas_call(spread_kernel, in_specs=[anywhere], out_specs=[anywhere] *...  2.84 us
  transfers between devices with their start and end apart: 10, of which 8 were waited for; matrix products, arithmetic and copies ran while one was open for 0% of the time, Pallas kernels for 17%

profile of v11, /device:TPU:6, one launch (start us, length us, event | category | flops | bytes accessed | tf_op | source)
XLA Modules:
  0.0 95.0 jit_solution(4899735199594613214)
XLA Ops:
  0.6 2.1 %pack.1 = bf16[8,272,256]{2,1,0:T(8,128)(2,1)} custom-call(bf16[256,128]{1,0:T(8,128)(2,1)} %bitcast.19, bf16[256,128]{1,0:T(8,128)(2,1)} %bitcast.20, s32[1,256]{1,0:T(1,128)} %pos_ref.3), custom_call_target="tpu_custom_call" | custom-call | tf_op jit(solution)/shard_map/pack/pallas_call | solution.py:58
  2.7 0.0 copy-start.2
  2.7 0.0 copy-start.3
  2.7 0.0 copy-start.4
  2.7 6.1 %all-to-all-start = ((bf16[8,272,256]{2,1,0:T(8,128)(2,1)}), bf16[8,272,256]{2,1,0:T(8,128)(2,1)S(1)}, u32[]{:S(2)}, u32[]{:S(2)}) async-start(bf16[8,272,256]{2,1,0:T(8,128)(2,1)} %pack.1), calls=%async_computation | async-start | bytes 2228224 | tf_op jit(solution)/shard_map/all_to_all | solution.py:353
  8.8 0.0 copy-start.7
  8.8 0.0 copy-start.8
  8.8 2.8 %spread.1 = (bf16[8,80,256]{2,1,0:T(8,128)(2,1)}, bf16[8,80,256]{2,1,0:T(8,128)(2,1)}, bf16[8,80,256]{2,1,0:T(8,128)(2,1)}, bf16[8,80,256]{2,1,0:T(8,128)(2,1)}) custom-call(bf16[256,5120]{1,0:T(8,128)(2,1)} %bitcast.18), custom_call_target="tpu_custom_call" | custom-call | tf_op jit(solution)/shard_map/spread/pallas_call | solution.py:223
  11.7 1.9 %collective-permute-start = (bf16[8,80,256]{2,1,0:T(8,128)(2,1)}, bf16[8,80,256]{2,1,0:T(8,128)(2,1)S(1)}, u32[]{:S(2)}, u32[]{:S(2)}) collective-permute-start(bf16[8,80,256]{2,1,0:T(8,128)(2,1)} %get-tuple-element.24), channel_id=1, source_target_pairs={{0,4},{1,5},{2,6},{3,7},{4,0},{5,1},{6,2},{7,3},{8,8},{9,9},{10,10... | collective-permute-start | bytes 983048 | tf_op jit(solution)/shard_map/ppermute | solution.py:249
  13.6 3.0 %collective-permute-start.1 = (bf16[8,80,256]{2,1,0:T(8,128)(2,1)}, bf16[8,80,256]{2,1,0:T(8,128)(2,1)S(1)}, u32[]{:S(2)}, u32[]{:S(2)}) collective-permute-start(bf16[8,80,256]{2,1,0:T(8,128)(2,1)} %get-tuple-element.25), channel_id=1, source_target_pairs={{0,5},{1,6},{2,7},{3,4},{4,1},{5,2},{6,3},{7,0},{8,9},{9,10},{10,1... | collective-permute-start | bytes 983048 | tf_op jit(solution)/shard_map/ppermute | solution.py:249
  16.6 2.7 %collective-permute-start.2 = (bf16[8,80,256]{2,1,0:T(8,128)(2,1)}, bf16[8,80,256]{2,1,0:T(8,128)(2,1)}, u32[]{:S(2)}, u32[]{:S(2)}) collective-permute-start(bf16[8,80,256]{2,1,0:T(8,128)(2,1)} %get-tuple-element.26), channel_id=1, source_target_pairs={{0,6},{1,7},{2,4},{3,5},{4,2},{5,3},{6,0},{7,1},{8,10},{9,11},{10,... | collective-permute-start | bytes 983048 | tf_op jit(solution)/shard_map/ppermute | solution.py:249
  19.3 2.4 %collective-permute-start.3 = (bf16[8,80,256]{2,1,0:T(8,128)(2,1)}, bf16[8,80,256]{2,1,0:T(8,128)(2,1)}, u32[]{:S(2)}, u32[]{:S(2)}) collective-permute-start(bf16[8,80,256]{2,1,0:T(8,128)(2,1)} %get-tuple-element.27), channel_id=1, source_target_pairs={{0,7},{1,4},{2,5},{3,6},{4,3},{5,0},{6,1},{7,2},{8,11},{9,8},{10,9... | collective-permute-start | bytes 983048 | tf_op jit(solution)/shard_map/ppermute | solution.py:249
  21.6 0.0 copy-done.2
  21.6 0.0 copy-done.3
  21.6 0.0 copy-done.4
  21.6 0.4 delta.1.delta_ref
  22.0 0.5 all-to-all-done.kv_ref
  22.5 0.0 copy-done.7
  22.5 0.0 copy-done.8
  22.5 11.7 %attention.1 = (f32[256,1024]{1,0:T(8,128)}, bf16[8,256,256]{2,1,0:T(8,128)(2,1)}) custom-call(bf16[256,1024]{1,0:T(8,128)(2,1)S(1)} %bitcast.14, bf16[256,1024]{1,0:T(8,128)(2,1)S(1)} %bitcast.16, f32[8,256]{1,0:T(8,128)S(1)} %delta.1.delta_ref, f32[8,256]{1,0:T(8,128)S(1)} %bitcast.17, s32[1,256]{1,0:T(1,128)S(1)} %copy-done.7, ...), custom_call_target="tpu_custom_call" | custom-call | flops 5368709120 | bytes 12582912 | tf_op jit(solution)/shard_map/attention/pallas_call | solution.py:155
  34.1 0.0 collective-permute-done.refs_0_
  34.2 0.0 collective-permute-done.1.refs_1_
  34.2 0.0 copy-start.5
  34.2 0.2 collective-permute-done.2.refs_2_
  34.4 2.9 %collective-permute-done.3.refs_3_ = bf16[8,80,256]{2,1,0:T(8,128)(2,1)} collective-permute-done((bf16[8,80,256]{2,1,0:T(8,128)(2,1)}, bf16[8,80,256]{2,1,0:T(8,128)(2,1)}, u32[]{:S(2)}, u32[]{:S(2)}) %collective-permute-start.3) | collective-permute-done | bytes 327712 | tf_op jit(solution)/shard_map/ppermute | solution.py:249
  37.3 6.0 %all-to-all-start.1 = ((bf16[8,256,256]{2,1,0:T(8,128)(2,1)}), bf16[8,256,256]{2,1,0:T(8,128)(2,1)S(1)}, u32[]{:S(2)}, u32[]{:S(2)}) async-start(bf16[8,256,256]{2,1,0:T(8,128)(2,1)} %get-tuple-element.31), calls=%async_computation.1 | async-start | bytes 2097152 | tf_op jit(solution)/shard_map/all_to_all | solution.py:353
  43.3 0.0 collective-permute-start.4
  43.3 0.5 collective-permute-start.5
  43.8 0.0 collective-permute-start.6
  43.8 0.5 collective-permute-start.7
  44.3 0.6 collective-permute-done.4.refs_4_
  44.9 0.6 collective-permute-done.5.refs_5_
  45.5 0.6 collective-permute-done.6.refs_6_
  46.1 0.0 copy-done.5
  46.1 0.5 collective-permute-done.7.refs_7_
  46.5 0.0 copy-start.6
  46.5 1.0 %copy-done.6 = bf16[8,80,256]{2,1,0:T(8,128)(2,1)S(1)} copy-done((bf16[8,80,256]{2,1,0:T(8,128)(2,1)S(1)}, bf16[8,80,256]{2,1,0:T(8,128)(2,1)}, u32[]{:S(2)}) %copy-start.6) | copy-done | bytes 327704
  47.5 1.4 %join.1 = (bf16[8,6,80,256]{3,2,1,0:T(8,128)(2,1)S(1)}, bf16[8,2,80,256]{3,2,1,0:T(8,128)(2,1)S(1)}) custom-call(bf16[8,80,256]{2,1,0:T(8,128)(2,1)S(1)} %collective-permute-done.refs_0_, bf16[8,80,256]{2,1,0:T(8,128)(2,1)S(1)} %copy-done.6, bf16[8,80,256]{2,1,0:T(8,128)(2,1)} %collective-permute-done.2.refs_2_, ...), custom_call_target="tpu_custom_call" | custom-call | tf_op jit(solution)/shard_map/join/pallas_call | solution.py:272
  48.9 0.0 copy-start
  48.9 0.9 copy-done
  49.7 5.6 %all-to-all-done.1.parts_ref = bf16[8,256,256]{2,1,0:T(8,128)(2,1)S(1)} async-done(((bf16[8,256,256]{2,1,0:T(8,128)(2,1)}), bf16[8,256,256]{2,1,0:T(8,128)(2,1)S(1)}, u32[]{:S(2)}, u32[]{:S(2)}) %all-to-all-start.1) | async-done | bytes 1048608 | tf_op jit(solution)/shard_map/all_to_all | solution.py:353
  55.3 0.0 copy-start.1
  55.3 0.9 finish.1
  56.2 18.5 %all_to_all.20.refs_2_ = bf16[8,256,256]{2,1,0:T(8,128)(2,1)S(1)} all-to-all(bf16[8,256,256]{2,1,0:T(8,128)(2,1)S(1)} %get-tuple-element.43), channel_id=1, replica_groups={{0,1,2,3,4,5,6,7},{14,15,12,13,10,11,8,9},{16,17,18,19,20,21,22,23},{30..., dimensions={0} | all-to-all | bytes 2097152 | tf_op jit(solution)/shard_map/all_to_all | solution.py:353
  74.8 0.0 copy-done.1
  74.8 0.9 project.1
  75.6 18.7 %all_to_all.21 = bf16[8,80,256]{2,1,0:T(8,128)(2,1)S(1)} all-to-all(bf16[8,80,256]{2,1,0:T(8,128)(2,1)S(1)} %project.1), channel_id=1, replica_groups={{64,96,0,32,192,224,128,160},{200,232,136,168,72,104,8,40},{80,112,16,4..., dimensions={0} | all-to-all | bytes 655360 | tf_op jit(solution)/shard_map/all_to_all | solution.py:361
  94.3 0.7 convert_reduce_fusion
Async XLA Ops:
  2.7 18.9 %copy-start.2 = (bf16[1,256,1024]{2,1,0:T(8,128)(2,1)S(1)}, bf16[1,256,1024]{2,1,0:T(8,128)(2,1)}, u32[]{:S(2)}) copy-start(bf16[1,256,1024]{2,1,0:T(8,128)(2,1)} %param.12) | copy-start | bytes 1572868
  2.7 18.9 %copy-start.3 = (bf16[1,256,1024]{2,1,0:T(8,128)(2,1)S(1)}, bf16[1,256,1024]{2,1,0:T(8,128)(2,1)}, u32[]{:S(2)}) copy-start(bf16[1,256,1024]{2,1,0:T(8,128)(2,1)} %param.9) | copy-start | bytes 1572868
  2.7 18.9 %copy-start.4 = (bf16[1,256,1024]{2,1,0:T(8,128)(2,1)S(1)}, bf16[1,256,1024]{2,1,0:T(8,128)(2,1)}, u32[]{:S(2)}) copy-start(bf16[1,256,1024]{2,1,0:T(8,128)(2,1)} %param.13) | copy-start | bytes 1572868
  2.7 19.7 %all-to-all-start = ((bf16[8,272,256]{2,1,0:T(8,128)(2,1)}), bf16[8,272,256]{2,1,0:T(8,128)(2,1)S(1)}, u32[]{:S(2)}, u32[]{:S(2)}) async-start(bf16[8,272,256]{2,1,0:T(8,128)(2,1)} %pack.1), calls=%async_computation | async-start | bytes 2228224 | tf_op jit(solution)/shard_map/all_to_all | solution.py:353
  8.8 13.7 %copy-start.7 = (s32[1,256]{1,0:T(1,128)S(1)}, s32[1,256]{1,0:T(1,128)}, u32[]{:S(2)}) copy-start(s32[1,256]{1,0:T(1,128)} %pos_ref.3) | copy-start | bytes 3076
  8.8 13.7 %copy-start.8 = (f32[1,256,8]{1,2,0:T(8,128)S(1)}, f32[1,256,8]{1,2,0:T(8,128)}, u32[]{:S(2)}) copy-start(f32[1,256,8]{1,2,0:T(8,128)} %param.14) | copy-start | bytes 24580
  11.7 22.5 %collective-permute-start = (bf16[8,80,256]{2,1,0:T(8,128)(2,1)}, bf16[8,80,256]{2,1,0:T(8,128)(2,1)S(1)}, u32[]{:S(2)}, u32[]{:S(2)}) collective-permute-start(bf16[8,80,256]{2,1,0:T(8,128)(2,1)} %get-tuple-element.24), channel_id=1, source_target_pairs={{0,4},{1,5},{2,6},{3,7},{4,0},{5,1},{6,2},{7,3},{8,8},{9,9},{10,10... | collective-permute-start | bytes 983048 | tf_op jit(solution)/shard_map/ppermute | solution.py:249
  13.6 20.6 %collective-permute-start.1 = (bf16[8,80,256]{2,1,0:T(8,128)(2,1)}, bf16[8,80,256]{2,1,0:T(8,128)(2,1)S(1)}, u32[]{:S(2)}, u32[]{:S(2)}) collective-permute-start(bf16[8,80,256]{2,1,0:T(8,128)(2,1)} %get-tuple-element.25), channel_id=1, source_target_pairs={{0,5},{1,6},{2,7},{3,4},{4,1},{5,2},{6,3},{7,0},{8,9},{9,10},{10,1... | collective-permute-start | bytes 983048 | tf_op jit(solution)/shard_map/ppermute | solution.py:249
  16.6 17.8 %collective-permute-start.2 = (bf16[8,80,256]{2,1,0:T(8,128)(2,1)}, bf16[8,80,256]{2,1,0:T(8,128)(2,1)}, u32[]{:S(2)}, u32[]{:S(2)}) collective-permute-start(bf16[8,80,256]{2,1,0:T(8,128)(2,1)} %get-tuple-element.26), channel_id=1, source_target_pairs={{0,6},{1,7},{2,4},{3,5},{4,2},{5,3},{6,0},{7,1},{8,10},{9,11},{10,... | collective-permute-start | bytes 983048 | tf_op jit(solution)/shard_map/ppermute | solution.py:249
  19.3 18.0 %collective-permute-start.3 = (bf16[8,80,256]{2,1,0:T(8,128)(2,1)}, bf16[8,80,256]{2,1,0:T(8,128)(2,1)}, u32[]{:S(2)}, u32[]{:S(2)}) collective-permute-start(bf16[8,80,256]{2,1,0:T(8,128)(2,1)} %get-tuple-element.27), channel_id=1, source_target_pairs={{0,7},{1,4},{2,5},{3,6},{4,3},{5,0},{6,1},{7,2},{8,11},{9,8},{10,9... | collective-permute-start | bytes 983048 | tf_op jit(solution)/shard_map/ppermute | solution.py:249
  34.2 11.9 %copy-start.5 = (bf16[8,80,256]{2,1,0:T(8,128)(2,1)}, bf16[8,80,256]{2,1,0:T(8,128)(2,1)S(1)}, u32[]{:S(2)}) copy-start(bf16[8,80,256]{2,1,0:T(8,128)(2,1)S(1)} %collective-permute-done.1.refs_1_) | copy-start | bytes 983044
  37.3 18.1 %all-to-all-start.1 = ((bf16[8,256,256]{2,1,0:T(8,128)(2,1)}), bf16[8,256,256]{2,1,0:T(8,128)(2,1)S(1)}, u32[]{:S(2)}, u32[]{:S(2)}) async-start(bf16[8,256,256]{2,1,0:T(8,128)(2,1)} %get-tuple-element.31), calls=%async_computation.1 | async-start | bytes 2097152 | tf_op jit(solution)/shard_map/all_to_all | solution.py:353
  43.3 1.6 %collective-permute-start.4 = (bf16[8,80,256]{2,1,0:T(8,128)(2,1)S(1)}, bf16[8,80,256]{2,1,0:T(8,128)(2,1)S(1)}, u32[]{:S(2)}, u32[]{:S(2)}) collective-permute-start(bf16[8,80,256]{2,1,0:T(8,128)(2,1)S(1)} %collective-permute-done.refs_0_), channel_id=1, source_target_pairs={{0,8},{8,0},{16,24},{24,16},{1,9},{9,1},{17,25},{25,17},{2,10},{10... | collective-permute-start | bytes 983048 | tf_op jit(solution)/shard_map/ppermute | solution.py:366
  43.3 2.2 %collective-permute-start.5 = (bf16[8,80,256]{2,1,0:T(8,128)(2,1)S(1)}, bf16[8,80,256]{2,1,0:T(8,128)(2,1)S(1)}, u32[]{:S(2)}, u32[]{:S(2)}) collective-permute-start(bf16[8,80,256]{2,1,0:T(8,128)(2,1)S(1)} %collective-permute-done.1.refs_1_), channel_id=1, source_target_pairs={{0,8},{8,0},{16,24},{24,16},{1,9},{9,1},{17,25},{25,17},{2,10},{10... | collective-permute-start | bytes 983048 | tf_op jit(solution)/shard_map/ppermute | solution.py:366
  43.8 2.3 %collective-permute-start.6 = (bf16[8,80,256]{2,1,0:T(8,128)(2,1)}, bf16[8,80,256]{2,1,0:T(8,128)(2,1)S(1)}, u32[]{:S(2)}, u32[]{:S(2)}) collective-permute-start(bf16[8,80,256]{2,1,0:T(8,128)(2,1)} %collective-permute-done.2.refs_2_), channel_id=1, source_target_pairs={{0,8},{8,0},{16,24},{24,16},{1,9},{9,1},{17,25},{25,17},{2,10},{10... | collective-permute-start | bytes 983048 | tf_op jit(solution)/shard_map/ppermute | solution.py:366
  43.8 2.7 %collective-permute-start.7 = (bf16[8,80,256]{2,1,0:T(8,128)(2,1)}, bf16[8,80,256]{2,1,0:T(8,128)(2,1)S(1)}, u32[]{:S(2)}, u32[]{:S(2)}) collective-permute-start(bf16[8,80,256]{2,1,0:T(8,128)(2,1)} %collective-permute-done.3.refs_3_), channel_id=1, source_target_pairs={{0,8},{8,0},{16,24},{24,16},{1,9},{9,1},{17,25},{25,17},{2,10},{10... | collective-permute-start | bytes 983048 | tf_op jit(solution)/shard_map/ppermute | solution.py:366
  46.5 1.0 %copy-start.6 = (bf16[8,80,256]{2,1,0:T(8,128)(2,1)S(1)}, bf16[8,80,256]{2,1,0:T(8,128)(2,1)}, u32[]{:S(2)}) copy-start(bf16[8,80,256]{2,1,0:T(8,128)(2,1)} %copy-done.5) | copy-start | bytes 983044
  48.9 0.9 copy-start
  55.3 19.5 %copy-start.1 = (bf16[8,2,80,256]{3,2,1,0:T(8,128)(2,1)S(1)}, bf16[8,2,80,256]{3,2,1,0:T(8,128)(2,1)}, u32[]{:S(2)}) copy-start(bf16[8,2,80,256]{3,2,1,0:T(8,128)(2,1)} %copy-done) | copy-start | bytes 1966084

commit v12 on v11

--- a/solution.py
+++ b/solution.py
@@ -238,15 +238,15 @@
 
 def pass_along(pieces):
     heads, ctx = lax.axis_size("heads"), lax.axis_size("ctx")
-    passed = []
-    for i, piece in enumerate(pieces):
+    passed = list(pieces)
+    for i in (0, 2, 1, 3):
         route = []
         for h in range(heads):
             for c in range(ctx):
                 x, y = divmod(c, Y)
                 to_x = x if h % 2 else 1 - x
                 route.append((h * ctx + c, h * ctx + to_x * Y + (y + i) % Y))
-        passed.append(lax.ppermute(piece, ("heads", "ctx"), route))
+        passed[i] = lax.ppermute(pieces[i], ("heads", "ctx"), route)
     return passed
 
 
@@ -376,7 +376,9 @@
     query_grad, partial = attention(
         queries[0], out_grad[0], delta, jnp.transpose(lse[0]), positions, kv
     )
+    own = [own[i] for i in (0, 2, 1, 3)]
     partial, own = lax.optimization_barrier((partial, own))
+    own = [own[i] for i in (0, 2, 1, 3)]
     turned = join(own, [with_neighbour(block) for block in own])
     key_grad, value_grad, low = finish(exchange_ctx(partial, PART_ORDER))
     low, turned = lax.optimization_barrier((low, turned))

time: 95.5 us -> 95.2 us (level)
  transfers between devices with their start and end apart: 10 -> 10, of which waited for: 8 -> 7; matrix products, arithmetic and copies ran while one was open for 0% -> 0% of each run, Pallas kernels for 17% -> 17%
where the time goes in v12:
time: 95.2 us; the launch traced here: 94.7 us
  blocking collectives  36.9 us (39%)
  starting transfers between devices  22.8 us (24%)
  Pallas kernels  20 us (21%)
  waiting for transfers between devices  11.6 us (12%)
  local copies, waits for them, and re-layouts  1.88 us (2%)
    all_to_all x1, blocking collectives, exchange_dp(): lax.all_to_all(parts, ('dp', 'heads'), 0, 0, axis_index_groups=groups, ti...  18.5 us
    all_to_all x1, blocking collectives, exchange_ctx(): lax.all_to_all(parts, ('heads', 'ctx'), 0, 0, axis_index_groups=groups, t...  18.4 us
    pallas_call x1, Pallas kernels, attention(): pl.pallas_call(attention_kernel, in_specs=[pl.BlockSpec(memory_space=pltp...  11.7 us
    all_to_all x2, starting transfers between devices, exchange_ctx(): lax.all_to_all(parts, ('heads', 'ctx'), 0, 0, axis_index_groups=groups, t...  11.3 us
    ppermute x4, starting transfers between devices, pass_along(): passed[i] = lax.ppermute(pieces[i], ('heads', 'ctx'), route)  10.6 us
    all_to_all x2, waiting for transfers between devices, exchange_ctx(): lax.all_to_all(parts, ('heads', 'ctx'), 0, 0, axis_index_groups=groups, t...  6.02 us
    ppermute x4, waiting for transfers between devices, pass_along(): passed[i] = lax.ppermute(pieces[i], ('heads', 'ctx'), route)  3.36 us
    pallas_call x1, Pallas kernels, spread(): pl.pallas_call(spread_kernel, in_specs=[anywhere], out_specs=[anywhere] *...  2.83 us
  transfers between devices with their start and end apart: 10, of which 7 were waited for; matrix products, arithmetic and copies ran while one was open for 0% of the time, Pallas kernels for 17%

profile of v12, /device:TPU:6, one launch (start us, length us, event | category | flops | bytes accessed | tf_op | source)
XLA Modules:
  0.0 94.7 jit_solution(1097694321579034742)
XLA Ops:
  0.6 2.1 %pack.1 = bf16[8,272,256]{2,1,0:T(8,128)(2,1)} custom-call(bf16[256,128]{1,0:T(8,128)(2,1)} %bitcast.19, bf16[256,128]{1,0:T(8,128)(2,1)} %bitcast.20, s32[1,256]{1,0:T(1,128)} %pos_ref.3), custom_call_target="tpu_custom_call" | custom-call | tf_op jit(solution)/shard_map/pack/pallas_call | solution.py:58
  2.7 0.0 copy-start.2
  2.7 0.0 copy-start.3
  2.7 0.0 copy-start.4
  2.7 6.1 %all-to-all-start = ((bf16[8,272,256]{2,1,0:T(8,128)(2,1)}), bf16[8,272,256]{2,1,0:T(8,128)(2,1)S(1)}, u32[]{:S(2)}, u32[]{:S(2)}) async-start(bf16[8,272,256]{2,1,0:T(8,128)(2,1)} %pack.1), calls=%async_computation | async-start | bytes 2228224 | tf_op jit(solution)/shard_map/all_to_all | solution.py:353
  8.8 0.0 copy-start.7
  8.8 0.0 copy-start.8
  8.8 2.8 %spread.1 = (bf16[8,80,256]{2,1,0:T(8,128)(2,1)}, bf16[8,80,256]{2,1,0:T(8,128)(2,1)}, bf16[8,80,256]{2,1,0:T(8,128)(2,1)}, bf16[8,80,256]{2,1,0:T(8,128)(2,1)}) custom-call(bf16[256,5120]{1,0:T(8,128)(2,1)} %bitcast.18), custom_call_target="tpu_custom_call" | custom-call | tf_op jit(solution)/shard_map/spread/pallas_call | solution.py:223
  11.7 1.9 %collective-permute-start = (bf16[8,80,256]{2,1,0:T(8,128)(2,1)}, bf16[8,80,256]{2,1,0:T(8,128)(2,1)S(1)}, u32[]{:S(2)}, u32[]{:S(2)}) collective-permute-start(bf16[8,80,256]{2,1,0:T(8,128)(2,1)} %get-tuple-element.24), channel_id=1, source_target_pairs={{0,4},{1,5},{2,6},{3,7},{4,0},{5,1},{6,2},{7,3},{8,8},{9,9},{10,10... | collective-permute-start | bytes 983048 | tf_op jit(solution)/shard_map/ppermute | solution.py:249
  13.6 4.5 %collective-permute-start.1 = (bf16[8,80,256]{2,1,0:T(8,128)(2,1)}, bf16[8,80,256]{2,1,0:T(8,128)(2,1)S(1)}, u32[]{:S(2)}, u32[]{:S(2)}) collective-permute-start(bf16[8,80,256]{2,1,0:T(8,128)(2,1)} %get-tuple-element.26), channel_id=1, source_target_pairs={{0,6},{1,7},{2,4},{3,5},{4,2},{5,3},{6,0},{7,1},{8,10},{9,11},{10,... | collective-permute-start | bytes 983048 | tf_op jit(solution)/shard_map/ppermute | solution.py:249
  18.1 0.6 collective-permute-start.2
  18.6 3.6 %collective-permute-start.3 = (bf16[8,80,256]{2,1,0:T(8,128)(2,1)}, bf16[8,80,256]{2,1,0:T(8,128)(2,1)}, u32[]{:S(2)}, u32[]{:S(2)}) collective-permute-start(bf16[8,80,256]{2,1,0:T(8,128)(2,1)} %get-tuple-element.27), channel_id=1, source_target_pairs={{0,7},{1,4},{2,5},{3,6},{4,3},{5,0},{6,1},{7,2},{8,11},{9,8},{10,9... | collective-permute-start | bytes 983048 | tf_op jit(solution)/shard_map/ppermute | solution.py:249
  22.2 0.0 copy-done.2
  22.2 0.0 copy-done.3
  22.2 0.0 copy-done.4
  22.2 0.4 delta.1.delta_ref
  22.6 0.0 all-to-all-done.kv_ref
  22.6 0.0 copy-done.7
  22.6 0.0 copy-done.8
  22.6 11.7 %attention.1 = (f32[256,1024]{1,0:T(8,128)}, bf16[8,256,256]{2,1,0:T(8,128)(2,1)}) custom-call(bf16[256,1024]{1,0:T(8,128)(2,1)S(1)} %bitcast.14, bf16[256,1024]{1,0:T(8,128)(2,1)S(1)} %bitcast.16, f32[8,256]{1,0:T(8,128)S(1)} %delta.1.delta_ref, f32[8,256]{1,0:T(8,128)S(1)} %bitcast.17, s32[1,256]{1,0:T(1,128)S(1)} %copy-done.7, ...), custom_call_target="tpu_custom_call" | custom-call | flops 5368709120 | bytes 12582912 | tf_op jit(solution)/shard_map/attention/pallas_call | solution.py:155
  34.3 0.0 collective-permute-done.refs_0_
  34.3 0.0 collective-permute-done.1.refs_2_
  34.3 0.0 copy-start.5
  34.3 0.1 collective-permute-done.2.refs_1_
  34.5 3.2 %collective-permute-done.3.refs_3_ = bf16[8,80,256]{2,1,0:T(8,128)(2,1)} collective-permute-done((bf16[8,80,256]{2,1,0:T(8,128)(2,1)}, bf16[8,80,256]{2,1,0:T(8,128)(2,1)}, u32[]{:S(2)}, u32[]{:S(2)}) %collective-permute-start.3) | collective-permute-done | bytes 327712 | tf_op jit(solution)/shard_map/ppermute | solution.py:249
  37.7 5.2 %all-to-all-start.1 = ((bf16[8,256,256]{2,1,0:T(8,128)(2,1)}), bf16[8,256,256]{2,1,0:T(8,128)(2,1)S(1)}, u32[]{:S(2)}, u32[]{:S(2)}) async-start(bf16[8,256,256]{2,1,0:T(8,128)(2,1)} %get-tuple-element.31), calls=%async_computation.1 | async-start | bytes 2097152 | tf_op jit(solution)/shard_map/all_to_all | solution.py:353
  42.9 0.0 collective-permute-start.4
  42.9 0.5 collective-permute-start.5
  43.4 0.0 collective-permute-start.6
  43.4 0.5 collective-permute-start.7
  43.9 1.0 %collective-permute-done.4.refs_4_ = bf16[8,80,256]{2,1,0:T(8,128)(2,1)S(1)} collective-permute-done((bf16[8,80,256]{2,1,0:T(8,128)(2,1)S(1)}, bf16[8,80,256]{2,1,0:T(8,128)(2,1)S(1)}, u32[]{:S(2)}, u32[]{:S(2)}) %collective-permute-start.4) | collective-permute-done | bytes 327712 | tf_op jit(solution)/shard_map/ppermute | solution.py:366
  44.9 0.4 collective-permute-done.5.refs_5_
  45.3 0.6 collective-permute-done.6.refs_6_
  45.9 0.0 copy-done.5
  45.9 0.2 collective-permute-done.7.refs_7_
  46.1 0.0 copy-start.6
  46.1 1.0 %copy-done.6 = bf16[8,80,256]{2,1,0:T(8,128)(2,1)S(1)} copy-done((bf16[8,80,256]{2,1,0:T(8,128)(2,1)S(1)}, bf16[8,80,256]{2,1,0:T(8,128)(2,1)}, u32[]{:S(2)}) %copy-start.6) | copy-done | bytes 327704
  47.1 1.4 %join.1 = (bf16[8,6,80,256]{3,2,1,0:T(8,128)(2,1)S(1)}, bf16[8,2,80,256]{3,2,1,0:T(8,128)(2,1)S(1)}) custom-call(bf16[8,80,256]{2,1,0:T(8,128)(2,1)S(1)} %collective-permute-done.refs_0_, bf16[8,80,256]{2,1,0:T(8,128)(2,1)} %collective-permute-done.2.refs_1_, bf16[8,80,256]{2,1,0:T(8,128)(2,1)S(1)} %copy-done.6, ...), custom_call_target="tpu_custom_call" | custom-call | tf_op jit(solution)/shard_map/join/pallas_call | solution.py:272
  48.4 0.0 copy-start
  48.4 0.9 copy-done
  49.3 6.0 %all-to-all-done.1.parts_ref = bf16[8,256,256]{2,1,0:T(8,128)(2,1)S(1)} async-done(((bf16[8,256,256]{2,1,0:T(8,128)(2,1)}), bf16[8,256,256]{2,1,0:T(8,128)(2,1)S(1)}, u32[]{:S(2)}, u32[]{:S(2)}) %all-to-all-start.1) | async-done | bytes 1048608 | tf_op jit(solution)/shard_map/all_to_all | solution.py:353
  55.3 0.0 copy-start.1
  55.3 0.9 finish.1
  56.3 18.4 %all_to_all.20.refs_2_ = bf16[8,256,256]{2,1,0:T(8,128)(2,1)S(1)} all-to-all(bf16[8,256,256]{2,1,0:T(8,128)(2,1)S(1)} %get-tuple-element.43), channel_id=1, replica_groups={{0,1,2,3,4,5,6,7},{14,15,12,13,10,11,8,9},{16,17,18,19,20,21,22,23},{30..., dimensions={0} | all-to-all | bytes 2097152 | tf_op jit(solution)/shard_map/all_to_all | solution.py:353
  74.6 0.0 copy-done.1
  74.6 0.8 project.1
  75.5 18.5 %all_to_all.21 = bf16[8,80,256]{2,1,0:T(8,128)(2,1)S(1)} all-to-all(bf16[8,80,256]{2,1,0:T(8,128)(2,1)S(1)} %project.1), channel_id=1, replica_groups={{64,96,0,32,192,224,128,160},{200,232,136,168,72,104,8,40},{80,112,16,4..., dimensions={0} | all-to-all | bytes 655360 | tf_op jit(solution)/shard_map/all_to_all | solution.py:361
  94.0 0.7 convert_reduce_fusion
Async XLA Ops:
  2.7 19.5 %copy-start.2 = (bf16[1,256,1024]{2,1,0:T(8,128)(2,1)S(1)}, bf16[1,256,1024]{2,1,0:T(8,128)(2,1)}, u32[]{:S(2)}) copy-start(bf16[1,256,1024]{2,1,0:T(8,128)(2,1)} %param.12) | copy-start | bytes 1572868
  2.7 19.5 %copy-start.3 = (bf16[1,256,1024]{2,1,0:T(8,128)(2,1)S(1)}, bf16[1,256,1024]{2,1,0:T(8,128)(2,1)}, u32[]{:S(2)}) copy-start(bf16[1,256,1024]{2,1,0:T(8,128)(2,1)} %param.9) | copy-start | bytes 1572868
  2.7 19.5 %copy-start.4 = (bf16[1,256,1024]{2,1,0:T(8,128)(2,1)S(1)}, bf16[1,256,1024]{2,1,0:T(8,128)(2,1)}, u32[]{:S(2)}) copy-start(bf16[1,256,1024]{2,1,0:T(8,128)(2,1)} %param.13) | copy-start | bytes 1572868
  2.7 19.9 %all-to-all-start = ((bf16[8,272,256]{2,1,0:T(8,128)(2,1)}), bf16[8,272,256]{2,1,0:T(8,128)(2,1)S(1)}, u32[]{:S(2)}, u32[]{:S(2)}) async-start(bf16[8,272,256]{2,1,0:T(8,128)(2,1)} %pack.1), calls=%async_computation | async-start | bytes 2228224 | tf_op jit(solution)/shard_map/all_to_all | solution.py:353
  8.8 13.8 %copy-start.7 = (s32[1,256]{1,0:T(1,128)S(1)}, s32[1,256]{1,0:T(1,128)}, u32[]{:S(2)}) copy-start(s32[1,256]{1,0:T(1,128)} %pos_ref.3) | copy-start | bytes 3076
  8.8 13.8 %copy-start.8 = (f32[1,256,8]{1,2,0:T(8,128)S(1)}, f32[1,256,8]{1,2,0:T(8,128)}, u32[]{:S(2)}) copy-start(f32[1,256,8]{1,2,0:T(8,128)} %param.14) | copy-start | bytes 24580
  11.7 22.6 %collective-permute-start = (bf16[8,80,256]{2,1,0:T(8,128)(2,1)}, bf16[8,80,256]{2,1,0:T(8,128)(2,1)S(1)}, u32[]{:S(2)}, u32[]{:S(2)}) collective-permute-start(bf16[8,80,256]{2,1,0:T(8,128)(2,1)} %get-tuple-element.24), channel_id=1, source_target_pairs={{0,4},{1,5},{2,6},{3,7},{4,0},{5,1},{6,2},{7,3},{8,8},{9,9},{10,10... | collective-permute-start | bytes 983048 | tf_op jit(solution)/shard_map/ppermute | solution.py:249
  13.6 20.7 %collective-permute-start.1 = (bf16[8,80,256]{2,1,0:T(8,128)(2,1)}, bf16[8,80,256]{2,1,0:T(8,128)(2,1)S(1)}, u32[]{:S(2)}, u32[]{:S(2)}) collective-permute-start(bf16[8,80,256]{2,1,0:T(8,128)(2,1)} %get-tuple-element.26), channel_id=1, source_target_pairs={{0,6},{1,7},{2,4},{3,5},{4,2},{5,3},{6,0},{7,1},{8,10},{9,11},{10,... | collective-permute-start | bytes 983048 | tf_op jit(solution)/shard_map/ppermute | solution.py:249
  18.1 16.4 %collective-permute-start.2 = (bf16[8,80,256]{2,1,0:T(8,128)(2,1)}, bf16[8,80,256]{2,1,0:T(8,128)(2,1)}, u32[]{:S(2)}, u32[]{:S(2)}) collective-permute-start(bf16[8,80,256]{2,1,0:T(8,128)(2,1)} %get-tuple-element.25), channel_id=1, source_target_pairs={{0,5},{1,6},{2,7},{3,4},{4,1},{5,2},{6,3},{7,0},{8,9},{9,10},{10,1... | collective-permute-start | bytes 983048 | tf_op jit(solution)/shard_map/ppermute | solution.py:249
  18.6 19.0 %collective-permute-start.3 = (bf16[8,80,256]{2,1,0:T(8,128)(2,1)}, bf16[8,80,256]{2,1,0:T(8,128)(2,1)}, u32[]{:S(2)}, u32[]{:S(2)}) collective-permute-start(bf16[8,80,256]{2,1,0:T(8,128)(2,1)} %get-tuple-element.27), channel_id=1, source_target_pairs={{0,7},{1,4},{2,5},{3,6},{4,3},{5,0},{6,1},{7,2},{8,11},{9,8},{10,9... | collective-permute-start | bytes 983048 | tf_op jit(solution)/shard_map/ppermute | solution.py:249
  34.3 11.5 %copy-start.5 = (bf16[8,80,256]{2,1,0:T(8,128)(2,1)}, bf16[8,80,256]{2,1,0:T(8,128)(2,1)S(1)}, u32[]{:S(2)}) copy-start(bf16[8,80,256]{2,1,0:T(8,128)(2,1)S(1)} %collective-permute-done.1.refs_2_) | copy-start | bytes 983044
  37.7 17.7 %all-to-all-start.1 = ((bf16[8,256,256]{2,1,0:T(8,128)(2,1)}), bf16[8,256,256]{2,1,0:T(8,128)(2,1)S(1)}, u32[]{:S(2)}, u32[]{:S(2)}) async-start(bf16[8,256,256]{2,1,0:T(8,128)(2,1)} %get-tuple-element.31), calls=%async_computation.1 | async-start | bytes 2097152 | tf_op jit(solution)/shard_map/all_to_all | solution.py:353
  42.9 2.1 %collective-permute-start.4 = (bf16[8,80,256]{2,1,0:T(8,128)(2,1)S(1)}, bf16[8,80,256]{2,1,0:T(8,128)(2,1)S(1)}, u32[]{:S(2)}, u32[]{:S(2)}) collective-permute-start(bf16[8,80,256]{2,1,0:T(8,128)(2,1)S(1)} %collective-permute-done.refs_0_), channel_id=1, source_target_pairs={{0,8},{8,0},{16,24},{24,16},{1,9},{9,1},{17,25},{25,17},{2,10},{10... | collective-permute-start | bytes 983048 | tf_op jit(solution)/shard_map/ppermute | solution.py:366
  42.9 2.4 %collective-permute-start.5 = (bf16[8,80,256]{2,1,0:T(8,128)(2,1)}, bf16[8,80,256]{2,1,0:T(8,128)(2,1)S(1)}, u32[]{:S(2)}, u32[]{:S(2)}) collective-permute-start(bf16[8,80,256]{2,1,0:T(8,128)(2,1)} %collective-permute-done.2.refs_1_), channel_id=1, source_target_pairs={{0,8},{8,0},{16,24},{24,16},{1,9},{9,1},{17,25},{25,17},{2,10},{10... | collective-permute-start | bytes 983048 | tf_op jit(solution)/shard_map/ppermute | solution.py:366
  43.4 2.5 %collective-permute-start.6 = (bf16[8,80,256]{2,1,0:T(8,128)(2,1)S(1)}, bf16[8,80,256]{2,1,0:T(8,128)(2,1)S(1)}, u32[]{:S(2)}, u32[]{:S(2)}) collective-permute-start(bf16[8,80,256]{2,1,0:T(8,128)(2,1)S(1)} %collective-permute-done.1.refs_2_), channel_id=1, source_target_pairs={{0,8},{8,0},{16,24},{24,16},{1,9},{9,1},{17,25},{25,17},{2,10},{10... | collective-permute-start | bytes 983048 | tf_op jit(solution)/shard_map/ppermute | solution.py:366
  43.4 2.7 %collective-permute-start.7 = (bf16[8,80,256]{2,1,0:T(8,128)(2,1)}, bf16[8,80,256]{2,1,0:T(8,128)(2,1)S(1)}, u32[]{:S(2)}, u32[]{:S(2)}) collective-permute-start(bf16[8,80,256]{2,1,0:T(8,128)(2,1)} %collective-permute-done.3.refs_3_), channel_id=1, source_target_pairs={{0,8},{8,0},{16,24},{24,16},{1,9},{9,1},{17,25},{25,17},{2,10},{10... | collective-permute-start | bytes 983048 | tf_op jit(solution)/shard_map/ppermute | solution.py:366
  46.1 1.0 %copy-start.6 = (bf16[8,80,256]{2,1,0:T(8,128)(2,1)S(1)}, bf16[8,80,256]{2,1,0:T(8,128)(2,1)}, u32[]{:S(2)}) copy-start(bf16[8,80,256]{2,1,0:T(8,128)(2,1)} %copy-done.5) | copy-start | bytes 983044
  48.4 0.9 copy-start
  55.3 19.3 %copy-start.1 = (bf16[8,2,80,256]{3,2,1,0:T(8,128)(2,1)S(1)}, bf16[8,2,80,256]{3,2,1,0:T(8,128)(2,1)}, u32[]{:S(2)}) copy-start(bf16[8,2,80,256]{3,2,1,0:T(8,128)(2,1)} %copy-done) | copy-start | bytes 1966084
